TPU v7x, 256 devices: a whole 4x4x8 slice. The times are simulated.
256 devices in a mesh: pool: 4 (over z_lo), row: 16 (over y, x), col: 4 (over z_hi, core).
Axes of the slice: x: 4, y: 4, z: 8 (z_hi: 2, z_lo: 4; z = z_hi * 4 + z_lo), core: 2. Of those that a mesh axis runs over, the one named last changes fastest.
Arguments:
- valence_bands: bfloat16 [4, 2, 48, 2304], P('pool'), may hold values from -6 to 6
- conduction_bands: bfloat16 [512, 2, 48, 2304], P(('pool', 'row', 'col')), may hold values from -6 to 6
- valence_level_energy: float32 [4], replicated, may hold values from -12 to -2
- conduction_energy: float32 [512], P(('pool', 'row', 'col')), may hold values from 2 to 20
- g_index: int32 [5120], replicated, may hold values from 0 to 110591, as said below
Outputs:
- chi_real: float32 [5120, 5120], P(('pool', 'row'), 'col')
- chi_imag: float32 [5120, 5120], P(('pool', 'row'), 'col')
Inputs may be any that keep to these rules, and one draw needn't show every extreme that they name: `g_index`: the 5120 entries are distinct, and the indices 0 and 48**3 - 1 always occur.
All inputs are finite; a program needn't handle non-finite values.
Results may differ from a plain program's by a relative error of at most 0.012.
The roundings to bfloat16 on the way count: a program that leaves them out, or rounds other values in their place, can miss the bound.
Values may be sent and summed in bfloat16 or wider, within the bound.
No kernel may reach another device: no remote copies, remote signals or barrier semaphores. Data moves between devices by JAX's collectives and lax.ppermute only.
A program may use at most 256 MiB of HBM per device.

v0:
```python
import functools
import math

import jax
import jax.numpy as jnp
import ml_dtypes
import numpy as np
from jax import lax
from jax.experimental import pallas as pl
from jax.experimental.pallas import tpu as pltpu
from jax.sharding import Mesh, PartitionSpec as P

NV = 4
N = 48
NG = 5120
F32 = jnp.float32
BF16 = jnp.bfloat16
AXES = ("p", "y", "x", "h", "c")


def tables():
    k = np.arange(N)
    ang = (k[:, None] * k[None, :] % N).astype(np.float32) * np.float32(2.0 * math.pi / N)
    fac = np.float32(1.0 / math.sqrt(N))
    cos = (np.cos(ang) * fac).astype(ml_dtypes.bfloat16)
    sin = (np.sin(ang) * fac).astype(ml_dtypes.bfloat16)
    return cos, sin


def wide_tables():
    cos, sin = tables()
    cs = cos.astype(np.float32)
    sn = sin.astype(np.float32)
    eye8 = np.eye(8, dtype=np.float32)
    wz = np.zeros((2, 8, 48, 2, 48, 8), np.float32)
    for (f, g, tab) in ((0, 0, cs), (1, 0, sn), (0, 1, -sn), (1, 1, cs)):
        wz[f, :, :, g] = np.einsum("ab,kz->azkb", eye8, tab)
    wz = wz.reshape(768, 768)
    eye16 = np.eye(16, dtype=np.float32)
    wy = np.zeros((6, 2, 16, 8, 2, 16, 48), np.float32)
    for (f, g, tab) in ((0, 0, cs), (1, 0, sn), (0, 1, -sn), (1, 1, cs)):
        t = tab.reshape(48, 6, 8)
        wy[:, f, :, :, g] = np.einsum("ab,kmi->maibk", eye16, t)
    wy = wy.reshape(1536, 1536)
    return wz.astype(ml_dtypes.bfloat16), wy.astype(ml_dtypes.bfloat16), cos, sin


def coeff_kernel(core, own, part, other, cond, wz, wy, tc, ts, q, kx, w, left, right, xs, zs, s, oh, m):
    first = core[0] == 0

    def zstep(i, _):
        cols = pl.ds(pl.multiple_of(i * 384, 128), 384)
        for v in range(NV):
            if v == 0:
                vr = own[0, 0, :, cols].astype(F32)
                vi = own[0, 1, :, cols].astype(F32)
            else:
                a = part[v - 1, :, cols].astype(F32)
                b = other[v - 1, :, cols].astype(F32)
                vr = jnp.where(first, a, b)
                vi = jnp.where(first, b, a)
            for c in range(2):
                cr = cond[c, 0, :, cols].astype(F32)
                ci = cond[c, 1, :, cols].astype(F32)
                rows = slice((v * 2 + c) * N, (v * 2 + c + 1) * N)
                xs[rows, 0:384] = (vr * cr + vi * ci).astype(BF16)
                xs[rows, 384:768] = (vr * ci - vi * cr).astype(BF16)
        z = jnp.dot(xs[...], wz[...], preferred_element_type=F32).astype(BF16)
        for t in range(3):
            for f in range(2):
                zs[t, :, pl.ds(pl.multiple_of((i * 2 + f) * 128, 128), 128)] = z[
                    :, f * 384 + t * 128 : f * 384 + (t + 1) * 128
                ]
        return 0

    lax.fori_loop(0, 6, zstep, 0)

    def ystep(t, _):
        for f in range(2):
            out = jnp.dot(zs[t], wy[:, f * 768 : (f + 1) * 768], preferred_element_type=F32)
            s[f * 384 : (f + 1) * 384, pl.ds(pl.multiple_of(t * 768, 128), 768)] = out.astype(BF16)
        return 0

    lax.fori_loop(0, 3, ystep, 0)

    def gstep(n, _):
        cols = pl.ds(pl.multiple_of(n * 256, 128), 256)
        qq = q[:, cols]
        rows = lax.broadcasted_iota(jnp.int32, (128, 256), 0)
        for k in range(18):
            oh[k * 128 : (k + 1) * 128] = jnp.where(rows == qq - 128 * k, 1.0, 0.0).astype(BF16)
        full = jnp.dot(s[...], oh[...], preferred_element_type=F32).reshape(2, 8, N, 256)
        kk = kx[:, cols]
        ohk = jnp.where(lax.broadcasted_iota(jnp.int32, (N, 256), 0) == kk, 1.0, 0.0).astype(BF16)
        co = jnp.dot(tc[...], ohk, preferred_element_type=F32)
        si = jnp.dot(ts[...], ohk, preferred_element_type=F32)
        m[0, :, cols] = jnp.sum(full[0] * co + full[1] * si, axis=1)
        m[1, :, cols] = jnp.sum(full[1] * co - full[0] * si, axis=1)
        return 0

    lax.fori_loop(0, 20, gstep, 0)

    for z in range(8):
        for f in range(2):
            right[z, :, f * 640 : (f + 1) * 640] = m[f, :, z * 640 : (z + 1) * 640].astype(BF16)
    weight = w[...]
    for r in range(16):
        parts = []
        for f in range(2):
            for b in range(4):
                lane = ((b // 2 * 4 + r // 4) * 2 + b % 2) * 320 + 80 * (r % 4)
                parts.append(m[f, :, lane : lane + 80])
        left[r] = (weight * jnp.concatenate(parts, axis=1)).astype(BF16)


def coefficients(core, own, part, other, cond, q, kx, w):
    wz, wy, cos, sin = wide_tables()
    vm = pl.BlockSpec(memory_space=pltpu.VMEM)
    sm = pl.BlockSpec(memory_space=pltpu.SMEM)
    return pl.pallas_call(
        coeff_kernel,
        out_shape=(
            jax.ShapeDtypeStruct((16, 8, 640), BF16),
            jax.ShapeDtypeStruct((8, 8, 1280), BF16),
        ),
        in_specs=[sm] + [vm] * 11,
        out_specs=(vm, vm),
        scratch_shapes=[
            pltpu.VMEM((384, 768), BF16),
            pltpu.VMEM((3, 384, 1536), BF16),
            pltpu.VMEM((768, 2304), BF16),
            pltpu.VMEM((2304, 256), BF16),
            pltpu.VMEM((2, 8, NG), F32),
        ],
        compiler_params=pltpu.CompilerParams(vmem_limit_bytes=48 * 2**20),
    )(core, own, part, other, cond, jnp.asarray(wz), jnp.asarray(wy), jnp.asarray(cos), jnp.asarray(sin), q, kx, w)


def chi_kernel(core, place, rows, l0, l1, l2, l3, r0, r1, r2, r3, r4, mine, theirs, lall, lk, rk):
    for i, piece in enumerate((l0, l1, l2, l3)):
        lall[2 * i : 2 * i + 2] = piece[...]
    base = 0
    for piece in (r0, r1, r2, r3, r4):
        size = piece.shape[0]
        rk[base : base + size] = piece[...]
        base += size

    def fill(k, _):
        r = rows[k]
        for u in range(4):
            pair = [lall[place[2 * u + e], r].astype(F32) for e in range(2)]
            lk[pl.ds(pl.multiple_of(k * 64 + u * 16, 16), 16), :] = jnp.concatenate(pair, axis=0).astype(BF16)
        return 0

    lax.fori_loop(0, 16, fill, 0)
    first = core[0] == 0
    half = 320

    def product(f):
        return lax.dot_general(
            lk[:, f * half : (f + 1) * half], rk[...], (((0,), (0,)), ((), ())), preferred_element_type=F32
        )

    re = product(0)
    im = product(1)
    chi_re = re[:, :640] + im[:, 640:]
    chi_im = im[:, :640] - re[:, 640:]
    for k, chi in enumerate((chi_re, chi_im)):
        a, b = chi[:, :half], chi[:, half:]
        cols = slice(k * half, (k + 1) * half)
        mine[:, cols] = jnp.where(first, a, b)
        theirs[:, cols] = jnp.where(first, b, a)


def chi_tiles(core, place, rows, lefts, rights):
    vm = pl.BlockSpec(memory_space=pltpu.VMEM)
    sm = pl.BlockSpec(memory_space=pltpu.SMEM)
    return pl.pallas_call(
        chi_kernel,
        out_shape=(jax.ShapeDtypeStruct((320, 640), F32),) * 2,
        in_specs=[sm] * 3 + [vm] * 9,
        out_specs=(vm, vm),
        scratch_shapes=[
            pltpu.VMEM((8, 16, 8, 640), BF16),
            pltpu.VMEM((1024, 640), BF16),
            pltpu.VMEM((1024, 1280), BF16),
        ],
        compiler_params=pltpu.CompilerParams(vmem_limit_bytes=48 * 2**20),
    )(core, place, rows, *lefts, *rights)


def send(values, target):
    def index(z, y, x, c):
        return ((((z % 4) * 4 + y % 4) * 4 + x % 4) * 2 + (z % 8) // 4) * 2 + c

    pairs = [
        (index(z, y, x, c), index(*target(z, y, x, c)))
        for z in range(8)
        for y in range(4)
        for x in range(4)
        for c in range(2)
    ]
    return lax.ppermute(values, AXES, pairs)


def send_z(values, step):
    return send(values, lambda z, y, x, c: (z + step, y, x, c))


def send_core(values):
    return send(values, lambda z, y, x, c: (z, y, x, 1 - c))


def plane(axis, move):
    def target(z, y, x, c):
        if axis == c:
            return z, y, move(x), c
        return z, move(y), x, c

    return target


def outward(a):
    return a + 1 if a % 2 else a - 1


def inward(a):
    return a ^ 1


def ring(move):
    def target(z, y, x, c):
        return (move((z - c) % 8) + c) % 8, y, x, c

    return target


def ordered(flag, one, two):
    return jnp.where(flag, jnp.concatenate([one, two]), jnp.concatenate([two, one]))


def local(valence, conduction, valence_energy, conduction_energy, g_index):
    p, y, x, h, c = (lax.axis_index(a) for a in AXES)
    z = h * 4 + p
    core = jnp.reshape(c, (1,)).astype(jnp.int32)

    piece = lax.dynamic_index_in_dim(valence[0], c, 0, keepdims=False)
    part = jnp.concatenate(
        [
            send_z(piece, -1)[None],
            send_z(piece, 1)[None],
            jnp.concatenate([send_z(piece[:32], 2), send_z(piece[32:], -2)])[None],
        ]
    )
    other = send_core(part)
    bands = (p + jnp.array([0, 1, 3, 2])) % NV

    scale = math.sqrt(NV * 512)
    weight = 2.0 / ((valence_energy[bands][:, None] - conduction_energy[None, :]) * scale)
    order = g_index.reshape(2, 2, 4, 320).transpose(0, 2, 1, 3).reshape(1, NG)
    column = order % (N * N)
    left, right = coefficients(
        core,
        valence,
        part,
        other,
        conduction,
        (column % N) * N + column // N,
        order // (N * N),
        weight.reshape(8, 1),
    )

    right = lax.all_to_all(right, ("h", "p"), 0, 0, tiled=True).reshape(64, 1280)
    left = lax.all_to_all(left, ("y", "x"), 0, 0, tiled=True)[None]

    a = jnp.where(c == 0, x, y)
    b = jnp.where(c == 0, y, x)
    two = ordered(a % 2 == 0, right, send(right, plane(0, inward)))
    four = ordered(a < 2, two, send(two, plane(0, outward)))
    up = send(four, plane(1, lambda i: i + 1))
    down = send(four, plane(1, lambda i: i - 1))
    far_low = send(up[:128], plane(1, lambda i: i + 1))
    far_high = send(down[128:], plane(1, lambda i: i - 1))
    rights = (four, up, down, far_low, far_high)
    step = jnp.array([0, 3, 1, 2])
    bb = jnp.repeat((b + step) % 4, 4)
    aa = jnp.tile(jnp.arange(4), 4)
    rows = jnp.where(c == 0, bb * 4 + aa, aa * 4 + bb).astype(jnp.int32)

    zz = (z - c) % 8
    odd = zz % 2
    left0 = ordered(odd == 0, left, send(left, ring(inward)))
    left1 = send(left0, ring(outward))
    left2 = send(left1, ring(inward))
    left3 = send(left2, ring(outward))
    sign = 2 * odd - 1
    blocks = (zz // 2 + jnp.stack([0 * odd, sign, -sign, 0 * odd + 2])) % 4
    held = (jnp.stack([2 * blocks, 2 * blocks + 1], 1).reshape(8) + c) % 8
    place = jnp.argmax(held[None, :] == jnp.arange(8)[:, None], axis=1).astype(jnp.int32)

    mine, theirs = chi_tiles(core, place, rows, (left0, left1, left2, left3), rights)
    tile = (mine + send_core(theirs)).astype(BF16).reshape(4, 80, 640)
    tile = lax.all_to_all(tile, "p", 0, 0, tiled=True)
    full = jnp.transpose(tile.reshape(4, 80, 2, 320), (2, 1, 0, 3)).reshape(2, 80, 1280).astype(F32)
    return full[0], full[1]


def solution(mesh):
    fine = Mesh(mesh.devices.reshape(4, 4, 4, 2, 2), AXES)
    bands = P(AXES)
    return jax.shard_map(
        local,
        mesh=fine,
        in_specs=(P("p"), bands, P(), bands, P()),
        out_specs=(P(("p", "y", "x"), ("h", "c")),) * 2,
        check_vma=False,
    )
```

profile of v0, /device:TPU:1, one launch (start us, length us, event | category | flops | bytes accessed | tf_op | source)
XLA Modules:
  0.0 153.3 jit_solution(12963601886830468372)
XLA Ops:
  0.7 1.0 dynamic-slice_bitcast_fusion
  1.6 2.5 %collective-permute-start.1 = (bf16[48,2304]{1,0:T(8,128)(2,1)S(1)}, bf16[48,2304]{1,0:T(8,128)(2,1)S(1)}, u32[]{:S(2)}, u32[]{:S(2)}) collective-permute-start(bf16[48,2304]{1,0:T(8,128)(2,1)S(1)} %dynamic-slice_bitcast_fusion), channel_id=1, source_target_pairs={{0,64},{1,65},{4,68},{5,69},{8,72},{9,73},{12,76},{13,77},{16,80},... | collective-permute-start | bytes 663560 | tf_op jit(solution)/shard_map/ppermute | solution.py:203
  4.2 4.0 %collective-permute-start = (bf16[48,2304]{1,0:T(8,128)(2,1)S(1)}, bf16[48,2304]{1,0:T(8,128)(2,1)S(1)}, u32[]{:S(2)}, u32[]{:S(2)}) collective-permute-start(bf16[48,2304]{1,0:T(8,128)(2,1)S(1)} %dynamic-slice_bitcast_fusion), channel_id=1, source_target_pairs={{0,194},{1,195},{4,198},{5,199},{8,202},{9,203},{12,206},{13,207},... | collective-permute-start | bytes 663560 | tf_op jit(solution)/shard_map/ppermute | solution.py:203
  8.2 1.5 dynamic-slice_bitcast_fusion.2
  9.7 1.8 %collective-permute-start.3 = (bf16[16,2304]{1,0:T(8,128)(2,1)}, bf16[16,2304]{1,0:T(8,128)(2,1)}, u32[]{:S(2)}, u32[]{:S(2)}) collective-permute-start(bf16[16,2304]{1,0:T(8,128)(2,1)} %dynamic-slice_bitcast_fusion.2), channel_id=1, source_target_pairs={{0,130},{1,131},{4,134},{5,135},{8,138},{9,139},{12,142},{13,143},... | collective-permute-start | bytes 221192 | tf_op jit(solution)/shard_map/ppermute | solution.py:203
  11.5 0.9 dynamic-slice_bitcast_fusion.1
  12.5 0.6 collective-permute-start.2
  13.1 0.7 sign_compare_fusion
  13.8 1.3 broadcast_divide_fusion
  15.2 0.7 compare_select_fusion
  15.9 0.6 gather_fusion
  16.7 0.1 ne.185
  16.8 0.7 ne.187
  17.6 0.7 div.63
  18.3 0.8 rem.209
  19.2 0.7 rem.211
  19.9 0.7 collective-permute-done.2
  20.6 0.9 maximum_bitcast_fusion
  21.6 1.6 %collective-permute-start.4 = (bf16[3,48,2304]{2,1,0:T(8,128)(2,1)S(1)}, bf16[3,48,2304]{2,1,0:T(8,128)(2,1)S(1)}, u32[]{:S(2)}, u32[]{:S(2)}) collective-permute-start(bf16[3,48,2304]{2,1,0:T(8,128)(2,1)S(1)} %pad_maximum_fusion.part), channel_id=1, source_target_pairs={{0,1},{1,0},{4,5},{5,4},{8,9},{9,8},{12,13},{13,12},{16,17},{17,16... | collective-permute-start | bytes 1990664 | tf_op jit(solution)/shard_map/ppermute | solution.py:203
  23.3 0.2 and_select_fusion
  23.5 1.5 collective-permute-done.4.other
  25.0 38.9 %shard_map.122 = (bf16[16,8,640]{2,1,0:T(8,128)(2,1)}, bf16[8,8,1280]{2,1,0:T(8,128)(2,1)S(1)}) custom-call(s32[1]{0:T(128)} %bitcast.core, bf16[1,2,48,2304]{3,2,1,0:T(8,128)(2,1)S(1)} %copy-done.1, bf16[3,48,2304]{2,1,0:T(8,128)(2,1)S(1)} %pad_maximum_fusion.part, bf16[3,48,2304]{2,1,0:T(8,128)(2,1)S(1)} %collective-permute-done.4.other, ...), custom_call_target="tpu_custom_call" | custom-call | tf_op jit(solution)/shard_map/pallas_call | solution.py:120
  63.9 13.7 %all_to_all.15 = bf16[8,8,1280]{2,1,0:T(8,128)(2,1)S(1)} all-to-all(bf16[8,8,1280]{2,1,0:T(8,128)(2,1)S(1)} %get-tuple-element.9), channel_id=1, replica_groups=mesh['p'=4,'y'=4,'x'=4,'h'=2,'c'=2] {'h','p'}, dimensions={0} | all-to-all | bytes 327680 | tf_op jit(solution)/shard_map/all_to_all | solution.py:273
  77.6 1.3 collective-permute-start.9
  78.9 6.5 %all-to-all-start = ((bf16[16,8,640]{2,1,0:T(8,128)(2,1)}), bf16[16,8,640]{2,1,0:T(8,128)(2,1)S(1)}, u32[]{:S(2)}, u32[]{:S(2)}) async-start(bf16[16,8,640]{2,1,0:T(8,128)(2,1)} %get-tuple-element.8), calls=%async_computation | async-start | bytes 327680 | tf_op jit(solution)/shard_map/all_to_all | solution.py:274
  85.4 2.7 %collective-permute-start.10 = (bf16[128,1280]{1,0:T(8,128)(2,1)S(1)}, bf16[128,1280]{1,0:T(8,128)(2,1)S(1)}, u32[]{:S(2)}, u32[]{:S(2)}) collective-permute-start(bf16[128,1280]{1,0:T(8,128)(2,1)S(1)} %maximum_select_fusion.2), channel_id=1, source_target_pairs={{0,12},{1,49},{4,8},{5,53},{8,4},{9,57},{12,0},{13,61},{16,28},{17... | collective-permute-start | bytes 983048 | tf_op jit(solution)/shard_map/ppermute | solution.py:203
  88.1 4.3 %all-to-all-done = bf16[16,8,640]{2,1,0:T(8,128)(2,1)S(1)} async-done(((bf16[16,8,640]{2,1,0:T(8,128)(2,1)}), bf16[16,8,640]{2,1,0:T(8,128)(2,1)S(1)}, u32[]{:S(2)}, u32[]{:S(2)}) %all-to-all-start) | async-done | bytes 163872 | tf_op jit(solution)/shard_map/all_to_all | solution.py:274
  92.4 5.4 %collective-permute-done.5 = bf16[1,16,8,640]{3,2,1,0:T(8,128)(2,1)S(1)} collective-permute-done((bf16[1,16,8,640]{3,2,1,0:T(8,128)(2,1)S(1)}, bf16[1,16,8,640]{3,2,1,0:T(8,128)(2,1)S(1)}, u32[]{:S(2)}, u32[]{:S(2)}) %collective-permute-start.5) | collective-permute-done | bytes 163872 | tf_op jit(solution)/shard_map/ppermute | solution.py:203
  97.8 0.1 collective-permute-start.6
  97.9 0.1 maximum_select_fusion.r0
  98.1 0.9 collective-permute-start.12
  99.0 0.6 collective-permute-start.11
  99.7 4.5 %collective-permute-done.6.l1 = bf16[2,16,8,640]{3,2,1,0:T(8,128)(2,1)S(1)} collective-permute-done((bf16[2,16,8,640]{3,2,1,0:T(8,128)(2,1)S(1)}, bf16[2,16,8,640]{3,2,1,0:T(8,128)(2,1)S(1)}, u32[]{:S(2)}, u32[]{:S(2)}) %collective-permute-start.6) | collective-permute-done | bytes 327712 | tf_op jit(solution)/shard_map/ppermute | solution.py:203
  104.3 0.1 copy.26
  104.7 8.7 %collective-permute-done.7.l2 = bf16[2,16,8,640]{3,2,1,0:T(8,128)(2,1)S(1)} collective-permute-done((bf16[2,16,8,640]{3,2,1,0:T(8,128)(2,1)S(1)}, bf16[2,16,8,640]{3,2,1,0:T(8,128)(2,1)S(1)}, u32[]{:S(2)}, u32[]{:S(2)}) %collective-permute-start.7) | collective-permute-done | bytes 327712 | tf_op jit(solution)/shard_map/ppermute | solution.py:203
  113.4 0.3 collective-permute-start.14
  113.8 1.3 collective-permute-start.13
  115.1 0.6 iota_reduce_fusion
  115.7 6.1 %collective-permute-done.8.l3 = bf16[2,16,8,640]{3,2,1,0:T(8,128)(2,1)S(1)} collective-permute-done((bf16[2,16,8,640]{3,2,1,0:T(8,128)(2,1)S(1)}, bf16[2,16,8,640]{3,2,1,0:T(8,128)(2,1)S(1)}, u32[]{:S(2)}, u32[]{:S(2)}) %collective-permute-start.8) | collective-permute-done | bytes 327712 | tf_op jit(solution)/shard_map/ppermute | solution.py:203
  121.8 3.4 %shard_map.123 = (f32[320,640]{1,0:T(8,128)S(1)}, f32[320,640]{1,0:T(8,128)S(1)}) custom-call(s32[1]{0:T(128)} %bitcast.core, s32[8]{0:T(128)S(1)} %get-tuple-element.7.place, s32[16]{0:T(128)S(1)} %broadcast_select_fusion.rows, bf16[2,16,8,640]{3,2,1,0:T(8,128)(2,1)S(1)} %maximum_select_fusion.1.l0, bf16[2,16,8,640]{3,2,1,0:T(8,128)(2,1)S(1)} %collective-permute-done.6.l1, ...), custom_call_target="tpu_custom_call" | custom-call | tf_op jit(solution)/shard_map/pallas_call | solution.py:178
  125.1 8.2 %collective-permute-start.15 = (f32[320,640]{1,0:T(8,128)S(1)}, f32[320,640]{1,0:T(8,128)S(1)}, u32[]{:S(2)}, u32[]{:S(2)}) collective-permute-start(f32[320,640]{1,0:T(8,128)S(1)} %get-tuple-element.11), channel_id=1, source_target_pairs={{0,1},{1,0},{4,5},{5,4},{8,9},{9,8},{12,13},{13,12},{16,17},{17,16... | collective-permute-start | bytes 2457608 | tf_op jit(solution)/shard_map/ppermute | solution.py:203
  133.4 2.0 %collective-permute-done.15 = f32[320,640]{1,0:T(8,128)S(1)} collective-permute-done((f32[320,640]{1,0:T(8,128)S(1)}, f32[320,640]{1,0:T(8,128)S(1)}, u32[]{:S(2)}, u32[]{:S(2)}) %collective-permute-start.15) | collective-permute-done | bytes 819232 | tf_op jit(solution)/shard_map/ppermute | solution.py:203
  135.4 14.1 %all_to_all.16 = bf16[4,80,640]{2,1,0:T(8,128)(2,1)S(1)} all-to-all(bf16[4,80,640]{2,1,0:T(8,128)(2,1)S(1)} %bitcast.23), channel_id=1, replica_groups=mesh['p'=4,'y'=4,'x'=4,'h'=2,'c'=2] {'p'}, dimensions={0} | all-to-all | bytes 819200 | tf_op jit(solution)/shard_map/all_to_all | solution.py:303
  149.6 0.7 reshape.360
  150.3 0.6 copy.33
  151.0 0.2 fusion.8
  151.2 1.1 squeeze.13
  152.2 1.1 squeeze.12
  (57 shorter events, 1.1 us)
Async XLA Ops:
  0.6 15.2 %copy-start = (f32[4]{0:T(128)S(1)}, f32[4]{0:T(128)}, u32[]{:S(2)}) copy-start(f32[4]{0:T(128)} %param.13) | copy-start | bytes 52
  0.6 15.9 %copy-start.9 = (f32[2]{0:T(128)S(1)}, f32[2]{0:T(128)}, u32[]{:S(2)}) copy-start(f32[2]{0:T(128)} %param.14) | copy-start | bytes 28
  1.6 19.9 %collective-permute-start.1 = (bf16[48,2304]{1,0:T(8,128)(2,1)S(1)}, bf16[48,2304]{1,0:T(8,128)(2,1)S(1)}, u32[]{:S(2)}, u32[]{:S(2)}) collective-permute-start(bf16[48,2304]{1,0:T(8,128)(2,1)S(1)} %dynamic-slice_bitcast_fusion), channel_id=1, source_target_pairs={{0,64},{1,65},{4,68},{5,69},{8,72},{9,73},{12,76},{13,77},{16,80},... | collective-permute-start | bytes 663560 | tf_op jit(solution)/shard_map/ppermute | solution.py:203
  4.2 17.4 %collective-permute-start = (bf16[48,2304]{1,0:T(8,128)(2,1)S(1)}, bf16[48,2304]{1,0:T(8,128)(2,1)S(1)}, u32[]{:S(2)}, u32[]{:S(2)}) collective-permute-start(bf16[48,2304]{1,0:T(8,128)(2,1)S(1)} %dynamic-slice_bitcast_fusion), channel_id=1, source_target_pairs={{0,194},{1,195},{4,198},{5,199},{8,202},{9,203},{12,206},{13,207},... | collective-permute-start | bytes 663560 | tf_op jit(solution)/shard_map/ppermute | solution.py:203
  9.7 10.2 %collective-permute-start.3 = (bf16[16,2304]{1,0:T(8,128)(2,1)}, bf16[16,2304]{1,0:T(8,128)(2,1)}, u32[]{:S(2)}, u32[]{:S(2)}) collective-permute-start(bf16[16,2304]{1,0:T(8,128)(2,1)} %dynamic-slice_bitcast_fusion.2), channel_id=1, source_target_pairs={{0,130},{1,131},{4,134},{5,135},{8,138},{9,139},{12,142},{13,143},... | collective-permute-start | bytes 221192 | tf_op jit(solution)/shard_map/ppermute | solution.py:203
  12.5 8.2 %collective-permute-start.2 = (bf16[32,2304]{1,0:T(8,128)(2,1)S(1)}, bf16[32,2304]{1,0:T(8,128)(2,1)S(1)}, u32[]{:S(2)}, u32[]{:S(2)}) collective-permute-start(bf16[32,2304]{1,0:T(8,128)(2,1)S(1)} %dynamic-slice_bitcast_fusion.1), channel_id=1, source_target_pairs={{0,128},{1,129},{4,132},{5,133},{8,136},{9,137},{12,140},{13,141},... | collective-permute-start | bytes 442376 | tf_op jit(solution)/shard_map/ppermute | solution.py:203
  15.8 9.2 %copy-start.1 = (bf16[1,2,48,2304]{3,2,1,0:T(8,128)(2,1)S(1)}, bf16[1,2,48,2304]{3,2,1,0:T(8,128)(2,1)}, u32[]{:S(2)}) copy-start(bf16[1,2,48,2304]{3,2,1,0:T(8,128)(2,1)} %own.1) | copy-start | bytes 1327108
  15.9 9.2 %copy-start.2 = (bf16[768,768]{1,0:T(8,128)(2,1)S(1)}, bf16[768,768]{1,0:T(8,128)(2,1)}, u32[]{:S(2)}) copy-start(bf16[768,768]{1,0:T(8,128)(2,1)} %constant.162.clone.wz) | copy-start | bytes 3538948
  15.9 9.1 %copy-start.3 = (bf16[2,2,48,2304]{3,2,1,0:T(8,128)(2,1)S(1)}, bf16[2,2,48,2304]{3,2,1,0:T(8,128)(2,1)}, u32[]{:S(2)}) copy-start(bf16[2,2,48,2304]{3,2,1,0:T(8,128)(2,1)} %cond.1) | copy-start | bytes 2654212
  15.9 9.1 %copy-start.4 = (bf16[48,48]{1,0:T(8,128)(2,1)S(1)}, bf16[48,48]{1,0:T(8,128)(2,1)}, u32[]{:S(2)}) copy-start(bf16[48,48]{1,0:T(8,128)(2,1)} %constant.165.clone.ts) | copy-start | bytes 13828
  15.9 9.1 %copy-start.5 = (bf16[48,48]{1,0:T(8,128)(2,1)S(1)}, bf16[48,48]{1,0:T(8,128)(2,1)}, u32[]{:S(2)}) copy-start(bf16[48,48]{1,0:T(8,128)(2,1)} %constant.164.clone.tc) | copy-start | bytes 13828
  19.2 4.1 %copy-start.6 = (s32[1,5120]{1,0:T(1,128)S(1)}, s32[1,5120]{1,0:T(1,128)}, u32[]{:S(2)}) copy-start(s32[1,5120]{1,0:T(1,128)} %div.63) | copy-start | bytes 61444
  19.9 3.4 %copy-start.7 = (s32[1,5120]{1,0:T(1,128)S(1)}, s32[1,5120]{1,0:T(1,128)}, u32[]{:S(2)}) copy-start(s32[1,5120]{1,0:T(1,128)} %rem.211) | copy-start | bytes 61444
  19.9 3.4 %copy-start.8 = (pred[1,5120]{1,0:T(4,128)(4,1)S(1)}, pred[1,5120]{1,0:T(4,128)(4,1)}, u32[]{:S(2)}) copy-start(pred[1,5120]{1,0:T(4,128)(4,1)} %ne.187) | copy-start | bytes 15364
  21.6 3.4 %collective-permute-start.4 = (bf16[3,48,2304]{2,1,0:T(8,128)(2,1)S(1)}, bf16[3,48,2304]{2,1,0:T(8,128)(2,1)S(1)}, u32[]{:S(2)}, u32[]{:S(2)}) collective-permute-start(bf16[3,48,2304]{2,1,0:T(8,128)(2,1)S(1)} %pad_maximum_fusion.part), channel_id=1, source_target_pairs={{0,1},{1,0},{4,5},{5,4},{8,9},{9,8},{12,13},{13,12},{16,17},{17,16... | collective-permute-start | bytes 1990664 | tf_op jit(solution)/shard_map/ppermute | solution.py:203
  77.6 7.8 %collective-permute-start.9 = (bf16[64,1280]{1,0:T(8,128)(2,1)S(1)}, bf16[64,1280]{1,0:T(8,128)(2,1)S(1)}, u32[]{:S(2)}, u32[]{:S(2)}) collective-permute-start(bf16[64,1280]{1,0:T(8,128)(2,1)S(1)} %bitcast.26), channel_id=1, source_target_pairs={{0,4},{1,17},{4,0},{5,21},{8,12},{9,25},{12,8},{13,29},{16,20},{17... | collective-permute-start | bytes 491528 | tf_op jit(solution)/shard_map/ppermute | solution.py:203
  78.9 13.5 %all-to-all-start = ((bf16[16,8,640]{2,1,0:T(8,128)(2,1)}), bf16[16,8,640]{2,1,0:T(8,128)(2,1)S(1)}, u32[]{:S(2)}, u32[]{:S(2)}) async-start(bf16[16,8,640]{2,1,0:T(8,128)(2,1)} %get-tuple-element.8), calls=%async_computation | async-start | bytes 327680 | tf_op jit(solution)/shard_map/all_to_all | solution.py:274
  85.3 14.3 %copy-start.10 = (s32[4]{0:T(128)S(1)}, s32[4]{0:T(128)}, u32[]{:S(2)}) copy-start(s32[4]{0:T(128)} %constant.166.clone) | copy-start | bytes 52
  85.4 12.5 %collective-permute-start.10 = (bf16[128,1280]{1,0:T(8,128)(2,1)S(1)}, bf16[128,1280]{1,0:T(8,128)(2,1)S(1)}, u32[]{:S(2)}, u32[]{:S(2)}) collective-permute-start(bf16[128,1280]{1,0:T(8,128)(2,1)S(1)} %maximum_select_fusion.2), channel_id=1, source_target_pairs={{0,12},{1,49},{4,8},{5,53},{8,4},{9,57},{12,0},{13,61},{16,28},{17... | collective-permute-start | bytes 983048 | tf_op jit(solution)/shard_map/ppermute | solution.py:203
  92.4 5.4 %collective-permute-start.5 = (bf16[1,16,8,640]{3,2,1,0:T(8,128)(2,1)S(1)}, bf16[1,16,8,640]{3,2,1,0:T(8,128)(2,1)S(1)}, u32[]{:S(2)}, u32[]{:S(2)}) collective-permute-start(bf16[1,16,8,640]{3,2,1,0:T(8,128)(2,1)S(1)} %bitcast.24), channel_id=1, source_target_pairs={{0,64},{1,195},{4,68},{5,199},{8,72},{9,203},{12,76},{13,207},{16,... | collective-permute-start | bytes 491528 | tf_op jit(solution)/shard_map/ppermute | solution.py:203
  97.8 6.4 %collective-permute-start.6 = (bf16[2,16,8,640]{3,2,1,0:T(8,128)(2,1)S(1)}, bf16[2,16,8,640]{3,2,1,0:T(8,128)(2,1)S(1)}, u32[]{:S(2)}, u32[]{:S(2)}) collective-permute-start(bf16[2,16,8,640]{3,2,1,0:T(8,128)(2,1)S(1)} %maximum_select_fusion.1.l0), channel_id=1, source_target_pairs={{0,194},{1,65},{4,198},{5,69},{8,202},{9,73},{12,206},{13,77},{16,... | collective-permute-start | bytes 983048 | tf_op jit(solution)/shard_map/ppermute | solution.py:203
  98.1 15.3 %collective-permute-start.12 = (bf16[256,1280]{1,0:T(8,128)(2,1)S(1)}, bf16[256,1280]{1,0:T(8,128)(2,1)S(1)}, u32[]{:S(2)}, u32[]{:S(2)}) collective-permute-start(bf16[256,1280]{1,0:T(8,128)(2,1)S(1)} %maximum_select_fusion.r0), channel_id=1, source_target_pairs={{0,48},{1,13},{4,52},{5,1},{8,56},{9,5},{12,60},{13,9},{16,0},{17,... | collective-permute-start | bytes 1966088 | tf_op jit(solution)/shard_map/ppermute | solution.py:203
  99.0 14.7 %collective-permute-start.11 = (bf16[256,1280]{1,0:T(8,128)(2,1)S(1)}, bf16[256,1280]{1,0:T(8,128)(2,1)S(1)}, u32[]{:S(2)}, u32[]{:S(2)}) collective-permute-start(bf16[256,1280]{1,0:T(8,128)(2,1)S(1)} %maximum_select_fusion.r0), channel_id=1, source_target_pairs={{0,16},{1,5},{4,20},{5,9},{8,24},{9,13},{12,28},{13,1},{16,32},{17... | collective-permute-start | bytes 1966088 | tf_op jit(solution)/shard_map/ppermute | solution.py:203
  104.3 9.1 %collective-permute-start.7 = (bf16[2,16,8,640]{3,2,1,0:T(8,128)(2,1)S(1)}, bf16[2,16,8,640]{3,2,1,0:T(8,128)(2,1)S(1)}, u32[]{:S(2)}, u32[]{:S(2)}) collective-permute-start(bf16[2,16,8,640]{3,2,1,0:T(8,128)(2,1)S(1)} %collective-permute-done.6.l1), channel_id=1, source_target_pairs={{0,64},{1,195},{4,68},{5,199},{8,72},{9,203},{12,76},{13,207},{16,... | collective-permute-start | bytes 983048 | tf_op jit(solution)/shard_map/ppermute | solution.py:203
  113.4 8.4 %collective-permute-start.8 = (bf16[2,16,8,640]{3,2,1,0:T(8,128)(2,1)S(1)}, bf16[2,16,8,640]{3,2,1,0:T(8,128)(2,1)S(1)}, u32[]{:S(2)}, u32[]{:S(2)}) collective-permute-start(bf16[2,16,8,640]{3,2,1,0:T(8,128)(2,1)S(1)} %collective-permute-done.7.l2), channel_id=1, source_target_pairs={{0,194},{1,65},{4,198},{5,69},{8,202},{9,73},{12,206},{13,77},{16,... | collective-permute-start | bytes 983048 | tf_op jit(solution)/shard_map/ppermute | solution.py:203
  113.4 8.4 %collective-permute-start.14 = (bf16[128,1280]{1,0:T(8,128)(2,1)S(1)}, bf16[128,1280]{1,0:T(8,128)(2,1)S(1)}, u32[]{:S(2)}, u32[]{:S(2)}) collective-permute-start(bf16[128,1280]{1,0:T(8,128)(2,1)S(1)} %slice.37), channel_id=1, source_target_pairs={{0,48},{1,13},{4,52},{5,1},{8,56},{9,5},{12,60},{13,9},{16,0},{17,... | collective-permute-start | bytes 983048 | tf_op jit(solution)/shard_map/ppermute | solution.py:203
  113.8 8.0 %collective-permute-start.13 = (bf16[128,1280]{1,0:T(8,128)(2,1)S(1)}, bf16[128,1280]{1,0:T(8,128)(2,1)S(1)}, u32[]{:S(2)}, u32[]{:S(2)}) collective-permute-start(bf16[128,1280]{1,0:T(8,128)(2,1)S(1)} %slice.36), channel_id=1, source_target_pairs={{0,16},{1,5},{4,20},{5,9},{8,24},{9,13},{12,28},{13,1},{16,32},{17... | collective-permute-start | bytes 983048 | tf_op jit(solution)/shard_map/ppermute | solution.py:203
  125.1 10.2 %collective-permute-start.15 = (f32[320,640]{1,0:T(8,128)S(1)}, f32[320,640]{1,0:T(8,128)S(1)}, u32[]{:S(2)}, u32[]{:S(2)}) collective-permute-start(f32[320,640]{1,0:T(8,128)S(1)} %get-tuple-element.11), channel_id=1, source_target_pairs={{0,1},{1,0},{4,5},{5,4},{8,9},{9,8},{12,13},{13,12},{16,17},{17,16... | collective-permute-start | bytes 2457608 | tf_op jit(solution)/shard_map/ppermute | solution.py:203
where the time goes:
time: 154 us; the launch traced here: 153 us
  Pallas kernels  42.3 us (27%)
  waiting for transfers between devices  33.1 us (21%)
  starting transfers between devices  32.6 us (21%)
  blocking collectives  27.8 us (18%)
  local copies, waits for them, and re-layouts  11.5 us (7%)
  other arithmetic  5.12 us (3%)
    pallas_call x1, Pallas kernels, coefficients(): pl.pallas_call(coeff_kernel, out_shape=(jax.ShapeDtypeStruct((16, 8, 640)...  38.9 us
    ppermute x16, waiting for transfers between devices, send(): return lax.ppermute(values, AXES, pairs)  28.9 us
    ppermute x16, starting transfers between devices, send(): return lax.ppermute(values, AXES, pairs)  26.1 us
    all_to_all x1, blocking collectives, local(): tile = lax.all_to_all(tile, 'p', 0, 0, tiled=True)  14.1 us
    all_to_all x1, blocking collectives, local(): lax.all_to_all(right, ('h', 'p'), 0, 0, tiled=True).reshape(64, 1280)  13.7 us
    all_to_all x1, starting transfers between devices, local(): left = lax.all_to_all(left, ('y', 'x'), 0, 0, tiled=True)[None]  6.48 us
    all_to_all x1, waiting for transfers between devices, local(): left = lax.all_to_all(left, ('y', 'x'), 0, 0, tiled=True)[None]  4.28 us
    pallas_call x1, Pallas kernels, chi_tiles(): pl.pallas_call(chi_kernel, out_shape=(jax.ShapeDtypeStruct((320, 640), F3...  3.37 us
  transfers between devices with their start and end apart: 17, of which 8 were waited for; matrix products, arithmetic and copies ran while one was open for 8% of the time, Pallas kernels for 0%

commit v1 on v0

v1 whole, which is shorter than its diff:
```python
import functools
import math

import jax
import jax.numpy as jnp
import ml_dtypes
import numpy as np
from jax import lax
from jax.experimental import pallas as pl
from jax.experimental.pallas import tpu as pltpu
from jax.sharding import Mesh, PartitionSpec as P

NV = 4
N = 48
NG = 5120
F32 = jnp.float32
BF16 = jnp.bfloat16
WINDOW = 256
GROUP = 4
AXES = ("p", "y", "x", "h", "c")


def tables():
    k = np.arange(N)
    ang = (k[:, None] * k[None, :] % N).astype(np.float32) * np.float32(2.0 * math.pi / N)
    fac = np.float32(1.0 / math.sqrt(N))
    cos = (np.cos(ang) * fac).astype(ml_dtypes.bfloat16)
    sin = (np.sin(ang) * fac).astype(ml_dtypes.bfloat16)
    return cos, sin


def wide_tables():
    cos, sin = tables()
    cs = cos.astype(np.float32)
    sn = sin.astype(np.float32)
    eye8 = np.eye(8, dtype=np.float32)
    wz = np.zeros((2, 8, 48, 2, 48, 8), np.float32)
    for (f, g, tab) in ((0, 0, cs), (1, 0, sn), (0, 1, -sn), (1, 1, cs)):
        wz[f, :, :, g] = np.einsum("ab,kz->azkb", eye8, tab)
    wz = wz.reshape(768, 768)
    eye16 = np.eye(16, dtype=np.float32)
    wy = np.zeros((6, 16, 8, 2, 16, 24), np.float32)
    half = sn[:24].copy()
    half[0] = cs[24]
    for j, tab in enumerate((cs[:24], half)):
        wy[:, :, :, j] = np.einsum("ab,kmi->maibk", eye16, tab.reshape(24, 6, 8))
    wy = wy.reshape(768, 768)
    return wz.astype(ml_dtypes.bfloat16), wy.astype(ml_dtypes.bfloat16), cos, sin


def column_of(y, z):
    slot = jnp.where(y < 24, y, 24 + (N - y) % 24)
    return (z // 16) * 768 + (slot // 24) * 384 + (z % 16) * 24 + slot % 24


def densities(val, cond, cols, xs, k):
    for v in range(len(val)):
        vr, vi = val[v](cols)
        for c in range(2):
            cr = cond[c, 0, :, cols].astype(F32)
            ci = cond[c, 1, :, cols].astype(F32)
            rows = slice((v * 2 + c) * N, (v * 2 + c + 1) * N)
            xs[k, rows, 0:384] = (vr * cr + vi * ci).astype(BF16)
            xs[k, rows, 384:768] = (vr * ci - vi * cr).astype(BF16)


def sections(val, cond, wz, wy, xs, zs, s):
    count = zs.shape[1] // 2
    for i in range(6):
        densities(val, cond, slice(i * 384, (i + 1) * 384), xs, i % 2)
        out = jnp.dot(xs[i % 2], wz[...], preferred_element_type=F32).astype(BF16)
        for t in range(3):
            for f in range(2):
                zs[t, f * count : (f + 1) * count, i * 128 : (i + 1) * 128] = out[
                    :, f * 384 + t * 128 : f * 384 + (t + 1) * 128
                ]
    edge = lax.broadcasted_iota(jnp.int32, (1, 384), 1) % 24 == 0
    for t in range(3):
        cp = jnp.dot(zs[t], wy[:, :384], preferred_element_type=F32)
        sp = jnp.dot(zs[t], wy[:, 384:], preferred_element_type=F32)
        cre, cim, sre, sim = cp[:count], cp[count:], sp[:count], sp[count:]
        outs = (
            (jnp.where(edge, cre, cre + sim), jnp.where(edge, sre, cre - sim)),
            (jnp.where(edge, cim, cim - sre), jnp.where(edge, sim, cim + sre)),
        )
        for f in range(2):
            for e in range(2):
                cols = slice((t * 2 + e) * 384, (t * 2 + e + 1) * 384)
                s[f * count : (f + 1) * count, cols] = outs[f][e].astype(BF16)
    s[:, N * N :] = jnp.zeros((2 * count, WINDOW), BF16)


def select(s, tc, ts, starts, key, m, row):
    pairs = s.shape[0] // (2 * N)

    def step(group, _):
        todo = []
        for u in range(GROUP):
            n = group * GROUP + u
            cols = pl.ds(pl.multiple_of(n * 256, 128), 256)
            column = key[:, cols] >> 6
            kx = key[:, cols] & 63
            hot = jnp.where(lax.broadcasted_iota(jnp.int32, (N, 256), 0) == kx, 1.0, 0.0).astype(BF16)
            co = jnp.dot(tc[...], hot, preferred_element_type=F32)
            si = jnp.dot(ts[...], hot, preferred_element_type=F32)
            low = (starts[0, n * 256] >> 6) // 128 * 128
            high = starts[0, n * 256 + 255] >> 6

            def window(base, column=column, co=co, si=si):
                rows = lax.broadcasted_iota(jnp.int32, (WINDOW, 256), 0)
                pick = jnp.where(rows == column - base, 1.0, 0.0).astype(BF16)
                part = s[:, pl.ds(pl.multiple_of(base, 128), WINDOW)]
                full = jnp.dot(part, pick, preferred_element_type=F32).reshape(2, pairs, N, 256)
                re = jnp.sum(full[0] * co + full[1] * si, axis=1)
                im = jnp.sum(full[1] * co - full[0] * si, axis=1)
                return re, im

            re, im = window(low)
            m[0, row : row + pairs, cols] = re
            m[1, row : row + pairs, cols] = im
            todo.append((window, low, high, cols))
        for window, low, high, cols in todo:

            def more(k, _, window=window, low=low, cols=cols):
                re, im = window(low + k * WINDOW)
                m[0, row : row + pairs, cols] += re
                m[1, row : row + pairs, cols] += im
                return 0

            lax.fori_loop(1, (high - low) // WINDOW + 1, more, 0)
        return 0

    lax.fori_loop(0, 20 // GROUP, step, 0)


def own_kernel(val, cond, wz, wy, tc, ts, starts, key, m, xs, zs, s):
    def band(cols):
        return val[0, 0, :, cols].astype(F32), val[0, 1, :, cols].astype(F32)

    sections([band], cond, wz, wy, xs, zs, s)
    select(s, tc, ts, starts, key, m, 0)


def rest_kernel(core, part, other, cond, wz, wy, tc, ts, starts, key, back, w, owned, left, right, xs, zs, s, m, mo):
    first = core[0] == 0

    def band(v):
        def read(cols):
            a = part[v, :, cols].astype(F32)
            b = other[v, :, cols].astype(F32)
            return jnp.where(first, a, b), jnp.where(first, b, a)

        return read

    sections([band(v) for v in range(3)], cond, wz, wy, xs, zs, s)
    select(s, tc, ts, starts, key, m, 2)
    m[:, 0:2, :] = owned[...]

    def unsort(group, _):
        for u in range(4):
            cols = pl.ds(pl.multiple_of((group * 4 + u) * 128, 128), 128)
            place = jnp.broadcast_to(back[:, cols], (8, 128))
            source = place >> 7
            lane = place & 127
            outs = [jnp.zeros((8, 128), F32)] * 2
            for k in range(40):
                hit = source == k
                for f in range(2):
                    got = jnp.take_along_axis(m[f, :, k * 128 : (k + 1) * 128], lane, axis=1)
                    outs[f] = jnp.where(hit, got, outs[f])
            for f in range(2):
                mo[f, :, cols] = outs[f]
        return 0

    lax.fori_loop(0, 10, unsort, 0)
    for z in range(8):
        for f in range(2):
            right[z, :, f * 640 : (f + 1) * 640] = mo[f, :, z * 640 : (z + 1) * 640].astype(BF16)
    weight = w[...]
    for r in range(16):
        parts = []
        for f in range(2):
            for b in range(4):
                lane = ((b // 2 * 4 + r // 4) * 2 + b % 2) * 320 + 80 * (r % 4)
                parts.append(mo[f, :, lane : lane + 80])
        left[r] = (weight * jnp.concatenate(parts, axis=1)).astype(BF16)


VM = pl.BlockSpec(memory_space=pltpu.VMEM)
SM = pl.BlockSpec(memory_space=pltpu.SMEM)


def scratch(pairs):
    rows = pairs * N
    return [
        pltpu.VMEM((2, rows, 768), BF16),
        pltpu.VMEM((3, 2 * rows, 768), BF16),
        pltpu.VMEM((2 * rows, N * N + WINDOW), BF16),
    ]


def own_coefficients(val, cond, wide, key):
    return pl.pallas_call(
        own_kernel,
        out_shape=jax.ShapeDtypeStruct((2, 2, NG), F32),
        in_specs=[VM] * 6 + [SM, VM],
        out_specs=VM,
        scratch_shapes=scratch(2),
        compiler_params=pltpu.CompilerParams(vmem_limit_bytes=40 * 2**20),
        cost_estimate=pl.CostEstimate(flops=5 * 10**9, bytes_accessed=3 * 10**7, transcendentals=0),
    )(val, cond, *wide, key, key)


def coefficients(core, part, other, cond, wide, key, back, w, owned):
    return pl.pallas_call(
        rest_kernel,
        out_shape=(
            jax.ShapeDtypeStruct((16, 8, 640), BF16),
            jax.ShapeDtypeStruct((8, 8, 1280), BF16),
        ),
        in_specs=[SM] + [VM] * 7 + [SM] + [VM] * 4,
        out_specs=(VM, VM),
        scratch_shapes=scratch(6) + [pltpu.VMEM((2, 8, NG), F32)] * 2,
        compiler_params=pltpu.CompilerParams(vmem_limit_bytes=40 * 2**20),
        cost_estimate=pl.CostEstimate(flops=10**10, bytes_accessed=5 * 10**7, transcendentals=0),
    )(core, part, other, cond, *wide, key, key, back, w, owned)


def chi_kernel(core, place, rows, l0, l1, l2, l3, r0, r1, r2, r3, mine, theirs, lall, lk, rk):
    for i, piece in enumerate((l0, l1, l2, l3)):
        lall[2 * i : 2 * i + 2] = piece[...]
    base = 0
    for piece in (r0, r1, r2, r3):
        size = piece.shape[0]
        rk[base : base + size] = piece[...]
        base += size

    def fill(k, _):
        r = rows[k]
        for u in range(4):
            pair = [lall[place[2 * u + e], r].astype(F32) for e in range(2)]
            lk[pl.ds(pl.multiple_of(k * 64 + u * 16, 16), 16), :] = jnp.concatenate(pair, axis=0).astype(BF16)
        return 0

    lax.fori_loop(0, 16, fill, 0)
    first = core[0] == 0
    half = 320

    def product(f):
        return lax.dot_general(
            lk[:, f * half : (f + 1) * half], rk[...], (((0,), (0,)), ((), ())), preferred_element_type=F32
        )

    re = product(0)
    im = product(1)
    chi_re = re[:, :640] + im[:, 640:]
    chi_im = im[:, :640] - re[:, 640:]
    for k, chi in enumerate((chi_re, chi_im)):
        a, b = chi[:, :half], chi[:, half:]
        cols = slice(k * half, (k + 1) * half)
        mine[:, cols] = jnp.where(first, a, b)
        theirs[:, cols] = jnp.where(first, b, a)


def chi_tiles(core, place, rows, lefts, rights):
    vm = pl.BlockSpec(memory_space=pltpu.VMEM)
    sm = pl.BlockSpec(memory_space=pltpu.SMEM)
    return pl.pallas_call(
        chi_kernel,
        out_shape=(jax.ShapeDtypeStruct((320, 640), F32),) * 2,
        in_specs=[sm] * 3 + [vm] * 8,
        out_specs=(vm, vm),
        scratch_shapes=[
            pltpu.VMEM((8, 16, 8, 640), BF16),
            pltpu.VMEM((1024, 640), BF16),
            pltpu.VMEM((1024, 1280), BF16),
        ],
        compiler_params=pltpu.CompilerParams(vmem_limit_bytes=48 * 2**20),
    )(core, place, rows, *lefts, *rights)


def send(values, target):
    def index(z, y, x, c):
        return ((((z % 4) * 4 + y % 4) * 4 + x % 4) * 2 + (z % 8) // 4) * 2 + c

    pairs = [
        (index(z, y, x, c), index(*target(z, y, x, c)))
        for z in range(8)
        for y in range(4)
        for x in range(4)
        for c in range(2)
    ]
    return lax.ppermute(values, AXES, pairs)


def send_z(values, step):
    return send(values, lambda z, y, x, c: (z + step, y, x, c))


def send_core(values):
    return send(values, lambda z, y, x, c: (z, y, x, 1 - c))


def plane(axis, move):
    def target(z, y, x, c):
        if axis == c:
            return z, y, move(x), c
        return z, move(y), x, c

    return target


def outward(a):
    return a + 1 if a % 2 else a - 1


def inward(a):
    return a ^ 1


def ring(move):
    def target(z, y, x, c):
        return (move((z - c) % 8) + c) % 8, y, x, c

    return target


def assemble_kernel(tile, re, im):
    for f, out in enumerate((re, im)):
        parts = [tile[k, :, f * 320 : (f + 1) * 320].astype(F32) for k in range(4)]
        out[...] = jnp.concatenate(parts, axis=1)


def assemble(tile):
    return pl.pallas_call(
        assemble_kernel,
        out_shape=(jax.ShapeDtypeStruct((80, 1280), F32),) * 2,
        in_specs=[VM],
        out_specs=(VM, VM),
    )(tile)


def local(valence, conduction, valence_energy, conduction_energy, g_index):
    p, y, x, h, c = (lax.axis_index(a) for a in AXES)
    z = h * 4 + p
    core = jnp.reshape(c, (1,)).astype(jnp.int32)

    piece = lax.dynamic_index_in_dim(valence[0], c, 0, keepdims=False)
    part = jnp.concatenate(
        [
            send_z(piece, -1)[None],
            send_z(piece, 1)[None],
            jnp.concatenate([send_z(piece[:32], 2), send_z(piece[32:], -2)])[None],
        ]
    )
    other = send_core(part)
    bands = (p + jnp.array([0, 1, 3, 2])) % NV
    scale = math.sqrt(NV * 512)
    weight = 2.0 / ((valence_energy[bands][:, None] - conduction_energy[None, :]) * scale)

    order = g_index.reshape(2, 2, 4, 320).transpose(0, 2, 1, 3).reshape(NG)
    plane_part = order % (N * N)
    key = (column_of(plane_part // N, plane_part % N) << 6) | (order // (N * N))
    lanes = lax.iota(jnp.int32, NG)
    key, perm = lax.sort((key, lanes), num_keys=1)
    back = lax.sort((perm << 13) | lanes) & 8191
    key = key.reshape(1, NG)

    wide = [jnp.asarray(t) for t in wide_tables()]
    owned = own_coefficients(valence, conduction, wide, key)
    left, right = coefficients(
        core, part, other, conduction, wide, key, back.reshape(1, NG), weight.reshape(8, 1), owned
    )

    left = lax.all_to_all(left, ("y", "x"), 0, 0, tiled=True)
    left, right = lax.optimization_barrier((left, right))
    right = lax.all_to_all(right, ("h", "p"), 0, 0, tiled=True).reshape(64, 1280)

    zz = (z - c) % 8
    left0 = jnp.stack([left, send(left, ring(inward))])
    left1 = send(left0, ring(outward))
    left2 = send(left1, ring(inward))
    left3 = send(left2, ring(outward))
    near = zz ^ 1
    one = (zz + 2 * (zz % 2) - 1) % 8
    two = (near + 2 * (near % 2) - 1) % 8
    three = ((one ^ 1) + 2 * ((one ^ 1) % 2) - 1) % 8
    held = jnp.stack([zz, near, one, one ^ 1, two, two ^ 1, three, three ^ 1])
    held = (held + c) % 8
    place = jnp.argmax(held[None, :] == jnp.arange(8)[:, None], axis=1).astype(jnp.int32)

    moves = (lambda i: i + 1, lambda i: i - 1, lambda i: i + 2)
    offsets = jnp.array([0, 3, 1, 2])
    four = jnp.concatenate([right] + [send(right, plane(0, move)) for move in moves])
    rights = [four] + [send(four, plane(1, move)) for move in moves]
    aa = jnp.tile((jnp.where(c == 0, x, y) + offsets) % 4, 4)
    bb = jnp.repeat((jnp.where(c == 0, y, x) + offsets) % 4, 4)
    rows = jnp.where(c == 0, bb * 4 + aa, aa * 4 + bb).astype(jnp.int32)

    mine, theirs = chi_tiles(core, place, rows, (left0, left1, left2, left3), rights)
    tile = (mine + send_core(theirs)).astype(BF16).reshape(4, 80, 640)
    return assemble(lax.all_to_all(tile, "p", 0, 0, tiled=True))


def solution(mesh):
    fine = Mesh(mesh.devices.reshape(4, 4, 4, 2, 2), AXES)
    bands = P(AXES)
    return jax.shard_map(
        local,
        mesh=fine,
        in_specs=(P("p"), bands, P(), bands, P()),
        out_specs=(P(("p", "y", "x"), ("h", "c")),) * 2,
        check_vma=False,
    )
```

time: 154 us -> 149 us (0.968)
  Pallas kernels: 42.3 us -> 25.9 us
  other arithmetic: 5.12 us -> 19.1 us
  starting transfers between devices: 32.6 us -> 39.6 us
  waiting for transfers between devices: 33.1 us -> 27 us
  local copies, waits for them, and re-layouts: 11.5 us -> 6.93 us
    pallas_call x1 -> x3, Pallas kernels: 38.9 us -> 22.6 us  [the longest x1 15.3 us: coefficients(): pl.pallas_call(rest_kernel, out_shape=(jax.ShapeDtypeStruct((16, 8, 640),...]
    sort x0 -> x2, other arithmetic: none -> 13.6 us  [the longest x1 7.49 us: local(): back = lax.sort(perm << 13 | lanes) & 8191]
    ppermute x16, starting transfers between devices: 26.1 us -> 36 us  [send(): return lax.ppermute(values, AXES, pairs)]
    ppermute x16, waiting for transfers between devices: 28.9 us -> 20.5 us  [send(): return lax.ppermute(values, AXES, pairs)]
    all_to_all x1, starting transfers between devices: 6.48 us -> 3.56 us  [local(): lax.all_to_all(right, ('h', 'p'), 0, 0, tiled=True).reshape(64, 1280)]
    all_to_all x1, waiting for transfers between devices: 4.28 us -> 6.54 us  [local(): lax.all_to_all(right, ('h', 'p'), 0, 0, tiled=True).reshape(64, 1280)]
    squeeze x2 -> x0, local copies, waits for them, and re-layouts: 2.16 us -> none  [local(): return (full[0], full[1])]
  transfers between devices with their start and end apart: 17 -> 17, of which waited for: 8 -> 7; matrix products, arithmetic and copies ran while one was open for 8% -> 16% of each run, Pallas kernels for 0% -> 4%
where the time goes in v1:
time: 149 us; the launch traced here: 148 us
  starting transfers between devices  39.6 us (27%)
  blocking collectives  28.9 us (19%)
  waiting for transfers between devices  27 us (18%)
  Pallas kernels  25.9 us (17%)
  other arithmetic  19.1 us (13%)
  local copies, waits for them, and re-layouts  6.93 us (5%)
    ppermute x16, starting transfers between devices, send(): return lax.ppermute(values, AXES, pairs)  36 us
    ppermute x16, waiting for transfers between devices, send(): return lax.ppermute(values, AXES, pairs)  20.5 us
    pallas_call x1, Pallas kernels, coefficients(): pl.pallas_call(rest_kernel, out_shape=(jax.ShapeDtypeStruct((16, 8, 640),...  15.3 us
    all_to_all x1, blocking collectives, local(): return assemble(lax.all_to_all(tile, 'p', 0, 0, tiled=True))  14.9 us
    all_to_all x1, blocking collectives, local(): left = lax.all_to_all(left, ('y', 'x'), 0, 0, tiled=True)  14 us
    sort x1, other arithmetic, local(): back = lax.sort(perm << 13 | lanes) & 8191  7.49 us
    all_to_all x1, waiting for transfers between devices, local(): lax.all_to_all(right, ('h', 'p'), 0, 0, tiled=True).reshape(64, 1280)  6.54 us
    sort x1, other arithmetic, local(): key, perm = lax.sort((key, lanes), num_keys=1)  6.11 us
  transfers between devices with their start and end apart: 17, of which 7 were waited for; matrix products, arithmetic and copies ran while one was open for 16% of the time, Pallas kernels for 4%

profile of v1, /device:TPU:1, one launch (start us, length us, event | category | flops | bytes accessed | tf_op | source)
XLA Modules:
  0.0 148.3 jit_solution(9602110961035918208)
XLA Ops:
  0.6 1.0 dynamic-slice_bitcast_fusion
  1.6 2.5 %collective-permute-start.1 = (bf16[48,2304]{1,0:T(8,128)(2,1)S(1)}, bf16[48,2304]{1,0:T(8,128)(2,1)S(1)}, u32[]{:S(2)}, u32[]{:S(2)}) collective-permute-start(bf16[48,2304]{1,0:T(8,128)(2,1)S(1)} %dynamic-slice_bitcast_fusion), channel_id=1, source_target_pairs={{0,64},{1,65},{4,68},{5,69},{8,72},{9,73},{12,76},{13,77},{16,80},... | collective-permute-start | bytes 663560 | tf_op jit(solution)/shard_map/ppermute | solution.py:293
  4.2 4.0 %collective-permute-start = (bf16[48,2304]{1,0:T(8,128)(2,1)S(1)}, bf16[48,2304]{1,0:T(8,128)(2,1)S(1)}, u32[]{:S(2)}, u32[]{:S(2)}) collective-permute-start(bf16[48,2304]{1,0:T(8,128)(2,1)S(1)} %dynamic-slice_bitcast_fusion), channel_id=1, source_target_pairs={{0,194},{1,195},{4,198},{5,199},{8,202},{9,203},{12,206},{13,207},... | collective-permute-start | bytes 663560 | tf_op jit(solution)/shard_map/ppermute | solution.py:293
  8.2 1.5 %dynamic-slice_bitcast_fusion.2 = bf16[16,2304]{1,0:T(8,128)(2,1)} fusion(bf16[1,2,48,2304]{3,2,1,0:T(8,128)(2,1)} %val.1, s32[]{:T(128)S(6)} %select_n.133, s32[]{:T(128)S(6)} %add.180), kind=kLoop, calls=%fused_computation.8 | loop fusion | bytes 147464 | tf_op jit(solution)/shard_map/slice | solution.py:353
  9.7 1.8 %collective-permute-start.3 = (bf16[16,2304]{1,0:T(8,128)(2,1)}, bf16[16,2304]{1,0:T(8,128)(2,1)}, u32[]{:S(2)}, u32[]{:S(2)}) collective-permute-start(bf16[16,2304]{1,0:T(8,128)(2,1)} %dynamic-slice_bitcast_fusion.2), channel_id=1, source_target_pairs={{0,130},{1,131},{4,134},{5,135},{8,138},{9,139},{12,142},{13,143},... | collective-permute-start | bytes 221192 | tf_op jit(solution)/shard_map/ppermute | solution.py:293
  11.5 0.9 dynamic-slice_bitcast_fusion.1
  12.4 0.6 collective-permute-start.2
  13.1 0.7 sign_compare_fusion
  13.8 0.7 broadcast_remainder_fusion
  14.5 0.7 and_select_fusion.1
  15.4 0.1 ne.153
  15.6 0.1 rem.288
  15.8 0.1 div.55
  15.9 0.1 fusion.5
  16.0 6.1 %sort.29 = (s32[5120]{0:T(1024)S(1)}, s32[5120]{0:T(1024)S(1)}) sort(s32[5120]{0:T(1024)S(1)} %fusion.5, s32[5120]{0:T(1024)S(1)} %iota.20), dimensions={0}, to_apply=%region_1.2 | sort | flops 66560 | bytes 81920 | tf_op jit(solution)/shard_map/sort | solution.py:365
  22.2 0.6 gather_fusion
  22.8 0.7 multiply_divide_fusion
  23.6 0.6 iota.22
  24.2 7.5 %sort.30 = (s32[5120]{0:T(1024)}, s32[5120]{0:T(1024)}) sort(s32[5120]{0:T(1024)S(1)} %iota_or_fusion, s32[5120]{0:T(1024)} %iota.22), dimensions={0}, to_apply=%region_2.3 | sort | flops 66560 | bytes 81920 | tf_op jit(solution)/shard_map/sort | solution.py:366
  31.7 0.9 maximum_bitcast_fusion
  32.7 1.8 %collective-permute-start.4 = (bf16[3,48,2304]{2,1,0:T(8,128)(2,1)S(1)}, bf16[3,48,2304]{2,1,0:T(8,128)(2,1)S(1)}, u32[]{:S(2)}, u32[]{:S(2)}) collective-permute-start(bf16[3,48,2304]{2,1,0:T(8,128)(2,1)S(1)} %pad_maximum_fusion.part), channel_id=1, source_target_pairs={{0,1},{1,0},{4,5},{5,4},{8,9},{9,8},{12,13},{13,12},{16,17},{17,16... | collective-permute-start | bytes 1990664 | tf_op jit(solution)/shard_map/ppermute | solution.py:293
  34.5 0.7 broadcast_and_fusion
  35.3 1.3 copy-done.4
  36.6 5.2 %shard_map.122.owned = f32[2,2,5120]{2,1,0:T(2,128)S(1)} custom-call(bf16[1,2,48,2304]{3,2,1,0:T(8,128)(2,1)S(1)} %copy-done.1, bf16[2,2,48,2304]{3,2,1,0:T(8,128)(2,1)S(1)} %copy-done.2, bf16[768,768]{1,0:T(8,128)(2,1)S(1)} %copy-done.4, bf16[768,768]{1,0:T(8,128)(2,1)S(1)} %copy-done.3, bf16[48,48]{1,0:T(8,128)(2,1)S(1)} %copy-done.6, ...), custom_call_target="tpu_custom_call" | custom-call | flops 5000000000 | bytes 30000000 | tf_op jit(solution)/shard_map/pallas_call | solution.py:203
  41.8 15.3 %shard_map.123 = (bf16[16,8,640]{2,1,0:T(8,128)(2,1)S(1)}, bf16[8,8,1280]{2,1,0:T(8,128)(2,1)}) custom-call(s32[1]{0:T(128)} %bitcast.core, bf16[3,48,2304]{2,1,0:T(8,128)(2,1)S(1)} %pad_maximum_fusion.part, bf16[3,48,2304]{2,1,0:T(8,128)(2,1)S(1)} %collective-permute-done.4.other, bf16[2,2,48,2304]{3,2,1,0:T(8,128)(2,1)S(1)} %copy-done.2, ...), custom_call_target="tpu_custom_call" | custom-call | flops 10000000000 | bytes 50000000 | tf_op jit(solution)/shard_map/pallas_call | solution.py:215
  57.1 14.0 %all_to_all.15 = bf16[16,8,640]{2,1,0:T(8,128)(2,1)S(1)} all-to-all(bf16[16,8,640]{2,1,0:T(8,128)(2,1)S(1)} %get-tuple-element.17), channel_id=1, replica_groups=mesh['p'=4,'y'=4,'x'=4,'h'=2,'c'=2] {'y','x'}, dimensions={0} | all-to-all | bytes 327680 | tf_op jit(solution)/shard_map/all_to_all | solution.py:375
  71.2 2.9 %collective-permute-start.5 = (bf16[16,8,640]{2,1,0:T(8,128)(2,1)S(1)}, bf16[16,8,640]{2,1,0:T(8,128)(2,1)S(1)}, u32[]{:S(2)}, u32[]{:S(2)}) collective-permute-start(bf16[16,8,640]{2,1,0:T(8,128)(2,1)S(1)} %all_to_all.15), channel_id=1, source_target_pairs={{0,64},{1,195},{4,68},{5,199},{8,72},{9,203},{12,76},{13,207},{16,... | collective-permute-start | bytes 491528 | tf_op jit(solution)/shard_map/ppermute | solution.py:293
  74.0 3.6 %all-to-all-start.1 = ((bf16[8,8,1280]{2,1,0:T(8,128)(2,1)}), bf16[8,8,1280]{2,1,0:T(8,128)(2,1)S(1)}, u32[]{:S(2)}, u32[]{:S(2)}) async-start(bf16[8,8,1280]{2,1,0:T(8,128)(2,1)} %get-tuple-element.20), calls=%async_computation.1 | async-start | bytes 327680 | tf_op jit(solution)/shard_map/all_to_all | solution.py:377
  77.6 1.5 %collective-permute-start.6 = (bf16[2,16,8,640]{3,2,1,0:T(8,128)(2,1)S(1)}, bf16[2,16,8,640]{3,2,1,0:T(8,128)(2,1)S(1)}, u32[]{:S(2)}, u32[]{:S(2)}) collective-permute-start(bf16[2,16,8,640]{3,2,1,0:T(8,128)(2,1)S(1)} %pad_maximum_fusion.2.l0), channel_id=1, source_target_pairs={{0,194},{1,65},{4,198},{5,69},{8,202},{9,73},{12,206},{13,77},{16,... | collective-permute-start | bytes 983048 | tf_op jit(solution)/shard_map/ppermute | solution.py:293
  79.2 6.5 %all-to-all-done.1 = bf16[8,8,1280]{2,1,0:T(8,128)(2,1)S(1)} async-done(((bf16[8,8,1280]{2,1,0:T(8,128)(2,1)}), bf16[8,8,1280]{2,1,0:T(8,128)(2,1)S(1)}, u32[]{:S(2)}, u32[]{:S(2)}) %all-to-all-start.1) | async-done | bytes 163872 | tf_op jit(solution)/shard_map/all_to_all | solution.py:377
  85.7 0.4 collective-permute-start.11
  86.1 1.5 %collective-permute-start.10 = (bf16[64,1280]{1,0:T(8,128)(2,1)S(1)}, bf16[64,1280]{1,0:T(8,128)(2,1)S(1)}, u32[]{:S(2)}, u32[]{:S(2)}) collective-permute-start(bf16[64,1280]{1,0:T(8,128)(2,1)S(1)} %bitcast.35), channel_id=1, source_target_pairs={{0,12},{1,49},{4,0},{5,53},{8,4},{9,57},{12,8},{13,61},{16,28},{17... | collective-permute-start | bytes 491528 | tf_op jit(solution)/shard_map/ppermute | solution.py:293
  88.0 1.9 %collective-permute-start.7 = (bf16[2,16,8,640]{3,2,1,0:T(8,128)(2,1)S(1)}, bf16[2,16,8,640]{3,2,1,0:T(8,128)(2,1)S(1)}, u32[]{:S(2)}, u32[]{:S(2)}) collective-permute-start(bf16[2,16,8,640]{3,2,1,0:T(8,128)(2,1)S(1)} %collective-permute-done.6.l1), channel_id=1, source_target_pairs={{0,64},{1,195},{4,68},{5,199},{8,72},{9,203},{12,76},{13,207},{16,... | collective-permute-start | bytes 983048 | tf_op jit(solution)/shard_map/ppermute | solution.py:293
  89.9 1.5 collective-permute-done.11
  91.4 1.7 %collective-permute-done.9 = bf16[64,1280]{1,0:T(8,128)(2,1)S(1)} collective-permute-done((bf16[64,1280]{1,0:T(8,128)(2,1)S(1)}, bf16[64,1280]{1,0:T(8,128)(2,1)S(1)}, u32[]{:S(2)}, u32[]{:S(2)}) %collective-permute-start.9) | collective-permute-done | bytes 163872 | tf_op jit(solution)/shard_map/ppermute | solution.py:293
  93.2 1.3 collective-permute-start.14
  94.5 1.4 collective-permute-start.13
  96.0 0.7 collective-permute-start.8
  96.7 0.6 iota_reduce_fusion
  97.3 7.2 %collective-permute-done.14.r3 = bf16[256,1280]{1,0:T(8,128)(2,1)S(1)} collective-permute-done((bf16[256,1280]{1,0:T(8,128)(2,1)S(1)}, bf16[256,1280]{1,0:T(8,128)(2,1)S(1)}, u32[]{:S(2)}, u32[]{:S(2)}) %collective-permute-start.14) | collective-permute-done | bytes 655392 | tf_op jit(solution)/shard_map/ppermute | solution.py:293
  104.5 5.7 %collective-permute-done.13.r2 = bf16[256,1280]{1,0:T(8,128)(2,1)S(1)} collective-permute-done((bf16[256,1280]{1,0:T(8,128)(2,1)S(1)}, bf16[256,1280]{1,0:T(8,128)(2,1)S(1)}, u32[]{:S(2)}, u32[]{:S(2)}) %collective-permute-start.13) | collective-permute-done | bytes 655392 | tf_op jit(solution)/shard_map/ppermute | solution.py:293
  110.1 2.5 %collective-permute-done.12.r1 = bf16[256,1280]{1,0:T(8,128)(2,1)S(1)} collective-permute-done((bf16[256,1280]{1,0:T(8,128)(2,1)S(1)}, bf16[256,1280]{1,0:T(8,128)(2,1)S(1)}, u32[]{:S(2)}, u32[]{:S(2)}) %collective-permute-start.12) | collective-permute-done | bytes 655392 | tf_op jit(solution)/shard_map/ppermute | solution.py:293
  112.6 3.4 %shard_map.124 = (f32[320,640]{1,0:T(8,128)S(1)}, f32[320,640]{1,0:T(8,128)S(1)}) custom-call(s32[1]{0:T(128)} %bitcast.core, s32[8]{0:T(128)S(1)} %get-tuple-element.13.place, s32[16]{0:T(128)S(1)} %broadcast_select_fusion.rows, bf16[2,16,8,640]{3,2,1,0:T(8,128)(2,1)S(1)} %pad_maximum_fusion.2.l0, bf16[2,16,8,640]{3,2,1,0:T(8,128)(2,1)S(1)} %collective-permute-done.6.l1, ...), custom_call_target="tpu_custom_call" | custom-call | tf_op jit(solution)/shard_map/pallas_call | solution.py:268
  116.0 13.5 %collective-permute-start.15 = (f32[320,640]{1,0:T(8,128)S(1)}, f32[320,640]{1,0:T(8,128)S(1)}, u32[]{:S(2)}, u32[]{:S(2)}) collective-permute-start(f32[320,640]{1,0:T(8,128)S(1)} %get-tuple-element.22), channel_id=1, source_target_pairs={{0,1},{1,0},{4,5},{5,4},{8,9},{9,8},{12,13},{13,12},{16,17},{17,16... | collective-permute-start | bytes 2457608 | tf_op jit(solution)/shard_map/ppermute | solution.py:293
  129.4 2.0 %collective-permute-done.15 = f32[320,640]{1,0:T(8,128)S(1)} collective-permute-done((f32[320,640]{1,0:T(8,128)S(1)}, f32[320,640]{1,0:T(8,128)S(1)}, u32[]{:S(2)}, u32[]{:S(2)}) %collective-permute-start.15) | collective-permute-done | bytes 819232 | tf_op jit(solution)/shard_map/ppermute | solution.py:293
  131.4 0.1 add_convert_fusion
  131.5 14.9 %all_to_all.16.tile = bf16[4,80,640]{2,1,0:T(8,128)(2,1)} all-to-all(bf16[4,80,640]{2,1,0:T(8,128)(2,1)S(1)} %bitcast.33), channel_id=1, replica_groups=mesh['p'=4,'y'=4,'x'=4,'h'=2,'c'=2] {'p'}, dimensions={0} | all-to-all | bytes 819200 | tf_op jit(solution)/shard_map/all_to_all | solution.py:402
  146.4 2.0 %shard_map.125 = (f32[80,1280]{1,0:T(8,128)}, f32[80,1280]{1,0:T(8,128)}) custom-call(bf16[4,80,640]{2,1,0:T(8,128)(2,1)} %all_to_all.16.tile), custom_call_target="tpu_custom_call" | custom-call | tf_op jit(solution)/shard_map/pallas_call | solution.py:335
  (45 shorter events, 1.0 us)
Async XLA Ops:
  0.6 21.5 %copy-start = (f32[4]{0:T(128)S(1)}, f32[4]{0:T(128)}, u32[]{:S(2)}) copy-start(f32[4]{0:T(128)} %param.13) | copy-start | bytes 52
  1.6 31.0 %collective-permute-start.1 = (bf16[48,2304]{1,0:T(8,128)(2,1)S(1)}, bf16[48,2304]{1,0:T(8,128)(2,1)S(1)}, u32[]{:S(2)}, u32[]{:S(2)}) collective-permute-start(bf16[48,2304]{1,0:T(8,128)(2,1)S(1)} %dynamic-slice_bitcast_fusion), channel_id=1, source_target_pairs={{0,64},{1,65},{4,68},{5,69},{8,72},{9,73},{12,76},{13,77},{16,80},... | collective-permute-start | bytes 663560 | tf_op jit(solution)/shard_map/ppermute | solution.py:293
  4.2 28.5 %collective-permute-start = (bf16[48,2304]{1,0:T(8,128)(2,1)S(1)}, bf16[48,2304]{1,0:T(8,128)(2,1)S(1)}, u32[]{:S(2)}, u32[]{:S(2)}) collective-permute-start(bf16[48,2304]{1,0:T(8,128)(2,1)S(1)} %dynamic-slice_bitcast_fusion), channel_id=1, source_target_pairs={{0,194},{1,195},{4,198},{5,199},{8,202},{9,203},{12,206},{13,207},... | collective-permute-start | bytes 663560 | tf_op jit(solution)/shard_map/ppermute | solution.py:293
  9.7 22.0 %collective-permute-start.3 = (bf16[16,2304]{1,0:T(8,128)(2,1)}, bf16[16,2304]{1,0:T(8,128)(2,1)}, u32[]{:S(2)}, u32[]{:S(2)}) collective-permute-start(bf16[16,2304]{1,0:T(8,128)(2,1)} %dynamic-slice_bitcast_fusion.2), channel_id=1, source_target_pairs={{0,130},{1,131},{4,134},{5,135},{8,138},{9,139},{12,142},{13,143},... | collective-permute-start | bytes 221192 | tf_op jit(solution)/shard_map/ppermute | solution.py:293
  12.4 19.3 %collective-permute-start.2 = (bf16[32,2304]{1,0:T(8,128)(2,1)S(1)}, bf16[32,2304]{1,0:T(8,128)(2,1)S(1)}, u32[]{:S(2)}, u32[]{:S(2)}) collective-permute-start(bf16[32,2304]{1,0:T(8,128)(2,1)S(1)} %dynamic-slice_bitcast_fusion.1), channel_id=1, source_target_pairs={{0,128},{1,129},{4,132},{5,133},{8,136},{9,137},{12,140},{13,141},... | collective-permute-start | bytes 442376 | tf_op jit(solution)/shard_map/ppermute | solution.py:293
  15.9 19.4 %copy-start.6 = (bf16[48,48]{1,0:T(8,128)(2,1)S(1)}, bf16[48,48]{1,0:T(8,128)(2,1)}, u32[]{:S(2)}) copy-start(bf16[48,48]{1,0:T(8,128)(2,1)} %constant.207.clone.tc) | copy-start | bytes 13828
  16.0 19.3 %copy-start.3 = (bf16[768,768]{1,0:T(8,128)(2,1)S(1)}, bf16[768,768]{1,0:T(8,128)(2,1)}, u32[]{:S(2)}) copy-start(bf16[768,768]{1,0:T(8,128)(2,1)} %constant.206.clone.wy) | copy-start | bytes 3538948
  22.1 13.1 %copy-start.1 = (bf16[1,2,48,2304]{3,2,1,0:T(8,128)(2,1)S(1)}, bf16[1,2,48,2304]{3,2,1,0:T(8,128)(2,1)}, u32[]{:S(2)}) copy-start(bf16[1,2,48,2304]{3,2,1,0:T(8,128)(2,1)} %val.1) | copy-start | bytes 1327108
  22.1 13.1 %copy-start.2 = (bf16[2,2,48,2304]{3,2,1,0:T(8,128)(2,1)S(1)}, bf16[2,2,48,2304]{3,2,1,0:T(8,128)(2,1)}, u32[]{:S(2)}) copy-start(bf16[2,2,48,2304]{3,2,1,0:T(8,128)(2,1)} %cond.3) | copy-start | bytes 2654212
  22.2 13.1 %copy-start.5 = (bf16[48,48]{1,0:T(8,128)(2,1)S(1)}, bf16[48,48]{1,0:T(8,128)(2,1)}, u32[]{:S(2)}) copy-start(bf16[48,48]{1,0:T(8,128)(2,1)} %constant.208.clone.ts) | copy-start | bytes 13828
  32.7 9.1 %collective-permute-start.4 = (bf16[3,48,2304]{2,1,0:T(8,128)(2,1)S(1)}, bf16[3,48,2304]{2,1,0:T(8,128)(2,1)S(1)}, u32[]{:S(2)}, u32[]{:S(2)}) collective-permute-start(bf16[3,48,2304]{2,1,0:T(8,128)(2,1)S(1)} %pad_maximum_fusion.part), channel_id=1, source_target_pairs={{0,1},{1,0},{4,5},{5,4},{8,9},{9,8},{12,13},{13,12},{16,17},{17,16... | collective-permute-start | bytes 1990664 | tf_op jit(solution)/shard_map/ppermute | solution.py:293
  35.3 1.3 copy-start.4
  71.2 6.4 %collective-permute-start.5 = (bf16[16,8,640]{2,1,0:T(8,128)(2,1)S(1)}, bf16[16,8,640]{2,1,0:T(8,128)(2,1)S(1)}, u32[]{:S(2)}, u32[]{:S(2)}) collective-permute-start(bf16[16,8,640]{2,1,0:T(8,128)(2,1)S(1)} %all_to_all.15), channel_id=1, source_target_pairs={{0,64},{1,195},{4,68},{5,199},{8,72},{9,203},{12,76},{13,207},{16,... | collective-permute-start | bytes 491528 | tf_op jit(solution)/shard_map/ppermute | solution.py:293
  74.0 11.7 %all-to-all-start.1 = ((bf16[8,8,1280]{2,1,0:T(8,128)(2,1)}), bf16[8,8,1280]{2,1,0:T(8,128)(2,1)S(1)}, u32[]{:S(2)}, u32[]{:S(2)}) async-start(bf16[8,8,1280]{2,1,0:T(8,128)(2,1)} %get-tuple-element.20), calls=%async_computation.1 | async-start | bytes 327680 | tf_op jit(solution)/shard_map/all_to_all | solution.py:377
  77.6 10.4 %collective-permute-start.6 = (bf16[2,16,8,640]{3,2,1,0:T(8,128)(2,1)S(1)}, bf16[2,16,8,640]{3,2,1,0:T(8,128)(2,1)S(1)}, u32[]{:S(2)}, u32[]{:S(2)}) collective-permute-start(bf16[2,16,8,640]{3,2,1,0:T(8,128)(2,1)S(1)} %pad_maximum_fusion.2.l0), channel_id=1, source_target_pairs={{0,194},{1,65},{4,198},{5,69},{8,202},{9,73},{12,206},{13,77},{16,... | collective-permute-start | bytes 983048 | tf_op jit(solution)/shard_map/ppermute | solution.py:293
  85.7 5.7 %collective-permute-start.11 = (bf16[64,1280]{1,0:T(8,128)(2,1)S(1)}, bf16[64,1280]{1,0:T(8,128)(2,1)S(1)}, u32[]{:S(2)}, u32[]{:S(2)}) collective-permute-start(bf16[64,1280]{1,0:T(8,128)(2,1)S(1)} %bitcast.34), channel_id=1, source_target_pairs={{0,8},{1,33},{4,12},{5,37},{8,0},{9,41},{12,4},{13,45},{16,24},{17... | collective-permute-start | bytes 491528 | tf_op jit(solution)/shard_map/ppermute | solution.py:293
  86.1 5.3 %collective-permute-start.10 = (bf16[64,1280]{1,0:T(8,128)(2,1)S(1)}, bf16[64,1280]{1,0:T(8,128)(2,1)S(1)}, u32[]{:S(2)}, u32[]{:S(2)}) collective-permute-start(bf16[64,1280]{1,0:T(8,128)(2,1)S(1)} %bitcast.35), channel_id=1, source_target_pairs={{0,12},{1,49},{4,0},{5,53},{8,4},{9,57},{12,8},{13,61},{16,28},{17... | collective-permute-start | bytes 491528 | tf_op jit(solution)/shard_map/ppermute | solution.py:293
  87.7 5.5 %collective-permute-start.9 = (bf16[64,1280]{1,0:T(8,128)(2,1)S(1)}, bf16[64,1280]{1,0:T(8,128)(2,1)S(1)}, u32[]{:S(2)}, u32[]{:S(2)}) collective-permute-start(bf16[64,1280]{1,0:T(8,128)(2,1)S(1)} %bitcast.36), channel_id=1, source_target_pairs={{0,4},{1,17},{4,8},{5,21},{8,12},{9,25},{12,0},{13,29},{16,20},{17... | collective-permute-start | bytes 491528 | tf_op jit(solution)/shard_map/ppermute | solution.py:293
  88.0 8.0 %collective-permute-start.7 = (bf16[2,16,8,640]{3,2,1,0:T(8,128)(2,1)S(1)}, bf16[2,16,8,640]{3,2,1,0:T(8,128)(2,1)S(1)}, u32[]{:S(2)}, u32[]{:S(2)}) collective-permute-start(bf16[2,16,8,640]{3,2,1,0:T(8,128)(2,1)S(1)} %collective-permute-done.6.l1), channel_id=1, source_target_pairs={{0,64},{1,195},{4,68},{5,199},{8,72},{9,203},{12,76},{13,207},{16,... | collective-permute-start | bytes 983048 | tf_op jit(solution)/shard_map/ppermute | solution.py:293
  93.2 11.3 %collective-permute-start.14 = (bf16[256,1280]{1,0:T(8,128)(2,1)S(1)}, bf16[256,1280]{1,0:T(8,128)(2,1)S(1)}, u32[]{:S(2)}, u32[]{:S(2)}) collective-permute-start(bf16[256,1280]{1,0:T(8,128)(2,1)S(1)} %pad_maximum_fusion.1.r0), channel_id=1, source_target_pairs={{0,32},{1,9},{4,36},{5,13},{8,40},{9,1},{12,44},{13,5},{16,48},{17... | collective-permute-start | bytes 1966088 | tf_op jit(solution)/shard_map/ppermute | solution.py:293
  94.5 15.6 %collective-permute-start.13 = (bf16[256,1280]{1,0:T(8,128)(2,1)S(1)}, bf16[256,1280]{1,0:T(8,128)(2,1)S(1)}, u32[]{:S(2)}, u32[]{:S(2)}) collective-permute-start(bf16[256,1280]{1,0:T(8,128)(2,1)S(1)} %pad_maximum_fusion.1.r0), channel_id=1, source_target_pairs={{0,48},{1,13},{4,52},{5,1},{8,56},{9,5},{12,60},{13,9},{16,0},{17,... | collective-permute-start | bytes 1966088 | tf_op jit(solution)/shard_map/ppermute | solution.py:293
  95.9 16.7 %collective-permute-start.12 = (bf16[256,1280]{1,0:T(8,128)(2,1)S(1)}, bf16[256,1280]{1,0:T(8,128)(2,1)S(1)}, u32[]{:S(2)}, u32[]{:S(2)}) collective-permute-start(bf16[256,1280]{1,0:T(8,128)(2,1)S(1)} %pad_maximum_fusion.1.r0), channel_id=1, source_target_pairs={{0,16},{1,5},{4,20},{5,9},{8,24},{9,13},{12,28},{13,1},{16,32},{17... | collective-permute-start | bytes 1966088 | tf_op jit(solution)/shard_map/ppermute | solution.py:293
  96.0 16.6 %collective-permute-start.8 = (bf16[2,16,8,640]{3,2,1,0:T(8,128)(2,1)S(1)}, bf16[2,16,8,640]{3,2,1,0:T(8,128)(2,1)S(1)}, u32[]{:S(2)}, u32[]{:S(2)}) collective-permute-start(bf16[2,16,8,640]{3,2,1,0:T(8,128)(2,1)S(1)} %collective-permute-done.7.l2), channel_id=1, source_target_pairs={{0,194},{1,65},{4,198},{5,69},{8,202},{9,73},{12,206},{13,77},{16,... | collective-permute-start | bytes 983048 | tf_op jit(solution)/shard_map/ppermute | solution.py:293
  116.0 15.4 %collective-permute-start.15 = (f32[320,640]{1,0:T(8,128)S(1)}, f32[320,640]{1,0:T(8,128)S(1)}, u32[]{:S(2)}, u32[]{:S(2)}) collective-permute-start(f32[320,640]{1,0:T(8,128)S(1)} %get-tuple-element.22), channel_id=1, source_target_pairs={{0,1},{1,0},{4,5},{5,4},{8,9},{9,8},{12,13},{13,12},{16,17},{17,16... | collective-permute-start | bytes 2457608 | tf_op jit(solution)/shard_map/ppermute | solution.py:293

commit v2 on v1

--- a/solution.py
+++ b/solution.py
@@ -17,6 +17,9 @@
 BF16 = jnp.bfloat16
 WINDOW = 256
 GROUP = 4
+BUCKETS = 24
+VM = pl.BlockSpec(memory_space=pltpu.VMEM)
+SM = pl.BlockSpec(memory_space=pltpu.SMEM)
 AXES = ("p", "y", "x", "h", "c")
 
 
@@ -49,8 +52,49 @@
 
 
 def column_of(y, z):
-    slot = jnp.where(y < 24, y, 24 + (N - y) % 24)
-    return (z // 16) * 768 + (slot // 24) * 384 + (z % 16) * 24 + slot % 24
+    within = jnp.where(y < 24, y, jnp.where(y == 24, 0, N - y))
+    return (z >> 4) * 768 + jnp.where(y < 24, 0, 384) + (z & 15) * 24 + within
+
+
+def sort_kernel(key, keys, place, held):
+    bucket = key[...] >> 13
+    slots = lax.broadcasted_iota(jnp.int32, (BUCKETS, 128), 0)
+    before = jnp.zeros((BUCKETS, 128), F32)
+    for k in range(40):
+        mine = bucket[:, k * 128 : (k + 1) * 128]
+        held[k] = jnp.where(slots == mine, 1.0, 0.0)
+        before += jnp.where(mine < slots, 1.0, 0.0)
+    upto = lax.broadcasted_iota(jnp.int32, (128, 128), 0) <= lax.broadcasted_iota(jnp.int32, (128, 128), 1)
+    counts = jnp.dot(
+        held[...].reshape(40 * BUCKETS, 128).astype(BF16),
+        jnp.where(upto, 1.0, 0.0).astype(BF16),
+        preferred_element_type=F32,
+    ).reshape(40, BUCKETS, 128)
+    base = jnp.sum(before, axis=1, keepdims=True) - 1.0
+    for k in range(40):
+        rank = jnp.sum(held[k] * (base + counts[k]), axis=0, keepdims=True)
+        place[:, k * 128 : (k + 1) * 128] = rank.astype(jnp.int32)
+        base = base + counts[k, :, 127:128]
+    high = place[...] >> 7
+    low = place[...] & 127
+    at = lax.broadcasted_iota(jnp.int32, (40, NG), 0) == high
+    parts = (bucket, (key[...] >> 6) & 127, key[...] & 63)
+    rows = jnp.concatenate([jnp.where(at, v.astype(F32), 0.0) for v in parts], axis=0).astype(BF16)
+    cols = jnp.where(lax.broadcasted_iota(jnp.int32, (128, NG), 0) == low, 1.0, 0.0).astype(BF16)
+    moved = lax.dot_general(rows, cols, (((1,), (1,)), ((), ())), preferred_element_type=F32).astype(jnp.int32)
+    keys[...] = (moved[0:40] << 13) | (moved[40:80] << 6) | moved[80:120]
+
+
+def sort_waves(key):
+    return pl.pallas_call(
+        sort_kernel,
+        out_shape=(jax.ShapeDtypeStruct((40, 128), jnp.int32), jax.ShapeDtypeStruct((1, NG), jnp.int32)),
+        in_specs=[VM],
+        out_specs=(VM, VM),
+        scratch_shapes=[pltpu.VMEM((40, BUCKETS, 128), F32)],
+        compiler_params=pltpu.CompilerParams(vmem_limit_bytes=20 * 2**20),
+        cost_estimate=pl.CostEstimate(flops=10**9, bytes_accessed=10**6, transcendentals=0),
+    )(key)
 
 
 def densities(val, cond, cols, xs, k):
@@ -95,16 +139,18 @@
 
     def step(group, _):
         todo = []
+        keys = key[pl.ds(pl.multiple_of(group * 2 * GROUP, 8), 2 * GROUP), :]
         for u in range(GROUP):
             n = group * GROUP + u
             cols = pl.ds(pl.multiple_of(n * 256, 128), 256)
-            column = key[:, cols] >> 6
-            kx = key[:, cols] & 63
+            waves = jnp.concatenate([keys[2 * u : 2 * u + 1], keys[2 * u + 1 : 2 * u + 2]], axis=1)
+            column = waves >> 6
+            kx = waves & 63
             hot = jnp.where(lax.broadcasted_iota(jnp.int32, (N, 256), 0) == kx, 1.0, 0.0).astype(BF16)
             co = jnp.dot(tc[...], hot, preferred_element_type=F32)
             si = jnp.dot(ts[...], hot, preferred_element_type=F32)
-            low = (starts[0, n * 256] >> 6) // 128 * 128
-            high = starts[0, n * 256 + 255] >> 6
+            low = starts[2 * n, 0] >> 13 << 7
+            high = starts[2 * n + 1, 127] >> 6 | 127
 
             def window(base, column=column, co=co, si=si):
                 rows = lax.broadcasted_iota(jnp.int32, (WINDOW, 256), 0)
@@ -186,10 +232,6 @@
         left[r] = (weight * jnp.concatenate(parts, axis=1)).astype(BF16)
 
 
-VM = pl.BlockSpec(memory_space=pltpu.VMEM)
-SM = pl.BlockSpec(memory_space=pltpu.SMEM)
-
-
 def scratch(pairs):
     rows = pairs * N
     return [
@@ -349,33 +391,30 @@
     part = jnp.concatenate(
         [
             send_z(piece, -1)[None],
+            jnp.concatenate([send_z(piece[:32], 2), send_z(piece[32:], -2)])[None],
             send_z(piece, 1)[None],
-            jnp.concatenate([send_z(piece[:32], 2), send_z(piece[32:], -2)])[None],
         ]
     )
     other = send_core(part)
-    bands = (p + jnp.array([0, 1, 3, 2])) % NV
+
+    order = g_index.reshape(2, 2, 4, 320).transpose(0, 2, 1, 3).reshape(NG)
+    plane_part = lax.rem(order, N * N)
+    key = (column_of(lax.div(plane_part, N), lax.rem(plane_part, N)) << 6) | lax.div(order, N * N)
+    key, back = sort_waves(key.reshape(1, NG))
+
+    energies = lax.dynamic_slice(jnp.tile(valence_energy, 2), (p,), (NV,))
     scale = math.sqrt(NV * 512)
-    weight = 2.0 / ((valence_energy[bands][:, None] - conduction_energy[None, :]) * scale)
-
-    order = g_index.reshape(2, 2, 4, 320).transpose(0, 2, 1, 3).reshape(NG)
-    plane_part = order % (N * N)
-    key = (column_of(plane_part // N, plane_part % N) << 6) | (order // (N * N))
-    lanes = lax.iota(jnp.int32, NG)
-    key, perm = lax.sort((key, lanes), num_keys=1)
-    back = lax.sort((perm << 13) | lanes) & 8191
-    key = key.reshape(1, NG)
+    weight = 2.0 / ((energies[:, None] - conduction_energy[None, :]) * scale)
 
     wide = [jnp.asarray(t) for t in wide_tables()]
     owned = own_coefficients(valence, conduction, wide, key)
     left, right = coefficients(
-        core, part, other, conduction, wide, key, back.reshape(1, NG), weight.reshape(8, 1), owned
+        core, part, other, conduction, wide, key, back, weight.reshape(8, 1), owned
     )
 
+    right = lax.all_to_all(right, ("h", "p"), 0, 0, tiled=True).reshape(64, 1280)
+    left, right = lax.optimization_barrier((left, right))
     left = lax.all_to_all(left, ("y", "x"), 0, 0, tiled=True)
-    left, right = lax.optimization_barrier((left, right))
-    right = lax.all_to_all(right, ("h", "p"), 0, 0, tiled=True).reshape(64, 1280)
-
     zz = (z - c) % 8
     left0 = jnp.stack([left, send(left, ring(inward))])
     left1 = send(left0, ring(outward))

time: 149 us -> 132 us (0.89)
  waiting for transfers between devices: 27 us -> 45.8 us
  other arithmetic: 19.1 us -> 1.8 us
  blocking collectives: 28.9 us -> 14.7 us
  starting transfers between devices: 39.6 us -> 36.3 us
  local copies, waits for them, and re-layouts: 6.93 us -> 5.28 us
    all_to_all x1 -> x0, blocking collectives: 14 us -> none  [local(): left = lax.all_to_all(left, ('y', 'x'), 0, 0, tiled=True)]
    ppermute x16, waiting for transfers between devices: 20.5 us -> 34.3 us  [send(): return lax.ppermute(values, AXES, pairs)]
    sort x2 -> x0, other arithmetic: 13.6 us -> none  [the longest x1 7.49 us: local(): back = lax.sort(perm << 13 | lanes) & 8191]
    ppermute x16, starting transfers between devices: 36 us -> 24.2 us  [send(): return lax.ppermute(values, AXES, pairs)]
    all_to_all x0 -> x1, starting transfers between devices: none -> 6.73 us  [local(): left = lax.all_to_all(left, ('y', 'x'), 0, 0, tiled=True)]
    all_to_all x1, waiting for transfers between devices: 6.54 us -> 9.22 us  [local(): lax.all_to_all(right, ('h', 'p'), 0, 0, tiled=True).reshape(64, 1280)]
    all_to_all x0 -> x1, waiting for transfers between devices: none -> 2.34 us  [local(): left = lax.all_to_all(left, ('y', 'x'), 0, 0, tiled=True)]
    all_to_all x1, starting transfers between devices: 3.56 us -> 5.28 us  [local(): lax.all_to_all(right, ('h', 'p'), 0, 0, tiled=True).reshape(64, 1280)]
  transfers between devices with their start and end apart: 17 -> 18, of which waited for: 7 -> 11; matrix products, arithmetic and copies ran while one was open for 16% -> 4% of each run, Pallas kernels for 4% -> 5%
where the time goes in v2:
time: 132 us
  waiting for transfers between devices  45.8 us (35%)
  starting transfers between devices  36.3 us (27%)
  Pallas kernels  26.9 us (20%)
  blocking collectives  14.7 us (11%)
  local copies, waits for them, and re-layouts  5.28 us (4%)
  other arithmetic  1.8 us (1%)
    ppermute x16, waiting for transfers between devices, send(): return lax.ppermute(values, AXES, pairs)  34.3 us
    ppermute x16, starting transfers between devices, send(): return lax.ppermute(values, AXES, pairs)  24.2 us
    pallas_call x1, Pallas kernels, coefficients(): pl.pallas_call(rest_kernel, out_shape=(jax.ShapeDtypeStruct((16, 8, 640),...  15.4 us
    all_to_all x1, blocking collectives, local(): return assemble(lax.all_to_all(tile, 'p', 0, 0, tiled=True))  14.7 us
    all_to_all x1, waiting for transfers between devices, local(): lax.all_to_all(right, ('h', 'p'), 0, 0, tiled=True).reshape(64, 1280)  9.22 us
    all_to_all x1, starting transfers between devices, local(): left = lax.all_to_all(left, ('y', 'x'), 0, 0, tiled=True)  6.73 us
    all_to_all x1, starting transfers between devices, local(): lax.all_to_all(right, ('h', 'p'), 0, 0, tiled=True).reshape(64, 1280)  5.28 us
    pallas_call x1, Pallas kernels, own_coefficients(): pl.pallas_call(own_kernel, out_shape=jax.ShapeDtypeStruct((2, 2, NG), F32...  5.21 us
  transfers between devices with their start and end apart: 18, of which 11 were waited for; matrix products, arithmetic and copies ran while one was open for 4% of the time, Pallas kernels for 5%

profile of v2, /device:TPU:1, one launch (start us, length us, event | category | flops | bytes accessed | tf_op | source)
XLA Modules:
  0.0 131.8 jit_solution(12652538462870190042)
XLA Ops:
  0.6 1.0 dynamic-slice_bitcast_fusion
  1.6 2.5 %collective-permute-start.3 = (bf16[48,2304]{1,0:T(8,128)(2,1)S(1)}, bf16[48,2304]{1,0:T(8,128)(2,1)S(1)}, u32[]{:S(2)}, u32[]{:S(2)}) collective-permute-start(bf16[48,2304]{1,0:T(8,128)(2,1)S(1)} %dynamic-slice_bitcast_fusion), channel_id=1, source_target_pairs={{0,64},{1,65},{4,68},{5,69},{8,72},{9,73},{12,76},{13,77},{16,80},... | collective-permute-start | bytes 663560 | tf_op jit(solution)/shard_map/ppermute | solution.py:335
  4.1 4.0 %collective-permute-start = (bf16[48,2304]{1,0:T(8,128)(2,1)S(1)}, bf16[48,2304]{1,0:T(8,128)(2,1)S(1)}, u32[]{:S(2)}, u32[]{:S(2)}) collective-permute-start(bf16[48,2304]{1,0:T(8,128)(2,1)S(1)} %dynamic-slice_bitcast_fusion), channel_id=1, source_target_pairs={{0,194},{1,195},{4,198},{5,199},{8,202},{9,203},{12,206},{13,207},... | collective-permute-start | bytes 663560 | tf_op jit(solution)/shard_map/ppermute | solution.py:335
  8.2 0.9 dynamic-slice_bitcast_fusion.2
  9.1 1.8 %collective-permute-start.2 = (bf16[16,2304]{1,0:T(8,128)(2,1)S(1)}, bf16[16,2304]{1,0:T(8,128)(2,1)S(1)}, u32[]{:S(2)}, u32[]{:S(2)}) collective-permute-start(bf16[16,2304]{1,0:T(8,128)(2,1)S(1)} %dynamic-slice_bitcast_fusion.2), channel_id=1, source_target_pairs={{0,130},{1,131},{4,134},{5,135},{8,138},{9,139},{12,142},{13,143},... | collective-permute-start | bytes 221192 | tf_op jit(solution)/shard_map/ppermute | solution.py:335
  10.9 0.9 dynamic-slice_bitcast_fusion.1
  11.8 0.6 collective-permute-start.1
  12.4 0.7 shift-right-arithmetic_multiply_fusion
  13.2 0.1 reshape.239
  13.3 0.1 mul.66
  13.4 0.1 div.52
  13.5 0.1 div.54
  13.7 0.1 div.58
  13.9 0.1 mul.68
  14.3 1.0 collective-permute-done.2
  15.3 4.7 %collective-permute-done.1 = bf16[32,2304]{1,0:T(8,128)(2,1)S(1)} collective-permute-done((bf16[32,2304]{1,0:T(8,128)(2,1)S(1)}, bf16[32,2304]{1,0:T(8,128)(2,1)S(1)}, u32[]{:S(2)}, u32[]{:S(2)}) %collective-permute-start.1) | collective-permute-done | bytes 147488 | tf_op jit(solution)/shard_map/ppermute | solution.py:335
  20.1 1.8 %collective-permute-start.4 = (bf16[3,48,2304]{2,1,0:T(8,128)(2,1)S(1)}, bf16[3,48,2304]{2,1,0:T(8,128)(2,1)S(1)}, u32[]{:S(2)}, u32[]{:S(2)}) collective-permute-start(bf16[3,48,2304]{2,1,0:T(8,128)(2,1)S(1)} %pad_maximum_fusion.part), channel_id=1, source_target_pairs={{0,1},{1,0},{4,5},{5,4},{8,9},{9,8},{12,13},{13,12},{16,17},{17,16... | collective-permute-start | bytes 1990664 | tf_op jit(solution)/shard_map/ppermute | solution.py:335
  22.1 0.9 shard_map.113
  23.1 0.3 copy-done.1
  23.4 0.4 copy-done.2
  23.8 0.4 copy-done.3
  24.1 5.2 %shard_map.114.owned = f32[2,2,5120]{2,1,0:T(2,128)S(1)} custom-call(bf16[1,2,48,2304]{3,2,1,0:T(8,128)(2,1)S(1)} %copy-done, bf16[2,2,48,2304]{3,2,1,0:T(8,128)(2,1)S(1)} %copy-done.1, bf16[768,768]{1,0:T(8,128)(2,1)S(1)} %copy-done.3, bf16[768,768]{1,0:T(8,128)(2,1)S(1)} %copy-done.2, bf16[48,48]{1,0:T(8,128)(2,1)S(1)} %copy-done.5, ...), custom_call_target="tpu_custom_call" | custom-call | flops 5000000000 | bytes 30000000 | tf_op jit(solution)/shard_map/pallas_call | solution.py:245
  29.4 15.4 %shard_map.115 = (bf16[16,8,640]{2,1,0:T(8,128)(2,1)}, bf16[8,8,1280]{2,1,0:T(8,128)(2,1)}) custom-call(s32[1]{0:T(128)} %bitcast.core, bf16[3,48,2304]{2,1,0:T(8,128)(2,1)S(1)} %pad_maximum_fusion.part, bf16[3,48,2304]{2,1,0:T(8,128)(2,1)S(1)} %collective-permute-done.4.other, bf16[2,2,48,2304]{3,2,1,0:T(8,128)(2,1)S(1)} %copy-done.1, ...), custom_call_target="tpu_custom_call" | custom-call | flops 10000000000 | bytes 50000000 | tf_op jit(solution)/shard_map/pallas_call | solution.py:257
  44.8 5.3 %all-to-all-start = ((bf16[8,8,1280]{2,1,0:T(8,128)(2,1)}), bf16[8,8,1280]{2,1,0:T(8,128)(2,1)S(1)}, u32[]{:S(2)}, u32[]{:S(2)}) async-start(bf16[8,8,1280]{2,1,0:T(8,128)(2,1)} %get-tuple-element.15), calls=%async_computation | async-start | bytes 327680 | tf_op jit(solution)/shard_map/all_to_all | solution.py:415
  50.1 9.2 %all-to-all-done = bf16[8,8,1280]{2,1,0:T(8,128)(2,1)S(1)} async-done(((bf16[8,8,1280]{2,1,0:T(8,128)(2,1)}), bf16[8,8,1280]{2,1,0:T(8,128)(2,1)S(1)}, u32[]{:S(2)}, u32[]{:S(2)}) %all-to-all-start) | async-done | bytes 163872 | tf_op jit(solution)/shard_map/all_to_all | solution.py:415
  59.3 6.7 %all-to-all-start.1 = ((bf16[16,8,640]{2,1,0:T(8,128)(2,1)}), bf16[16,8,640]{2,1,0:T(8,128)(2,1)S(1)}, u32[]{:S(2)}, u32[]{:S(2)}) async-start(bf16[16,8,640]{2,1,0:T(8,128)(2,1)} %get-tuple-element.16), calls=%async_computation.1 | async-start | bytes 327680 | tf_op jit(solution)/shard_map/all_to_all | solution.py:417
  66.2 0.1 reshape.231
  66.3 0.1 stack.44
  66.4 2.9 %collective-permute-start.11 = (bf16[64,1280]{1,0:T(8,128)(2,1)S(1)}, bf16[64,1280]{1,0:T(8,128)(2,1)S(1)}, u32[]{:S(2)}, u32[]{:S(2)}) collective-permute-start(bf16[64,1280]{1,0:T(8,128)(2,1)S(1)} %bitcast.29), channel_id=1, source_target_pairs={{0,8},{1,33},{4,12},{5,37},{8,0},{9,41},{12,4},{13,45},{16,24},{17... | collective-permute-start | bytes 491528 | tf_op jit(solution)/shard_map/ppermute | solution.py:335
  69.3 0.9 collective-permute-start.10
  70.2 0.6 collective-permute-start.9
  70.8 2.3 %all-to-all-done.1 = bf16[16,8,640]{2,1,0:T(8,128)(2,1)S(1)} async-done(((bf16[16,8,640]{2,1,0:T(8,128)(2,1)}), bf16[16,8,640]{2,1,0:T(8,128)(2,1)S(1)}, u32[]{:S(2)}, u32[]{:S(2)}) %all-to-all-start.1) | async-done | bytes 163872 | tf_op jit(solution)/shard_map/all_to_all | solution.py:417
  73.1 5.7 %collective-permute-done.5 = bf16[16,8,640]{2,1,0:T(8,128)(2,1)S(1)} collective-permute-done((bf16[16,8,640]{2,1,0:T(8,128)(2,1)S(1)}, bf16[16,8,640]{2,1,0:T(8,128)(2,1)S(1)}, u32[]{:S(2)}, u32[]{:S(2)}) %collective-permute-start.5) | collective-permute-done | bytes 163872 | tf_op jit(solution)/shard_map/ppermute | solution.py:335
  78.8 0.1 collective-permute-start.6
  79.0 5.8 %collective-permute-done.6.l1 = bf16[2,16,8,640]{3,2,1,0:T(8,128)(2,1)S(1)} collective-permute-done((bf16[2,16,8,640]{3,2,1,0:T(8,128)(2,1)S(1)}, bf16[2,16,8,640]{3,2,1,0:T(8,128)(2,1)S(1)}, u32[]{:S(2)}, u32[]{:S(2)}) %collective-permute-start.6) | collective-permute-done | bytes 327712 | tf_op jit(solution)/shard_map/ppermute | solution.py:335
  84.9 0.6 collective-permute-start.14
  85.5 2.0 %collective-permute-start.13 = (bf16[256,1280]{1,0:T(8,128)(2,1)S(1)}, bf16[256,1280]{1,0:T(8,128)(2,1)S(1)}, u32[]{:S(2)}, u32[]{:S(2)}) collective-permute-start(bf16[256,1280]{1,0:T(8,128)(2,1)S(1)} %constant_dynamic-update-slice_fusion.r0), channel_id=1, source_target_pairs={{0,48},{1,13},{4,52},{5,1},{8,56},{9,5},{12,60},{13,9},{16,0},{17,... | collective-permute-start | bytes 1966088 | tf_op jit(solution)/shard_map/ppermute | solution.py:335
  87.4 5.2 %collective-permute-done.7.l2 = bf16[2,16,8,640]{3,2,1,0:T(8,128)(2,1)S(1)} collective-permute-done((bf16[2,16,8,640]{3,2,1,0:T(8,128)(2,1)S(1)}, bf16[2,16,8,640]{3,2,1,0:T(8,128)(2,1)S(1)}, u32[]{:S(2)}, u32[]{:S(2)}) %collective-permute-start.7) | collective-permute-done | bytes 327712 | tf_op jit(solution)/shard_map/ppermute | solution.py:335
  92.6 0.6 iota_reduce_fusion
  93.2 3.0 %collective-permute-done.14.r3 = bf16[256,1280]{1,0:T(8,128)(2,1)S(1)} collective-permute-done((bf16[256,1280]{1,0:T(8,128)(2,1)S(1)}, bf16[256,1280]{1,0:T(8,128)(2,1)S(1)}, u32[]{:S(2)}, u32[]{:S(2)}) %collective-permute-start.14) | collective-permute-done | bytes 655392 | tf_op jit(solution)/shard_map/ppermute | solution.py:335
  96.2 5.1 %collective-permute-done.13.r2 = bf16[256,1280]{1,0:T(8,128)(2,1)S(1)} collective-permute-done((bf16[256,1280]{1,0:T(8,128)(2,1)S(1)}, bf16[256,1280]{1,0:T(8,128)(2,1)S(1)}, u32[]{:S(2)}, u32[]{:S(2)}) %collective-permute-start.13) | collective-permute-done | bytes 655392 | tf_op jit(solution)/shard_map/ppermute | solution.py:335
  101.3 1.9 %collective-permute-done.12.r1 = bf16[256,1280]{1,0:T(8,128)(2,1)S(1)} collective-permute-done((bf16[256,1280]{1,0:T(8,128)(2,1)S(1)}, bf16[256,1280]{1,0:T(8,128)(2,1)S(1)}, u32[]{:S(2)}, u32[]{:S(2)}) %collective-permute-start.12) | collective-permute-done | bytes 655392 | tf_op jit(solution)/shard_map/ppermute | solution.py:335
  103.2 3.4 %shard_map.116 = (f32[320,640]{1,0:T(8,128)S(1)}, f32[320,640]{1,0:T(8,128)S(1)}) custom-call(s32[1]{0:T(128)} %bitcast.core, s32[8]{0:T(128)S(1)} %get-tuple-element.11.place, s32[16]{0:T(128)S(1)} %broadcast_select_fusion.rows, bf16[2,16,8,640]{3,2,1,0:T(8,128)(2,1)S(1)} %pad_maximum_fusion.1.l0, bf16[2,16,8,640]{3,2,1,0:T(8,128)(2,1)S(1)} %collective-permute-done.6.l1, ...), custom_call_target="tpu_custom_call" | custom-call | tf_op jit(solution)/shard_map/pallas_call | solution.py:310
  106.6 6.4 %collective-permute-start.15 = (f32[320,640]{1,0:T(8,128)S(1)}, f32[320,640]{1,0:T(8,128)S(1)}, u32[]{:S(2)}, u32[]{:S(2)}) collective-permute-start(f32[320,640]{1,0:T(8,128)S(1)} %get-tuple-element.19), channel_id=1, source_target_pairs={{0,1},{1,0},{4,5},{5,4},{8,9},{9,8},{12,13},{13,12},{16,17},{17,16... | collective-permute-start | bytes 2457608 | tf_op jit(solution)/shard_map/ppermute | solution.py:335
  113.0 2.0 %collective-permute-done.15 = f32[320,640]{1,0:T(8,128)S(1)} collective-permute-done((f32[320,640]{1,0:T(8,128)S(1)}, f32[320,640]{1,0:T(8,128)S(1)}, u32[]{:S(2)}, u32[]{:S(2)}) %collective-permute-start.15) | collective-permute-done | bytes 819232 | tf_op jit(solution)/shard_map/ppermute | solution.py:335
  114.9 0.1 add_convert_fusion
  115.1 14.7 %all_to_all.15.tile = bf16[4,80,640]{2,1,0:T(8,128)(2,1)} all-to-all(bf16[4,80,640]{2,1,0:T(8,128)(2,1)S(1)} %bitcast.27), channel_id=1, replica_groups=mesh['p'=4,'y'=4,'x'=4,'h'=2,'c'=2] {'p'}, dimensions={0} | all-to-all | bytes 819200 | tf_op jit(solution)/shard_map/all_to_all | solution.py:441
  129.8 2.0 %shard_map.117 = (f32[80,1280]{1,0:T(8,128)}, f32[80,1280]{1,0:T(8,128)}) custom-call(bf16[4,80,640]{2,1,0:T(8,128)(2,1)} %all_to_all.15.tile), custom_call_target="tpu_custom_call" | custom-call | tf_op jit(solution)/shard_map/pallas_call | solution.py:377
  (51 shorter events, 1.1 us)
Async XLA Ops:
  0.6 13.5 %copy-start.8 = (f32[4]{0:T(128)S(1)}, f32[4]{0:T(128)}, u32[]{:S(2)}) copy-start(f32[4]{0:T(128)} %param.12) | copy-start | bytes 52
  1.6 18.4 %collective-permute-start.3 = (bf16[48,2304]{1,0:T(8,128)(2,1)S(1)}, bf16[48,2304]{1,0:T(8,128)(2,1)S(1)}, u32[]{:S(2)}, u32[]{:S(2)}) collective-permute-start(bf16[48,2304]{1,0:T(8,128)(2,1)S(1)} %dynamic-slice_bitcast_fusion), channel_id=1, source_target_pairs={{0,64},{1,65},{4,68},{5,69},{8,72},{9,73},{12,76},{13,77},{16,80},... | collective-permute-start | bytes 663560 | tf_op jit(solution)/shard_map/ppermute | solution.py:335
  4.1 15.9 %collective-permute-start = (bf16[48,2304]{1,0:T(8,128)(2,1)S(1)}, bf16[48,2304]{1,0:T(8,128)(2,1)S(1)}, u32[]{:S(2)}, u32[]{:S(2)}) collective-permute-start(bf16[48,2304]{1,0:T(8,128)(2,1)S(1)} %dynamic-slice_bitcast_fusion), channel_id=1, source_target_pairs={{0,194},{1,195},{4,198},{5,199},{8,202},{9,203},{12,206},{13,207},... | collective-permute-start | bytes 663560 | tf_op jit(solution)/shard_map/ppermute | solution.py:335
  9.1 6.2 %collective-permute-start.2 = (bf16[16,2304]{1,0:T(8,128)(2,1)S(1)}, bf16[16,2304]{1,0:T(8,128)(2,1)S(1)}, u32[]{:S(2)}, u32[]{:S(2)}) collective-permute-start(bf16[16,2304]{1,0:T(8,128)(2,1)S(1)} %dynamic-slice_bitcast_fusion.2), channel_id=1, source_target_pairs={{0,130},{1,131},{4,134},{5,135},{8,138},{9,139},{12,142},{13,143},... | collective-permute-start | bytes 221192 | tf_op jit(solution)/shard_map/ppermute | solution.py:335
  11.8 8.2 %collective-permute-start.1 = (bf16[32,2304]{1,0:T(8,128)(2,1)S(1)}, bf16[32,2304]{1,0:T(8,128)(2,1)S(1)}, u32[]{:S(2)}, u32[]{:S(2)}) collective-permute-start(bf16[32,2304]{1,0:T(8,128)(2,1)S(1)} %dynamic-slice_bitcast_fusion.1), channel_id=1, source_target_pairs={{0,128},{1,129},{4,132},{5,133},{8,136},{9,137},{12,140},{13,141},... | collective-permute-start | bytes 442376 | tf_op jit(solution)/shard_map/ppermute | solution.py:335
  13.3 8.6 %copy-start.7 = (f32[2]{0:T(128)S(1)}, f32[2]{0:T(128)}, u32[]{:S(2)}) copy-start(f32[2]{0:T(128)} %param.13) | copy-start | bytes 28
  20.0 3.0 %copy-start.5 = (bf16[48,48]{1,0:T(8,128)(2,1)S(1)}, bf16[48,48]{1,0:T(8,128)(2,1)}, u32[]{:S(2)}) copy-start(bf16[48,48]{1,0:T(8,128)(2,1)} %constant.137.clone.tc) | copy-start | bytes 13828
  20.1 9.2 %collective-permute-start.4 = (bf16[3,48,2304]{2,1,0:T(8,128)(2,1)S(1)}, bf16[3,48,2304]{2,1,0:T(8,128)(2,1)S(1)}, u32[]{:S(2)}, u32[]{:S(2)}) collective-permute-start(bf16[3,48,2304]{2,1,0:T(8,128)(2,1)S(1)} %pad_maximum_fusion.part), channel_id=1, source_target_pairs={{0,1},{1,0},{4,5},{5,4},{8,9},{9,8},{12,13},{13,12},{16,17},{17,16... | collective-permute-start | bytes 1990664 | tf_op jit(solution)/shard_map/ppermute | solution.py:335
  22.1 1.0 copy-start
  22.1 1.3 copy-start.1
  22.1 1.7 %copy-start.2 = (bf16[768,768]{1,0:T(8,128)(2,1)S(1)}, bf16[768,768]{1,0:T(8,128)(2,1)}, u32[]{:S(2)}) copy-start(bf16[768,768]{1,0:T(8,128)(2,1)} %constant.136.clone.wy) | copy-start | bytes 3538948
  22.1 2.0 %copy-start.3 = (bf16[768,768]{1,0:T(8,128)(2,1)S(1)}, bf16[768,768]{1,0:T(8,128)(2,1)}, u32[]{:S(2)}) copy-start(bf16[768,768]{1,0:T(8,128)(2,1)} %constant.135.clone.wz) | copy-start | bytes 3538948
  22.1 2.0 %copy-start.4 = (bf16[48,48]{1,0:T(8,128)(2,1)S(1)}, bf16[48,48]{1,0:T(8,128)(2,1)}, u32[]{:S(2)}) copy-start(bf16[48,48]{1,0:T(8,128)(2,1)} %constant.138.clone.ts) | copy-start | bytes 13828
  29.4 36.7 %copy-start.6 = (s32[4]{0:T(128)S(1)}, s32[4]{0:T(128)}, u32[]{:S(2)}) copy-start(s32[4]{0:T(128)} %constant.139.clone) | copy-start | bytes 52
  44.8 14.5 %all-to-all-start = ((bf16[8,8,1280]{2,1,0:T(8,128)(2,1)}), bf16[8,8,1280]{2,1,0:T(8,128)(2,1)S(1)}, u32[]{:S(2)}, u32[]{:S(2)}) async-start(bf16[8,8,1280]{2,1,0:T(8,128)(2,1)} %get-tuple-element.15), calls=%async_computation | async-start | bytes 327680 | tf_op jit(solution)/shard_map/all_to_all | solution.py:415
  59.3 13.8 %all-to-all-start.1 = ((bf16[16,8,640]{2,1,0:T(8,128)(2,1)}), bf16[16,8,640]{2,1,0:T(8,128)(2,1)S(1)}, u32[]{:S(2)}, u32[]{:S(2)}) async-start(bf16[16,8,640]{2,1,0:T(8,128)(2,1)} %get-tuple-element.16), calls=%async_computation.1 | async-start | bytes 327680 | tf_op jit(solution)/shard_map/all_to_all | solution.py:417
  66.4 18.4 %collective-permute-start.11 = (bf16[64,1280]{1,0:T(8,128)(2,1)S(1)}, bf16[64,1280]{1,0:T(8,128)(2,1)S(1)}, u32[]{:S(2)}, u32[]{:S(2)}) collective-permute-start(bf16[64,1280]{1,0:T(8,128)(2,1)S(1)} %bitcast.29), channel_id=1, source_target_pairs={{0,8},{1,33},{4,12},{5,37},{8,0},{9,41},{12,4},{13,45},{16,24},{17... | collective-permute-start | bytes 491528 | tf_op jit(solution)/shard_map/ppermute | solution.py:335
  69.3 9.7 %collective-permute-start.10 = (bf16[64,1280]{1,0:T(8,128)(2,1)S(1)}, bf16[64,1280]{1,0:T(8,128)(2,1)S(1)}, u32[]{:S(2)}, u32[]{:S(2)}) collective-permute-start(bf16[64,1280]{1,0:T(8,128)(2,1)S(1)} %bitcast.30), channel_id=1, source_target_pairs={{0,12},{1,49},{4,0},{5,53},{8,4},{9,57},{12,8},{13,61},{16,28},{17... | collective-permute-start | bytes 491528 | tf_op jit(solution)/shard_map/ppermute | solution.py:335
  70.2 8.7 %collective-permute-start.9 = (bf16[64,1280]{1,0:T(8,128)(2,1)S(1)}, bf16[64,1280]{1,0:T(8,128)(2,1)S(1)}, u32[]{:S(2)}, u32[]{:S(2)}) collective-permute-start(bf16[64,1280]{1,0:T(8,128)(2,1)S(1)} %bitcast.31), channel_id=1, source_target_pairs={{0,4},{1,17},{4,8},{5,21},{8,12},{9,25},{12,0},{13,29},{16,20},{17... | collective-permute-start | bytes 491528 | tf_op jit(solution)/shard_map/ppermute | solution.py:335
  73.1 5.7 %collective-permute-start.5 = (bf16[16,8,640]{2,1,0:T(8,128)(2,1)S(1)}, bf16[16,8,640]{2,1,0:T(8,128)(2,1)S(1)}, u32[]{:S(2)}, u32[]{:S(2)}) collective-permute-start(bf16[16,8,640]{2,1,0:T(8,128)(2,1)S(1)} %all-to-all-done.1), channel_id=1, source_target_pairs={{0,64},{1,195},{4,68},{5,199},{8,72},{9,203},{12,76},{13,207},{16,... | collective-permute-start | bytes 491528 | tf_op jit(solution)/shard_map/ppermute | solution.py:335
  78.8 6.0 %collective-permute-start.6 = (bf16[2,16,8,640]{3,2,1,0:T(8,128)(2,1)S(1)}, bf16[2,16,8,640]{3,2,1,0:T(8,128)(2,1)S(1)}, u32[]{:S(2)}, u32[]{:S(2)}) collective-permute-start(bf16[2,16,8,640]{3,2,1,0:T(8,128)(2,1)S(1)} %pad_maximum_fusion.1.l0), channel_id=1, source_target_pairs={{0,194},{1,65},{4,198},{5,69},{8,202},{9,73},{12,206},{13,77},{16,... | collective-permute-start | bytes 983048 | tf_op jit(solution)/shard_map/ppermute | solution.py:335
  84.8 7.7 %collective-permute-start.7 = (bf16[2,16,8,640]{3,2,1,0:T(8,128)(2,1)S(1)}, bf16[2,16,8,640]{3,2,1,0:T(8,128)(2,1)S(1)}, u32[]{:S(2)}, u32[]{:S(2)}) collective-permute-start(bf16[2,16,8,640]{3,2,1,0:T(8,128)(2,1)S(1)} %collective-permute-done.6.l1), channel_id=1, source_target_pairs={{0,64},{1,195},{4,68},{5,199},{8,72},{9,203},{12,76},{13,207},{16,... | collective-permute-start | bytes 983048 | tf_op jit(solution)/shard_map/ppermute | solution.py:335
  84.9 11.4 %collective-permute-start.14 = (bf16[256,1280]{1,0:T(8,128)(2,1)S(1)}, bf16[256,1280]{1,0:T(8,128)(2,1)S(1)}, u32[]{:S(2)}, u32[]{:S(2)}) collective-permute-start(bf16[256,1280]{1,0:T(8,128)(2,1)S(1)} %constant_dynamic-update-slice_fusion.r0), channel_id=1, source_target_pairs={{0,32},{1,9},{4,36},{5,13},{8,40},{9,1},{12,44},{13,5},{16,48},{17... | collective-permute-start | bytes 1966088 | tf_op jit(solution)/shard_map/ppermute | solution.py:335
  85.5 15.9 %collective-permute-start.13 = (bf16[256,1280]{1,0:T(8,128)(2,1)S(1)}, bf16[256,1280]{1,0:T(8,128)(2,1)S(1)}, u32[]{:S(2)}, u32[]{:S(2)}) collective-permute-start(bf16[256,1280]{1,0:T(8,128)(2,1)S(1)} %constant_dynamic-update-slice_fusion.r0), channel_id=1, source_target_pairs={{0,48},{1,13},{4,52},{5,1},{8,56},{9,5},{12,60},{13,9},{16,0},{17,... | collective-permute-start | bytes 1966088 | tf_op jit(solution)/shard_map/ppermute | solution.py:335
  87.4 15.8 %collective-permute-start.12 = (bf16[256,1280]{1,0:T(8,128)(2,1)S(1)}, bf16[256,1280]{1,0:T(8,128)(2,1)S(1)}, u32[]{:S(2)}, u32[]{:S(2)}) collective-permute-start(bf16[256,1280]{1,0:T(8,128)(2,1)S(1)} %constant_dynamic-update-slice_fusion.r0), channel_id=1, source_target_pairs={{0,16},{1,5},{4,20},{5,9},{8,24},{9,13},{12,28},{13,1},{16,32},{17... | collective-permute-start | bytes 1966088 | tf_op jit(solution)/shard_map/ppermute | solution.py:335
  92.6 10.6 %collective-permute-start.8 = (bf16[2,16,8,640]{3,2,1,0:T(8,128)(2,1)S(1)}, bf16[2,16,8,640]{3,2,1,0:T(8,128)(2,1)S(1)}, u32[]{:S(2)}, u32[]{:S(2)}) collective-permute-start(bf16[2,16,8,640]{3,2,1,0:T(8,128)(2,1)S(1)} %collective-permute-done.7.l2), channel_id=1, source_target_pairs={{0,194},{1,65},{4,198},{5,69},{8,202},{9,73},{12,206},{13,77},{16,... | collective-permute-start | bytes 983048 | tf_op jit(solution)/shard_map/ppermute | solution.py:335
  106.6 8.4 %collective-permute-start.15 = (f32[320,640]{1,0:T(8,128)S(1)}, f32[320,640]{1,0:T(8,128)S(1)}, u32[]{:S(2)}, u32[]{:S(2)}) collective-permute-start(f32[320,640]{1,0:T(8,128)S(1)} %get-tuple-element.19), channel_id=1, source_target_pairs={{0,1},{1,0},{4,5},{5,4},{8,9},{9,8},{12,13},{13,12},{16,17},{17,16... | collective-permute-start | bytes 2457608 | tf_op jit(solution)/shard_map/ppermute | solution.py:335

commit v3 on v2

--- a/solution.py
+++ b/solution.py
@@ -321,12 +321,13 @@
     )(core, place, rows, *lefts, *rights)
 
 
+def device(z, y, x, c):
+    return ((((z % 4) * 4 + y % 4) * 4 + x % 4) * 2 + (z % 8) // 4) * 2 + c
+
+
 def send(values, target):
-    def index(z, y, x, c):
-        return ((((z % 4) * 4 + y % 4) * 4 + x % 4) * 2 + (z % 8) // 4) * 2 + c
-
     pairs = [
-        (index(z, y, x, c), index(*target(z, y, x, c)))
+        (device(z, y, x, c), device(*target(z, y, x, c)))
         for z in range(8)
         for y in range(4)
         for x in range(4)
@@ -365,6 +366,17 @@
         return (move((z - c) % 8) + c) % 8, y, x, c
 
     return target
+
+
+def pair_exchange(left):
+    groups = []
+    for c in range(2):
+        for k in range(4):
+            zs = [(2 * k + e + c) % 8 for e in range(2)]
+            groups.append([device(z, y, x, c) for z in zs for y in range(4) for x in range(4)])
+    twice = jnp.concatenate([left, left])
+    got = lax.all_to_all(twice, AXES, 0, 0, axis_index_groups=groups, tiled=True)
+    return got.reshape(2, 16, 8, 640)
 
 
 def assemble_kernel(tile, re, im):
@@ -391,11 +403,10 @@
     part = jnp.concatenate(
         [
             send_z(piece, -1)[None],
-            jnp.concatenate([send_z(piece[:32], 2), send_z(piece[32:], -2)])[None],
+            send(piece, lambda z, y, x, c: (z + 2 - 4 * c, y, x, c))[None],
             send_z(piece, 1)[None],
         ]
     )
-    other = send_core(part)
 
     order = g_index.reshape(2, 2, 4, 320).transpose(0, 2, 1, 3).reshape(NG)
     plane_part = lax.rem(order, N * N)
@@ -408,15 +419,16 @@
 
     wide = [jnp.asarray(t) for t in wide_tables()]
     owned = own_coefficients(valence, conduction, wide, key)
+    part, owned = lax.optimization_barrier((part, owned))
+    other = send_core(part)
     left, right = coefficients(
         core, part, other, conduction, wide, key, back, weight.reshape(8, 1), owned
     )
 
     right = lax.all_to_all(right, ("h", "p"), 0, 0, tiled=True).reshape(64, 1280)
     left, right = lax.optimization_barrier((left, right))
-    left = lax.all_to_all(left, ("y", "x"), 0, 0, tiled=True)
+    left0 = pair_exchange(left)
     zz = (z - c) % 8
-    left0 = jnp.stack([left, send(left, ring(inward))])
     left1 = send(left0, ring(outward))
     left2 = send(left1, ring(inward))
     left3 = send(left2, ring(outward))
@@ -424,7 +436,7 @@
     one = (zz + 2 * (zz % 2) - 1) % 8
     two = (near + 2 * (near % 2) - 1) % 8
     three = ((one ^ 1) + 2 * ((one ^ 1) % 2) - 1) % 8
-    held = jnp.stack([zz, near, one, one ^ 1, two, two ^ 1, three, three ^ 1])
+    held = jnp.stack([zz & 6, zz | 1, one & 6, one | 1, two & 6, two | 1, three & 6, three | 1])
     held = (held + c) % 8
     place = jnp.argmax(held[None, :] == jnp.arange(8)[:, None], axis=1).astype(jnp.int32)
 

time: 132 us -> 123 us (0.932)
  waiting for transfers between devices: 45.8 us -> 28.9 us
  blocking collectives: 14.7 us -> 28.6 us
  starting transfers between devices: 36.3 us -> 29.4 us
  other arithmetic: 1.8 us -> 3.42 us
    all_to_all x0 -> x1, blocking collectives: none -> 13.9 us  [local(): lax.all_to_all(right, ('h', 'p'), 0, 0, tiled=True).reshape(64, 1280)]
    ppermute x16 -> x14, waiting for transfers between devices: 34.3 us -> 25 us  [send(): return lax.ppermute(values, AXES, pairs)]
    all_to_all x2 -> x1, waiting for transfers between devices: 11.6 us -> 3.88 us  [pair_exchange(): lax.all_to_all(twice, AXES, 0, 0, axis_index_groups=groups, tiled=True)]
    ppermute x16 -> x14, starting transfers between devices: 24.2 us -> 20.2 us  [send(): return lax.ppermute(values, AXES, pairs)]
    all_to_all x2 -> x1, starting transfers between devices: 12 us -> 9.21 us  [pair_exchange(): lax.all_to_all(twice, AXES, 0, 0, axis_index_groups=groups, tiled=True)]
    slice x2 -> x0, local copies, waits for them, and re-layouts: 1.81 us -> none  [the longest x1 0.92 us: local(): piece[:32]]
    concatenate x1 -> x2, other arithmetic: 0.08 us -> 1.76 us  [the longest x1 1.01 us: local(): jnp.concatenate([send_z(piece, -1)[None], send(piece, lambda z, y, x, c:...]
  transfers between devices with their start and end apart: 18 -> 15, of which waited for: 11 -> 10; matrix products, arithmetic and copies ran while one was open for 4% -> 2% of each run, Pallas kernels for 5% -> 5%
where the time goes in v3:
time: 123 us; the launch traced here: 122 us
  starting transfers between devices  29.4 us (24%)
  waiting for transfers between devices  28.9 us (23%)
  blocking collectives  28.6 us (23%)
  Pallas kernels  26.3 us (21%)
  local copies, waits for them, and re-layouts  4.71 us (4%)
  other arithmetic  3.42 us (3%)
    ppermute x14, waiting for transfers between devices, send(): return lax.ppermute(values, AXES, pairs)  25 us
    ppermute x14, starting transfers between devices, send(): return lax.ppermute(values, AXES, pairs)  20.2 us
    pallas_call x1, Pallas kernels, coefficients(): pl.pallas_call(rest_kernel, out_shape=(jax.ShapeDtypeStruct((16, 8, 640),...  14.8 us
    all_to_all x1, blocking collectives, local(): return assemble(lax.all_to_all(tile, 'p', 0, 0, tiled=True))  14.7 us
    all_to_all x1, blocking collectives, local(): lax.all_to_all(right, ('h', 'p'), 0, 0, tiled=True).reshape(64, 1280)  13.9 us
    all_to_all x1, starting transfers between devices, pair_exchange(): lax.all_to_all(twice, AXES, 0, 0, axis_index_groups=groups, tiled=True)  9.21 us
    pallas_call x1, Pallas kernels, own_coefficients(): pl.pallas_call(own_kernel, out_shape=jax.ShapeDtypeStruct((2, 2, NG), F32...  5.2 us
    all_to_all x1, waiting for transfers between devices, pair_exchange(): lax.all_to_all(twice, AXES, 0, 0, axis_index_groups=groups, tiled=True)  3.88 us
  transfers between devices with their start and end apart: 15, of which 10 were waited for; matrix products, arithmetic and copies ran while one was open for 2% of the time, Pallas kernels for 5%

profile of v3, /device:TPU:1, one launch (start us, length us, event | category | flops | bytes accessed | tf_op | source)
XLA Modules:
  0.0 122.4 jit_solution(1052526058516435844)
XLA Ops:
  0.6 1.0 dynamic-slice_bitcast_fusion
  1.6 2.5 %collective-permute-start.2 = (bf16[48,2304]{1,0:T(8,128)(2,1)S(1)}, bf16[48,2304]{1,0:T(8,128)(2,1)S(1)}, u32[]{:S(2)}, u32[]{:S(2)}) collective-permute-start(bf16[48,2304]{1,0:T(8,128)(2,1)S(1)} %dynamic-slice_bitcast_fusion), channel_id=1, source_target_pairs={{0,64},{1,65},{4,68},{5,69},{8,72},{9,73},{12,76},{13,77},{16,80},... | collective-permute-start | bytes 663560 | tf_op jit(solution)/shard_map/ppermute | solution.py:336
  4.1 5.1 %collective-permute-start.1 = (bf16[48,2304]{1,0:T(8,128)(2,1)S(1)}, bf16[48,2304]{1,0:T(8,128)(2,1)S(1)}, u32[]{:S(2)}, u32[]{:S(2)}) collective-permute-start(bf16[48,2304]{1,0:T(8,128)(2,1)S(1)} %dynamic-slice_bitcast_fusion), channel_id=1, source_target_pairs={{0,128},{1,131},{4,132},{5,135},{8,136},{9,139},{12,140},{13,143},... | collective-permute-start | bytes 663560 | tf_op jit(solution)/shard_map/ppermute | solution.py:336
  9.3 0.7 collective-permute-start
  10.0 0.7 shift-right-arithmetic_multiply_fusion
  10.7 0.1 reshape.241
  10.8 0.1 mul.66
  11.0 0.1 div.52
  11.1 0.1 div.54
  11.3 0.1 div.58
  11.5 0.1 mul.68
  11.7 0.9 shard_map.113
  12.7 0.3 copy-done.1
  13.0 0.4 copy-done.2
  13.4 0.4 copy-done.3
  13.7 5.2 %shard_map.114.owned = f32[2,2,5120]{2,1,0:T(2,128)S(1)} custom-call(bf16[1,2,48,2304]{3,2,1,0:T(8,128)(2,1)S(1)} %copy-done, bf16[2,2,48,2304]{3,2,1,0:T(8,128)(2,1)S(1)} %copy-done.1, bf16[768,768]{1,0:T(8,128)(2,1)S(1)} %copy-done.3, bf16[768,768]{1,0:T(8,128)(2,1)S(1)} %copy-done.2, bf16[48,48]{1,0:T(8,128)(2,1)S(1)} %copy-done.6, ...), custom_call_target="tpu_custom_call" | custom-call | flops 5000000000 | bytes 30000000 | tf_op jit(solution)/shard_map/pallas_call | solution.py:245
  19.0 0.2 collective-permute-done
  19.2 1.0 pad_maximum_fusion.part
  20.2 0.3 collective-permute-start.3
  20.8 1.8 %collective-permute-done.3.other = bf16[3,48,2304]{2,1,0:T(8,128)(2,1)S(1)} collective-permute-done((bf16[3,48,2304]{2,1,0:T(8,128)(2,1)S(1)}, bf16[3,48,2304]{2,1,0:T(8,128)(2,1)S(1)}, u32[]{:S(2)}, u32[]{:S(2)}) %collective-permute-start.3) | collective-permute-done | bytes 663584 | tf_op jit(solution)/shard_map/ppermute | solution.py:336
  22.6 1.3 %copy-done.4 = bf16[768,768]{1,0:T(8,128)(2,1)S(1)} copy-done((bf16[768,768]{1,0:T(8,128)(2,1)S(1)}, bf16[768,768]{1,0:T(8,128)(2,1)}, u32[]{:S(2)}) %copy-start.4) | copy-done | bytes 1179672
  23.9 14.8 %shard_map.115 = (bf16[16,8,640]{2,1,0:T(8,128)(2,1)S(1)}, bf16[8,8,1280]{2,1,0:T(8,128)(2,1)S(1)}) custom-call(s32[1]{0:T(128)} %bitcast.core, bf16[3,48,2304]{2,1,0:T(8,128)(2,1)S(1)} %pad_maximum_fusion.part, bf16[3,48,2304]{2,1,0:T(8,128)(2,1)S(1)} %collective-permute-done.3.other, bf16[2,2,48,2304]{3,2,1,0:T(8,128)(2,1)S(1)} %copy-done.1, ...), custom_call_target="tpu_custom_call" | custom-call | flops 10000000000 | bytes 50000000 | tf_op jit(solution)/shard_map/pallas_call | solution.py:257
  38.6 13.9 %all_to_all.15 = bf16[8,8,1280]{2,1,0:T(8,128)(2,1)S(1)} all-to-all(bf16[8,8,1280]{2,1,0:T(8,128)(2,1)S(1)} %get-tuple-element.19), channel_id=1, replica_groups=mesh['p'=4,'y'=4,'x'=4,'h'=2,'c'=2] {'h','p'}, dimensions={0} | all-to-all | bytes 327680 | tf_op jit(solution)/shard_map/all_to_all | solution.py:428
  52.5 0.8 pad_maximum_fusion.1
  53.3 9.2 %all-to-all-start.1 = ((bf16[32,8,640]{2,1,0:T(8,128)(2,1)}), bf16[32,8,640]{2,1,0:T(8,128)(2,1)S(1)}, u32[]{:S(2)}, u32[]{:S(2)}) async-start(bf16[32,8,640]{2,1,0:T(8,128)(2,1)} %pad_maximum_fusion.1), calls=%async_computation.1 | async-start | bytes 655360 | tf_op jit(solution)/shard_map/all_to_all | solution.py:378
  62.7 0.1 tile.9
  62.8 0.1 reshape.232
  62.9 0.1 stack.35
  63.0 2.8 %collective-permute-start.9 = (bf16[64,1280]{1,0:T(8,128)(2,1)S(1)}, bf16[64,1280]{1,0:T(8,128)(2,1)S(1)}, u32[]{:S(2)}, u32[]{:S(2)}) collective-permute-start(bf16[64,1280]{1,0:T(8,128)(2,1)S(1)} %bitcast.24), channel_id=1, source_target_pairs={{0,8},{1,33},{4,12},{5,37},{8,0},{9,41},{12,4},{13,45},{16,24},{17... | collective-permute-start | bytes 491528 | tf_op jit(solution)/shard_map/ppermute | solution.py:336
  65.8 0.9 collective-permute-start.8
  66.6 0.6 collective-permute-start.7
  67.2 3.9 %all-to-all-done.1 = bf16[32,8,640]{2,1,0:T(8,128)(2,1)S(1)} async-done(((bf16[32,8,640]{2,1,0:T(8,128)(2,1)}), bf16[32,8,640]{2,1,0:T(8,128)(2,1)S(1)}, u32[]{:S(2)}, u32[]{:S(2)}) %all-to-all-start.1) | async-done | bytes 327712 | tf_op jit(solution)/shard_map/all_to_all | solution.py:378
  71.1 2.7 %collective-permute-done.7 = bf16[64,1280]{1,0:T(8,128)(2,1)S(1)} collective-permute-done((bf16[64,1280]{1,0:T(8,128)(2,1)S(1)}, bf16[64,1280]{1,0:T(8,128)(2,1)S(1)}, u32[]{:S(2)}, u32[]{:S(2)}) %collective-permute-start.7) | collective-permute-done | bytes 163872 | tf_op jit(solution)/shard_map/ppermute | solution.py:336
  73.9 3.4 %collective-permute-done.4.l1 = bf16[2,16,8,640]{3,2,1,0:T(8,128)(2,1)S(1)} collective-permute-done((bf16[2,16,8,640]{3,2,1,0:T(8,128)(2,1)S(1)}, bf16[2,16,8,640]{3,2,1,0:T(8,128)(2,1)S(1)}, u32[]{:S(2)}, u32[]{:S(2)}) %collective-permute-start.4) | collective-permute-done | bytes 327712 | tf_op jit(solution)/shard_map/ppermute | solution.py:336
  77.4 1.1 collective-permute-start.5
  78.5 1.3 %collective-permute-start.12 = (bf16[256,1280]{1,0:T(8,128)(2,1)S(1)}, bf16[256,1280]{1,0:T(8,128)(2,1)S(1)}, u32[]{:S(2)}, u32[]{:S(2)}) collective-permute-start(bf16[256,1280]{1,0:T(8,128)(2,1)S(1)} %constant_dynamic-update-slice_fusion.r0), channel_id=1, source_target_pairs={{0,32},{1,9},{4,36},{5,13},{8,40},{9,1},{12,44},{13,5},{16,48},{17... | collective-permute-start | bytes 1966088 | tf_op jit(solution)/shard_map/ppermute | solution.py:336
  79.8 1.5 %collective-permute-start.11 = (bf16[256,1280]{1,0:T(8,128)(2,1)S(1)}, bf16[256,1280]{1,0:T(8,128)(2,1)S(1)}, u32[]{:S(2)}, u32[]{:S(2)}) collective-permute-start(bf16[256,1280]{1,0:T(8,128)(2,1)S(1)} %constant_dynamic-update-slice_fusion.r0), channel_id=1, source_target_pairs={{0,48},{1,13},{4,52},{5,1},{8,56},{9,5},{12,60},{13,9},{16,0},{17,... | collective-permute-start | bytes 1966088 | tf_op jit(solution)/shard_map/ppermute | solution.py:336
  81.3 3.2 %collective-permute-done.5.l2 = bf16[2,16,8,640]{3,2,1,0:T(8,128)(2,1)S(1)} collective-permute-done((bf16[2,16,8,640]{3,2,1,0:T(8,128)(2,1)S(1)}, bf16[2,16,8,640]{3,2,1,0:T(8,128)(2,1)S(1)}, u32[]{:S(2)}, u32[]{:S(2)}) %collective-permute-start.5) | collective-permute-done | bytes 327712 | tf_op jit(solution)/shard_map/ppermute | solution.py:336
  84.5 0.6 iota_reduce_fusion
  85.1 4.7 %collective-permute-done.12.r3 = bf16[256,1280]{1,0:T(8,128)(2,1)S(1)} collective-permute-done((bf16[256,1280]{1,0:T(8,128)(2,1)S(1)}, bf16[256,1280]{1,0:T(8,128)(2,1)S(1)}, u32[]{:S(2)}, u32[]{:S(2)}) %collective-permute-start.12) | collective-permute-done | bytes 655392 | tf_op jit(solution)/shard_map/ppermute | solution.py:336
  89.8 5.6 %collective-permute-done.11.r2 = bf16[256,1280]{1,0:T(8,128)(2,1)S(1)} collective-permute-done((bf16[256,1280]{1,0:T(8,128)(2,1)S(1)}, bf16[256,1280]{1,0:T(8,128)(2,1)S(1)}, u32[]{:S(2)}, u32[]{:S(2)}) %collective-permute-start.11) | collective-permute-done | bytes 655392 | tf_op jit(solution)/shard_map/ppermute | solution.py:336
  95.4 1.4 %collective-permute-done.10.r1 = bf16[256,1280]{1,0:T(8,128)(2,1)S(1)} collective-permute-done((bf16[256,1280]{1,0:T(8,128)(2,1)S(1)}, bf16[256,1280]{1,0:T(8,128)(2,1)S(1)}, u32[]{:S(2)}, u32[]{:S(2)}) %collective-permute-start.10) | collective-permute-done | bytes 655392 | tf_op jit(solution)/shard_map/ppermute | solution.py:336
  96.8 3.4 %shard_map.116 = (f32[320,640]{1,0:T(8,128)S(1)}, f32[320,640]{1,0:T(8,128)S(1)}) custom-call(s32[1]{0:T(128)} %bitcast.core, s32[8]{0:T(128)S(1)} %get-tuple-element.13.place, s32[16]{0:T(128)S(1)} %broadcast_select_fusion.rows, bf16[2,16,8,640]{3,2,1,0:T(8,128)(2,1)S(1)} %bitcast.22, bf16[2,16,8,640]{3,2,1,0:T(8,128)(2,1)S(1)} %collective-permute-done.4.l1, ...), custom_call_target="tpu_custom_call" | custom-call | tf_op jit(solution)/shard_map/pallas_call | solution.py:310
  100.2 3.4 %collective-permute-start.13 = (f32[320,640]{1,0:T(8,128)S(1)}, f32[320,640]{1,0:T(8,128)S(1)}, u32[]{:S(2)}, u32[]{:S(2)}) collective-permute-start(f32[320,640]{1,0:T(8,128)S(1)} %get-tuple-element.23), channel_id=1, source_target_pairs={{0,1},{1,0},{4,5},{5,4},{8,9},{9,8},{12,13},{13,12},{16,17},{17,16... | collective-permute-start | bytes 2457608 | tf_op jit(solution)/shard_map/ppermute | solution.py:336
  103.6 2.0 %collective-permute-done.13 = f32[320,640]{1,0:T(8,128)S(1)} collective-permute-done((f32[320,640]{1,0:T(8,128)S(1)}, f32[320,640]{1,0:T(8,128)S(1)}, u32[]{:S(2)}, u32[]{:S(2)}) %collective-permute-start.13) | collective-permute-done | bytes 819232 | tf_op jit(solution)/shard_map/ppermute | solution.py:336
  105.6 0.1 add_convert_fusion
  105.7 14.7 %all_to_all.16.tile = bf16[4,80,640]{2,1,0:T(8,128)(2,1)} all-to-all(bf16[4,80,640]{2,1,0:T(8,128)(2,1)S(1)} %bitcast.23), channel_id=1, replica_groups=mesh['p'=4,'y'=4,'x'=4,'h'=2,'c'=2] {'p'}, dimensions={0} | all-to-all | bytes 819200 | tf_op jit(solution)/shard_map/all_to_all | solution.py:453
  120.4 2.0 %shard_map.117 = (f32[80,1280]{1,0:T(8,128)}, f32[80,1280]{1,0:T(8,128)}) custom-call(bf16[4,80,640]{2,1,0:T(8,128)(2,1)} %all_to_all.16.tile), custom_call_target="tpu_custom_call" | custom-call | tf_op jit(solution)/shard_map/pallas_call | solution.py:389
  (45 shorter events, 0.8 us)
Async XLA Ops:
  1.6 17.4 %collective-permute-start.2 = (bf16[48,2304]{1,0:T(8,128)(2,1)S(1)}, bf16[48,2304]{1,0:T(8,128)(2,1)S(1)}, u32[]{:S(2)}, u32[]{:S(2)}) collective-permute-start(bf16[48,2304]{1,0:T(8,128)(2,1)S(1)} %dynamic-slice_bitcast_fusion), channel_id=1, source_target_pairs={{0,64},{1,65},{4,68},{5,69},{8,72},{9,73},{12,76},{13,77},{16,80},... | collective-permute-start | bytes 663560 | tf_op jit(solution)/shard_map/ppermute | solution.py:336
  4.1 14.8 %collective-permute-start.1 = (bf16[48,2304]{1,0:T(8,128)(2,1)S(1)}, bf16[48,2304]{1,0:T(8,128)(2,1)S(1)}, u32[]{:S(2)}, u32[]{:S(2)}) collective-permute-start(bf16[48,2304]{1,0:T(8,128)(2,1)S(1)} %dynamic-slice_bitcast_fusion), channel_id=1, source_target_pairs={{0,128},{1,131},{4,132},{5,135},{8,136},{9,139},{12,140},{13,143},... | collective-permute-start | bytes 663560 | tf_op jit(solution)/shard_map/ppermute | solution.py:336
  9.3 9.9 %collective-permute-start = (bf16[48,2304]{1,0:T(8,128)(2,1)S(1)}, bf16[48,2304]{1,0:T(8,128)(2,1)}, u32[]{:S(2)}, u32[]{:S(2)}) collective-permute-start(bf16[48,2304]{1,0:T(8,128)(2,1)S(1)} %dynamic-slice_bitcast_fusion), channel_id=1, source_target_pairs={{0,194},{1,195},{4,198},{5,199},{8,202},{9,203},{12,206},{13,207},... | collective-permute-start | bytes 663560 | tf_op jit(solution)/shard_map/ppermute | solution.py:336
  11.6 1.1 copy-start.6
  11.7 1.0 copy-start
  11.7 1.3 %copy-start.1 = (bf16[2,2,48,2304]{3,2,1,0:T(8,128)(2,1)S(1)}, bf16[2,2,48,2304]{3,2,1,0:T(8,128)(2,1)}, u32[]{:S(2)}) copy-start(bf16[2,2,48,2304]{3,2,1,0:T(8,128)(2,1)} %cond.3) | copy-start | bytes 2654212
  11.7 1.7 %copy-start.2 = (bf16[768,768]{1,0:T(8,128)(2,1)S(1)}, bf16[768,768]{1,0:T(8,128)(2,1)}, u32[]{:S(2)}) copy-start(bf16[768,768]{1,0:T(8,128)(2,1)} %constant.137.clone.wy) | copy-start | bytes 3538948
  11.7 2.0 %copy-start.3 = (bf16[768,768]{1,0:T(8,128)(2,1)S(1)}, bf16[768,768]{1,0:T(8,128)(2,1)}, u32[]{:S(2)}) copy-start(bf16[768,768]{1,0:T(8,128)(2,1)} %constant.136.clone.wz) | copy-start | bytes 3538948
  11.7 2.0 %copy-start.5 = (bf16[48,48]{1,0:T(8,128)(2,1)S(1)}, bf16[48,48]{1,0:T(8,128)(2,1)}, u32[]{:S(2)}) copy-start(bf16[48,48]{1,0:T(8,128)(2,1)} %constant.139.clone.ts) | copy-start | bytes 13828
  18.9 1.6 %copy-start.9 = (f32[4]{0:T(128)S(1)}, f32[4]{0:T(128)}, u32[]{:S(2)}) copy-start(f32[4]{0:T(128)} %param.12) | copy-start | bytes 52
  18.9 1.7 %copy-start.8 = (f32[2]{0:T(128)S(1)}, f32[2]{0:T(128)}, u32[]{:S(2)}) copy-start(f32[2]{0:T(128)} %param.13) | copy-start | bytes 28
  20.2 2.4 %collective-permute-start.3 = (bf16[3,48,2304]{2,1,0:T(8,128)(2,1)S(1)}, bf16[3,48,2304]{2,1,0:T(8,128)(2,1)S(1)}, u32[]{:S(2)}, u32[]{:S(2)}) collective-permute-start(bf16[3,48,2304]{2,1,0:T(8,128)(2,1)S(1)} %pad_maximum_fusion.part), channel_id=1, source_target_pairs={{0,1},{1,0},{4,5},{5,4},{8,9},{9,8},{12,13},{13,12},{16,17},{17,16... | collective-permute-start | bytes 1990664 | tf_op jit(solution)/shard_map/ppermute | solution.py:336
  22.6 1.3 %copy-start.4 = (bf16[768,768]{1,0:T(8,128)(2,1)S(1)}, bf16[768,768]{1,0:T(8,128)(2,1)}, u32[]{:S(2)}) copy-start(bf16[768,768]{1,0:T(8,128)(2,1)} %constant.136.clone.wz) | copy-start | bytes 3538948
  38.6 24.0 %copy-start.7 = (s32[4]{0:T(128)S(1)}, s32[4]{0:T(128)}, u32[]{:S(2)}) copy-start(s32[4]{0:T(128)} %constant.140.clone) | copy-start | bytes 52
  53.3 17.8 %all-to-all-start.1 = ((bf16[32,8,640]{2,1,0:T(8,128)(2,1)}), bf16[32,8,640]{2,1,0:T(8,128)(2,1)S(1)}, u32[]{:S(2)}, u32[]{:S(2)}) async-start(bf16[32,8,640]{2,1,0:T(8,128)(2,1)} %pad_maximum_fusion.1), calls=%async_computation.1 | async-start | bytes 655360 | tf_op jit(solution)/shard_map/all_to_all | solution.py:378
  63.0 15.4 %collective-permute-start.9 = (bf16[64,1280]{1,0:T(8,128)(2,1)S(1)}, bf16[64,1280]{1,0:T(8,128)(2,1)S(1)}, u32[]{:S(2)}, u32[]{:S(2)}) collective-permute-start(bf16[64,1280]{1,0:T(8,128)(2,1)S(1)} %bitcast.24), channel_id=1, source_target_pairs={{0,8},{1,33},{4,12},{5,37},{8,0},{9,41},{12,4},{13,45},{16,24},{17... | collective-permute-start | bytes 491528 | tf_op jit(solution)/shard_map/ppermute | solution.py:336
  65.8 8.1 %collective-permute-start.8 = (bf16[64,1280]{1,0:T(8,128)(2,1)S(1)}, bf16[64,1280]{1,0:T(8,128)(2,1)S(1)}, u32[]{:S(2)}, u32[]{:S(2)}) collective-permute-start(bf16[64,1280]{1,0:T(8,128)(2,1)S(1)} %bitcast.25), channel_id=1, source_target_pairs={{0,12},{1,49},{4,0},{5,53},{8,4},{9,57},{12,8},{13,61},{16,28},{17... | collective-permute-start | bytes 491528 | tf_op jit(solution)/shard_map/ppermute | solution.py:336
  66.6 7.2 %collective-permute-start.7 = (bf16[64,1280]{1,0:T(8,128)(2,1)S(1)}, bf16[64,1280]{1,0:T(8,128)(2,1)S(1)}, u32[]{:S(2)}, u32[]{:S(2)}) collective-permute-start(bf16[64,1280]{1,0:T(8,128)(2,1)S(1)} %bitcast.26), channel_id=1, source_target_pairs={{0,4},{1,17},{4,8},{5,21},{8,12},{9,25},{12,0},{13,29},{16,20},{17... | collective-permute-start | bytes 491528 | tf_op jit(solution)/shard_map/ppermute | solution.py:336
  71.1 6.2 %collective-permute-start.4 = (bf16[2,16,8,640]{3,2,1,0:T(8,128)(2,1)S(1)}, bf16[2,16,8,640]{3,2,1,0:T(8,128)(2,1)S(1)}, u32[]{:S(2)}, u32[]{:S(2)}) collective-permute-start(bf16[2,16,8,640]{3,2,1,0:T(8,128)(2,1)S(1)} %bitcast.21), channel_id=1, source_target_pairs={{0,194},{1,65},{4,198},{5,69},{8,202},{9,73},{12,206},{13,77},{16,... | collective-permute-start | bytes 983048 | tf_op jit(solution)/shard_map/ppermute | solution.py:336
  77.4 7.1 %collective-permute-start.5 = (bf16[2,16,8,640]{3,2,1,0:T(8,128)(2,1)S(1)}, bf16[2,16,8,640]{3,2,1,0:T(8,128)(2,1)S(1)}, u32[]{:S(2)}, u32[]{:S(2)}) collective-permute-start(bf16[2,16,8,640]{3,2,1,0:T(8,128)(2,1)S(1)} %collective-permute-done.4.l1), channel_id=1, source_target_pairs={{0,64},{1,195},{4,68},{5,199},{8,72},{9,203},{12,76},{13,207},{16,... | collective-permute-start | bytes 983048 | tf_op jit(solution)/shard_map/ppermute | solution.py:336
  78.5 11.4 %collective-permute-start.12 = (bf16[256,1280]{1,0:T(8,128)(2,1)S(1)}, bf16[256,1280]{1,0:T(8,128)(2,1)S(1)}, u32[]{:S(2)}, u32[]{:S(2)}) collective-permute-start(bf16[256,1280]{1,0:T(8,128)(2,1)S(1)} %constant_dynamic-update-slice_fusion.r0), channel_id=1, source_target_pairs={{0,32},{1,9},{4,36},{5,13},{8,40},{9,1},{12,44},{13,5},{16,48},{17... | collective-permute-start | bytes 1966088 | tf_op jit(solution)/shard_map/ppermute | solution.py:336
  79.8 15.6 %collective-permute-start.11 = (bf16[256,1280]{1,0:T(8,128)(2,1)S(1)}, bf16[256,1280]{1,0:T(8,128)(2,1)S(1)}, u32[]{:S(2)}, u32[]{:S(2)}) collective-permute-start(bf16[256,1280]{1,0:T(8,128)(2,1)S(1)} %constant_dynamic-update-slice_fusion.r0), channel_id=1, source_target_pairs={{0,48},{1,13},{4,52},{5,1},{8,56},{9,5},{12,60},{13,9},{16,0},{17,... | collective-permute-start | bytes 1966088 | tf_op jit(solution)/shard_map/ppermute | solution.py:336
  81.3 15.5 %collective-permute-start.10 = (bf16[256,1280]{1,0:T(8,128)(2,1)S(1)}, bf16[256,1280]{1,0:T(8,128)(2,1)S(1)}, u32[]{:S(2)}, u32[]{:S(2)}) collective-permute-start(bf16[256,1280]{1,0:T(8,128)(2,1)S(1)} %constant_dynamic-update-slice_fusion.r0), channel_id=1, source_target_pairs={{0,16},{1,5},{4,20},{5,9},{8,24},{9,13},{12,28},{13,1},{16,32},{17... | collective-permute-start | bytes 1966088 | tf_op jit(solution)/shard_map/ppermute | solution.py:336
  84.5 12.3 %collective-permute-start.6 = (bf16[2,16,8,640]{3,2,1,0:T(8,128)(2,1)S(1)}, bf16[2,16,8,640]{3,2,1,0:T(8,128)(2,1)S(1)}, u32[]{:S(2)}, u32[]{:S(2)}) collective-permute-start(bf16[2,16,8,640]{3,2,1,0:T(8,128)(2,1)S(1)} %collective-permute-done.5.l2), channel_id=1, source_target_pairs={{0,194},{1,65},{4,198},{5,69},{8,202},{9,73},{12,206},{13,77},{16,... | collective-permute-start | bytes 983048 | tf_op jit(solution)/shard_map/ppermute | solution.py:336
  100.2 5.4 %collective-permute-start.13 = (f32[320,640]{1,0:T(8,128)S(1)}, f32[320,640]{1,0:T(8,128)S(1)}, u32[]{:S(2)}, u32[]{:S(2)}) collective-permute-start(f32[320,640]{1,0:T(8,128)S(1)} %get-tuple-element.23), channel_id=1, source_target_pairs={{0,1},{1,0},{4,5},{5,4},{8,9},{9,8},{12,13},{13,12},{16,17},{17,16... | collective-permute-start | bytes 2457608 | tf_op jit(solution)/shard_map/ppermute | solution.py:336

commit v4 on v3

--- a/solution.py
+++ b/solution.py
@@ -48,7 +48,7 @@
     for j, tab in enumerate((cs[:24], half)):
         wy[:, :, :, j] = np.einsum("ab,kmi->maibk", eye16, tab.reshape(24, 6, 8))
     wy = wy.reshape(768, 768)
-    return wz.astype(ml_dtypes.bfloat16), wy.astype(ml_dtypes.bfloat16), cos, sin
+    return np.stack([wz, wy]).astype(ml_dtypes.bfloat16), cos, sin
 
 
 def column_of(y, z):
@@ -56,8 +56,18 @@
     return (z >> 4) * 768 + jnp.where(y < 24, 0, 384) + (z & 15) * 24 + within
 
 
-def sort_kernel(key, keys, place, held):
-    bucket = key[...] >> 13
+def wave_keys(waves):
+    x = ((waves.astype(F32) + 0.5) * (1.0 / (N * N))).astype(jnp.int32)
+    rest = waves - x * (N * N)
+    y = ((rest.astype(F32) + 0.5) * (1.0 / N)).astype(jnp.int32)
+    key = (column_of(y, rest - y * N) << 6) | x
+    starts = [(2 * h + c) * 1280 + p * 320 for h in range(2) for p in range(4) for c in range(2)]
+    return jnp.concatenate([key[:, s : s + 320] for s in starts], axis=1)
+
+
+def sort_kernel(waves, keys, place, held):
+    key = wave_keys(waves[...])
+    bucket = key >> 13
     slots = lax.broadcasted_iota(jnp.int32, (BUCKETS, 128), 0)
     before = jnp.zeros((BUCKETS, 128), F32)
     for k in range(40):
@@ -78,14 +88,14 @@
     high = place[...] >> 7
     low = place[...] & 127
     at = lax.broadcasted_iota(jnp.int32, (40, NG), 0) == high
-    parts = (bucket, (key[...] >> 6) & 127, key[...] & 63)
+    parts = (bucket, (key >> 6) & 127, key & 63)
     rows = jnp.concatenate([jnp.where(at, v.astype(F32), 0.0) for v in parts], axis=0).astype(BF16)
     cols = jnp.where(lax.broadcasted_iota(jnp.int32, (128, NG), 0) == low, 1.0, 0.0).astype(BF16)
     moved = lax.dot_general(rows, cols, (((1,), (1,)), ((), ())), preferred_element_type=F32).astype(jnp.int32)
     keys[...] = (moved[0:40] << 13) | (moved[40:80] << 6) | moved[80:120]
 
 
-def sort_waves(key):
+def sort_waves(waves):
     return pl.pallas_call(
         sort_kernel,
         out_shape=(jax.ShapeDtypeStruct((40, 128), jnp.int32), jax.ShapeDtypeStruct((1, NG), jnp.int32)),
@@ -94,7 +104,7 @@
         scratch_shapes=[pltpu.VMEM((40, BUCKETS, 128), F32)],
         compiler_params=pltpu.CompilerParams(vmem_limit_bytes=20 * 2**20),
         cost_estimate=pl.CostEstimate(flops=10**9, bytes_accessed=10**6, transcendentals=0),
-    )(key)
+    )(waves)
 
 
 def densities(val, cond, cols, xs, k):
@@ -108,11 +118,11 @@
             xs[k, rows, 384:768] = (vr * ci - vi * cr).astype(BF16)
 
 
-def sections(val, cond, wz, wy, xs, zs, s):
+def sections(val, cond, wide, xs, zs, s):
     count = zs.shape[1] // 2
     for i in range(6):
         densities(val, cond, slice(i * 384, (i + 1) * 384), xs, i % 2)
-        out = jnp.dot(xs[i % 2], wz[...], preferred_element_type=F32).astype(BF16)
+        out = jnp.dot(xs[i % 2], wide[0], preferred_element_type=F32).astype(BF16)
         for t in range(3):
             for f in range(2):
                 zs[t, f * count : (f + 1) * count, i * 128 : (i + 1) * 128] = out[
@@ -120,8 +130,8 @@
                 ]
     edge = lax.broadcasted_iota(jnp.int32, (1, 384), 1) % 24 == 0
     for t in range(3):
-        cp = jnp.dot(zs[t], wy[:, :384], preferred_element_type=F32)
-        sp = jnp.dot(zs[t], wy[:, 384:], preferred_element_type=F32)
+        cp = jnp.dot(zs[t], wide[1, :, :384], preferred_element_type=F32)
+        sp = jnp.dot(zs[t], wide[1, :, 384:], preferred_element_type=F32)
         cre, cim, sre, sim = cp[:count], cp[count:], sp[:count], sp[count:]
         outs = (
             (jnp.where(edge, cre, cre + sim), jnp.where(edge, sre, cre - sim)),
@@ -179,15 +189,15 @@
     lax.fori_loop(0, 20 // GROUP, step, 0)
 
 
-def own_kernel(val, cond, wz, wy, tc, ts, starts, key, m, xs, zs, s):
+def own_kernel(val, cond, wide, tc, ts, starts, key, m, xs, zs, s):
     def band(cols):
         return val[0, 0, :, cols].astype(F32), val[0, 1, :, cols].astype(F32)
 
-    sections([band], cond, wz, wy, xs, zs, s)
+    sections([band], cond, wide, xs, zs, s)
     select(s, tc, ts, starts, key, m, 0)
 
 
-def rest_kernel(core, part, other, cond, wz, wy, tc, ts, starts, key, back, w, owned, left, right, xs, zs, s, m, mo):
+def rest_kernel(core, part, other, cond, wide, tc, ts, starts, key, back, w, owned, left, right, xs, zs, s, m, mo):
     first = core[0] == 0
 
     def band(v):
@@ -198,7 +208,7 @@
 
         return read
 
-    sections([band(v) for v in range(3)], cond, wz, wy, xs, zs, s)
+    sections([band(v) for v in range(3)], cond, wide, xs, zs, s)
     select(s, tc, ts, starts, key, m, 2)
     m[:, 0:2, :] = owned[...]
 
@@ -229,7 +239,9 @@
             for b in range(4):
                 lane = ((b // 2 * 4 + r // 4) * 2 + b % 2) * 320 + 80 * (r % 4)
                 parts.append(mo[f, :, lane : lane + 80])
-        left[r] = (weight * jnp.concatenate(parts, axis=1)).astype(BF16)
+        block = (weight * jnp.concatenate(parts, axis=1)).astype(BF16)
+        left[r] = block
+        left[16 + r] = block
 
 
 def scratch(pairs):
@@ -245,10 +257,10 @@
     return pl.pallas_call(
         own_kernel,
         out_shape=jax.ShapeDtypeStruct((2, 2, NG), F32),
-        in_specs=[VM] * 6 + [SM, VM],
+        in_specs=[VM] * 5 + [SM, VM],
         out_specs=VM,
         scratch_shapes=scratch(2),
-        compiler_params=pltpu.CompilerParams(vmem_limit_bytes=40 * 2**20),
+        compiler_params=pltpu.CompilerParams(vmem_limit_bytes=16 * 2**20),
         cost_estimate=pl.CostEstimate(flops=5 * 10**9, bytes_accessed=3 * 10**7, transcendentals=0),
     )(val, cond, *wide, key, key)
 
@@ -257,68 +269,83 @@
     return pl.pallas_call(
         rest_kernel,
         out_shape=(
-            jax.ShapeDtypeStruct((16, 8, 640), BF16),
+            jax.ShapeDtypeStruct((32, 8, 640), BF16),
             jax.ShapeDtypeStruct((8, 8, 1280), BF16),
         ),
-        in_specs=[SM] + [VM] * 7 + [SM] + [VM] * 4,
+        in_specs=[SM] + [VM] * 6 + [SM] + [VM] * 4,
         out_specs=(VM, VM),
         scratch_shapes=scratch(6) + [pltpu.VMEM((2, 8, NG), F32)] * 2,
-        compiler_params=pltpu.CompilerParams(vmem_limit_bytes=40 * 2**20),
+        compiler_params=pltpu.CompilerParams(vmem_limit_bytes=24 * 2**20),
         cost_estimate=pl.CostEstimate(flops=10**10, bytes_accessed=5 * 10**7, transcendentals=0),
     )(core, part, other, cond, *wide, key, key, back, w, owned)
 
 
-def chi_kernel(core, place, rows, l0, l1, l2, l3, r0, r1, r2, r3, mine, theirs, lall, lk, rk):
+def left_kernel(place, rows, l0, l1, l2, l3, turned, held, lk):
     for i, piece in enumerate((l0, l1, l2, l3)):
-        lall[2 * i : 2 * i + 2] = piece[...]
-    base = 0
-    for piece in (r0, r1, r2, r3):
-        size = piece.shape[0]
-        rk[base : base + size] = piece[...]
-        base += size
+        held[2 * i : 2 * i + 2] = piece[...]
 
     def fill(k, _):
         r = rows[k]
         for u in range(4):
-            pair = [lall[place[2 * u + e], r].astype(F32) for e in range(2)]
+            pair = [held[place[2 * u + e], r].astype(F32) for e in range(2)]
             lk[pl.ds(pl.multiple_of(k * 64 + u * 16, 16), 16), :] = jnp.concatenate(pair, axis=0).astype(BF16)
         return 0
 
     lax.fori_loop(0, 16, fill, 0)
+    turned[...] = lk[...].T
+
+
+def left_matrix(place, rows, lefts):
+    return pl.pallas_call(
+        left_kernel,
+        out_shape=jax.ShapeDtypeStruct((640, 1024), BF16),
+        in_specs=[SM] * 2 + [VM] * 4,
+        out_specs=VM,
+        scratch_shapes=[pltpu.VMEM((8, 16, 8, 640), BF16), pltpu.VMEM((1024, 640), BF16)],
+        compiler_params=pltpu.CompilerParams(vmem_limit_bytes=12 * 2**20),
+    )(place, rows, *lefts)
+
+
+def products(left, right):
+    both = jnp.dot(left, right, preferred_element_type=F32)
+    re, im = both[:320], both[320:]
+    return re[:, :640] + im[:, 640:], im[:, :640] - re[:, 640:]
+
+
+def early_kernel(left, r0, r1, r2, acc, rk):
+    for i, piece in enumerate((r0, r1, r2)):
+        rk[i * 256 : (i + 1) * 256] = piece[...]
+    acc[0], acc[1] = products(left[:, :768], rk[...])
+
+
+def late_kernel(core, left, r3, acc, mine, theirs):
     first = core[0] == 0
-    half = 320
-
-    def product(f):
-        return lax.dot_general(
-            lk[:, f * half : (f + 1) * half], rk[...], (((0,), (0,)), ((), ())), preferred_element_type=F32
-        )
-
-    re = product(0)
-    im = product(1)
-    chi_re = re[:, :640] + im[:, 640:]
-    chi_im = im[:, :640] - re[:, 640:]
-    for k, chi in enumerate((chi_re, chi_im)):
-        a, b = chi[:, :half], chi[:, half:]
-        cols = slice(k * half, (k + 1) * half)
+    chis = products(left[:, 768:], r3[...])
+    for k in range(2):
+        chi = acc[k] + chis[k]
+        a, b = chi[:, :320], chi[:, 320:]
+        cols = slice(k * 320, (k + 1) * 320)
         mine[:, cols] = jnp.where(first, a, b)
-        theirs[:, cols] = jnp.where(first, b, a)
+        theirs[:, cols] = jnp.where(first, b, a).astype(BF16)
 
 
 def chi_tiles(core, place, rows, lefts, rights):
-    vm = pl.BlockSpec(memory_space=pltpu.VMEM)
-    sm = pl.BlockSpec(memory_space=pltpu.SMEM)
-    return pl.pallas_call(
-        chi_kernel,
-        out_shape=(jax.ShapeDtypeStruct((320, 640), F32),) * 2,
-        in_specs=[sm] * 3 + [vm] * 8,
-        out_specs=(vm, vm),
-        scratch_shapes=[
-            pltpu.VMEM((8, 16, 8, 640), BF16),
-            pltpu.VMEM((1024, 640), BF16),
-            pltpu.VMEM((1024, 1280), BF16),
-        ],
-        compiler_params=pltpu.CompilerParams(vmem_limit_bytes=48 * 2**20),
-    )(core, place, rows, *lefts, *rights)
+    left = left_matrix(place, rows, lefts)
+    acc = pl.pallas_call(
+        early_kernel,
+        out_shape=jax.ShapeDtypeStruct((2, 320, 640), F32),
+        in_specs=[VM] * 4,
+        out_specs=VM,
+        scratch_shapes=[pltpu.VMEM((768, 1280), BF16)],
+        compiler_params=pltpu.CompilerParams(vmem_limit_bytes=20 * 2**20),
+    )(left, *rights[:3])
+    return pl.pallas_call(
+        late_kernel,
+        out_shape=(jax.ShapeDtypeStruct((320, 640), F32), jax.ShapeDtypeStruct((320, 640), BF16)),
+        in_specs=[SM] + [VM] * 3,
+        out_specs=(VM, VM),
+        compiler_params=pltpu.CompilerParams(vmem_limit_bytes=20 * 2**20),
+    )(core, left, rights[3], acc)
 
 
 def device(z, y, x, c):
@@ -374,8 +401,7 @@
         for k in range(4):
             zs = [(2 * k + e + c) % 8 for e in range(2)]
             groups.append([device(z, y, x, c) for z in zs for y in range(4) for x in range(4)])
-    twice = jnp.concatenate([left, left])
-    got = lax.all_to_all(twice, AXES, 0, 0, axis_index_groups=groups, tiled=True)
+    got = lax.all_to_all(left, AXES, 0, 0, axis_index_groups=groups, tiled=True)
     return got.reshape(2, 16, 8, 640)
 
 
@@ -408,10 +434,7 @@
         ]
     )
 
-    order = g_index.reshape(2, 2, 4, 320).transpose(0, 2, 1, 3).reshape(NG)
-    plane_part = lax.rem(order, N * N)
-    key = (column_of(lax.div(plane_part, N), lax.rem(plane_part, N)) << 6) | lax.div(order, N * N)
-    key, back = sort_waves(key.reshape(1, NG))
+    key, back = sort_waves(g_index.reshape(1, NG))
 
     energies = lax.dynamic_slice(jnp.tile(valence_energy, 2), (p,), (NV,))
     scale = math.sqrt(NV * 512)
@@ -440,8 +463,8 @@
     held = (held + c) % 8
     place = jnp.argmax(held[None, :] == jnp.arange(8)[:, None], axis=1).astype(jnp.int32)
 
-    moves = (lambda i: i + 1, lambda i: i - 1, lambda i: i + 2)
-    offsets = jnp.array([0, 3, 1, 2])
+    moves = (lambda i: i + 2, lambda i: i - 1, lambda i: i + 1)
+    offsets = jnp.array([0, 2, 1, 3])
     four = jnp.concatenate([right] + [send(right, plane(0, move)) for move in moves])
     rights = [four] + [send(four, plane(1, move)) for move in moves]
     aa = jnp.tile((jnp.where(c == 0, x, y) + offsets) % 4, 4)
@@ -449,7 +472,7 @@
     rows = jnp.where(c == 0, bb * 4 + aa, aa * 4 + bb).astype(jnp.int32)
 
     mine, theirs = chi_tiles(core, place, rows, (left0, left1, left2, left3), rights)
-    tile = (mine + send_core(theirs)).astype(BF16).reshape(4, 80, 640)
+    tile = (mine + send_core(theirs).astype(F32)).astype(BF16).reshape(4, 80, 640)
     return assemble(lax.all_to_all(tile, "p", 0, 0, tiled=True))
 
 

time: 123 us -> 120 us (0.976)
  other arithmetic: 3.42 us -> 0.91 us
  starting transfers between devices: 29.4 us -> 27.9 us
  Pallas kernels: 26.3 us -> 27.6 us
    ppermute x14, starting transfers between devices: 20.2 us -> 18.7 us  [send(): return lax.ppermute(values, AXES, pairs)]
    pallas_call x2 -> x4, Pallas kernels: 18.1 us -> 19.4 us  [the longest x1 15.5 us: coefficients(): pl.pallas_call(rest_kernel, out_shape=(jax.ShapeDtypeStruct((32, 8, 640),...]
  transfers between devices with their start and end apart: 15 -> 15, of which waited for: 10 -> 9; matrix products, arithmetic and copies ran while one was open for 2% -> 1% of each run, Pallas kernels for 5% -> 8%
where the time goes in v4:
time: 120 us
  blocking collectives  28.8 us (24%)
  waiting for transfers between devices  28.6 us (24%)
  starting transfers between devices  27.9 us (23%)
  Pallas kernels  27.6 us (23%)
  local copies, waits for them, and re-layouts  5.01 us (4%)
    ppermute x14, waiting for transfers between devices, send(): return lax.ppermute(values, AXES, pairs)  24.2 us
    ppermute x14, starting transfers between devices, send(): return lax.ppermute(values, AXES, pairs)  18.7 us
    pallas_call x1, Pallas kernels, coefficients(): pl.pallas_call(rest_kernel, out_shape=(jax.ShapeDtypeStruct((32, 8, 640),...  15.5 us
    all_to_all x1, blocking collectives, local(): return assemble(lax.all_to_all(tile, 'p', 0, 0, tiled=True))  14.7 us
    all_to_all x1, blocking collectives, local(): lax.all_to_all(right, ('h', 'p'), 0, 0, tiled=True).reshape(64, 1280)  14 us
    all_to_all x1, starting transfers between devices, pair_exchange(): got = lax.all_to_all(left, AXES, 0, 0, axis_index_groups=groups, tiled=True)  9.2 us
    pallas_call x1, Pallas kernels, own_coefficients(): pl.pallas_call(own_kernel, out_shape=jax.ShapeDtypeStruct((2, 2, NG), F32...  5.17 us
    all_to_all x1, waiting for transfers between devices, pair_exchange(): got = lax.all_to_all(left, AXES, 0, 0, axis_index_groups=groups, tiled=True)  4.43 us
  transfers between devices with their start and end apart: 15, of which 9 were waited for; matrix products, arithmetic and copies ran while one was open for 1% of the time, Pallas kernels for 8%

profile of v4, /device:TPU:1, one launch (start us, length us, event | category | flops | bytes accessed | tf_op | source)
XLA Modules:
  0.0 119.7 jit_solution(1279669918664675068)
XLA Ops:
  0.6 0.0 copy-start.6
  0.6 1.0 dynamic-slice_bitcast_fusion
  1.6 2.5 %collective-permute-start.2 = (bf16[48,2304]{1,0:T(8,128)(2,1)S(1)}, bf16[48,2304]{1,0:T(8,128)(2,1)S(1)}, u32[]{:S(2)}, u32[]{:S(2)}) collective-permute-start(bf16[48,2304]{1,0:T(8,128)(2,1)S(1)} %dynamic-slice_bitcast_fusion), channel_id=1, source_target_pairs={{0,64},{1,65},{4,68},{5,69},{8,72},{9,73},{12,76},{13,77},{16,80},... | collective-permute-start | bytes 663560 | tf_op jit(solution)/shard_map/ppermute | solution.py:363
  4.2 5.1 %collective-permute-start.1 = (bf16[48,2304]{1,0:T(8,128)(2,1)S(1)}, bf16[48,2304]{1,0:T(8,128)(2,1)S(1)}, u32[]{:S(2)}, u32[]{:S(2)}) collective-permute-start(bf16[48,2304]{1,0:T(8,128)(2,1)S(1)} %dynamic-slice_bitcast_fusion), channel_id=1, source_target_pairs={{0,128},{1,131},{4,132},{5,135},{8,136},{9,139},{12,140},{13,143},... | collective-permute-start | bytes 663560 | tf_op jit(solution)/shard_map/ppermute | solution.py:363
  9.3 0.7 collective-permute-start
  10.0 0.7 copy-done.2
  10.7 1.0 shard_map.104
  11.8 0.2 copy-done.1
  12.0 0.8 copy-done.3
  12.8 5.2 %shard_map.105.owned = f32[2,2,5120]{2,1,0:T(2,128)S(1)} custom-call(bf16[1,2,48,2304]{3,2,1,0:T(8,128)(2,1)S(1)} %copy-done, bf16[2,2,48,2304]{3,2,1,0:T(8,128)(2,1)S(1)} %copy-done.1, bf16[2,768,768]{2,1,0:T(8,128)(2,1)S(1)} %copy-done.3, bf16[48,48]{1,0:T(8,128)(2,1)S(1)} %copy-done.6, bf16[48,48]{1,0:T(8,128)(2,1)S(1)} %copy-done.5, ...), custom_call_target="tpu_custom_call" | custom-call | flops 5000000000 | bytes 30000000 | tf_op jit(solution)/shard_map/pallas_call | solution.py:257
  18.0 1.2 %collective-permute-done = bf16[48,2304]{1,0:T(8,128)(2,1)S(1)} collective-permute-done((bf16[48,2304]{1,0:T(8,128)(2,1)S(1)}, bf16[48,2304]{1,0:T(8,128)(2,1)S(1)}, u32[]{:S(2)}, u32[]{:S(2)}) %collective-permute-start) | collective-permute-done | bytes 221216 | tf_op jit(solution)/shard_map/ppermute | solution.py:363
  19.2 0.1 pad_maximum_fusion.part
  19.3 0.3 collective-permute-start.3
  19.6 0.1 tile.21
  19.7 0.1 dynamic_slice.8
  19.8 0.1 multiply_divide_fusion
  19.8 0.1 div.15.w
  19.9 1.8 %collective-permute-done.3.other = bf16[3,48,2304]{2,1,0:T(8,128)(2,1)S(1)} collective-permute-done((bf16[3,48,2304]{2,1,0:T(8,128)(2,1)S(1)}, bf16[3,48,2304]{2,1,0:T(8,128)(2,1)S(1)}, u32[]{:S(2)}, u32[]{:S(2)}) %collective-permute-start.3) | collective-permute-done | bytes 663584 | tf_op jit(solution)/shard_map/ppermute | solution.py:363
  21.7 1.7 %copy-done.4 = bf16[2,768,768]{2,1,0:T(8,128)(2,1)S(1)} copy-done((bf16[2,768,768]{2,1,0:T(8,128)(2,1)S(1)}, bf16[2,768,768]{2,1,0:T(8,128)(2,1)}, u32[]{:S(2)}) %copy-start.4) | copy-done | bytes 2359320
  23.3 15.5 %shard_map.106 = (bf16[32,8,640]{2,1,0:T(8,128)(2,1)}, bf16[8,8,1280]{2,1,0:T(8,128)(2,1)S(1)}) custom-call(s32[1]{0:T(128)} %bitcast.core, bf16[3,48,2304]{2,1,0:T(8,128)(2,1)S(1)} %pad_maximum_fusion.part, bf16[3,48,2304]{2,1,0:T(8,128)(2,1)S(1)} %collective-permute-done.3.other, bf16[2,2,48,2304]{3,2,1,0:T(8,128)(2,1)S(1)} %copy-done.1, ...), custom_call_target="tpu_custom_call" | custom-call | flops 10000000000 | bytes 50000000 | tf_op jit(solution)/shard_map/pallas_call | solution.py:269
  38.8 14.0 %all_to_all.15 = bf16[8,8,1280]{2,1,0:T(8,128)(2,1)S(1)} all-to-all(bf16[8,8,1280]{2,1,0:T(8,128)(2,1)S(1)} %get-tuple-element.19), channel_id=1, replica_groups=mesh['p'=4,'y'=4,'x'=4,'h'=2,'c'=2] {'h','p'}, dimensions={0} | all-to-all | bytes 327680 | tf_op jit(solution)/shard_map/all_to_all | solution.py:451
  52.9 9.2 %all-to-all-start.1 = ((bf16[32,8,640]{2,1,0:T(8,128)(2,1)}), bf16[32,8,640]{2,1,0:T(8,128)(2,1)S(1)}, u32[]{:S(2)}, u32[]{:S(2)}) async-start(bf16[32,8,640]{2,1,0:T(8,128)(2,1)} %get-tuple-element.20), calls=%async_computation.1 | async-start | bytes 655360 | tf_op jit(solution)/shard_map/all_to_all | solution.py:404
  62.2 0.1 tile.9
  62.3 0.1 broadcast_in_dim.16
  62.4 0.1 reshape.138
  62.5 0.1 stack.35
  62.6 1.2 %collective-permute-start.9 = (bf16[64,1280]{1,0:T(8,128)(2,1)S(1)}, bf16[64,1280]{1,0:T(8,128)(2,1)S(1)}, u32[]{:S(2)}, u32[]{:S(2)}) collective-permute-start(bf16[64,1280]{1,0:T(8,128)(2,1)S(1)} %bitcast.22), channel_id=1, source_target_pairs={{0,4},{1,17},{4,8},{5,21},{8,12},{9,25},{12,0},{13,29},{16,20},{17... | collective-permute-start | bytes 491528 | tf_op jit(solution)/shard_map/ppermute | solution.py:363
  63.8 1.5 %collective-permute-start.8 = (bf16[64,1280]{1,0:T(8,128)(2,1)S(1)}, bf16[64,1280]{1,0:T(8,128)(2,1)S(1)}, u32[]{:S(2)}, u32[]{:S(2)}) collective-permute-start(bf16[64,1280]{1,0:T(8,128)(2,1)S(1)} %bitcast.23), channel_id=1, source_target_pairs={{0,12},{1,49},{4,0},{5,53},{8,4},{9,57},{12,8},{13,61},{16,28},{17... | collective-permute-start | bytes 491528 | tf_op jit(solution)/shard_map/ppermute | solution.py:363
  65.3 1.5 %collective-permute-start.7 = (bf16[64,1280]{1,0:T(8,128)(2,1)S(1)}, bf16[64,1280]{1,0:T(8,128)(2,1)S(1)}, u32[]{:S(2)}, u32[]{:S(2)}) collective-permute-start(bf16[64,1280]{1,0:T(8,128)(2,1)S(1)} %bitcast.24), channel_id=1, source_target_pairs={{0,8},{1,33},{4,12},{5,37},{8,0},{9,41},{12,4},{13,45},{16,24},{17... | collective-permute-start | bytes 491528 | tf_op jit(solution)/shard_map/ppermute | solution.py:363
  66.8 4.4 %all-to-all-done.1 = bf16[32,8,640]{2,1,0:T(8,128)(2,1)S(1)} async-done(((bf16[32,8,640]{2,1,0:T(8,128)(2,1)}), bf16[32,8,640]{2,1,0:T(8,128)(2,1)S(1)}, u32[]{:S(2)}, u32[]{:S(2)}) %all-to-all-start.1) | async-done | bytes 327712 | tf_op jit(solution)/shard_map/all_to_all | solution.py:404
  71.2 2.3 %collective-permute-done.7 = bf16[64,1280]{1,0:T(8,128)(2,1)S(1)} collective-permute-done((bf16[64,1280]{1,0:T(8,128)(2,1)S(1)}, bf16[64,1280]{1,0:T(8,128)(2,1)S(1)}, u32[]{:S(2)}, u32[]{:S(2)}) %collective-permute-start.7) | collective-permute-done | bytes 163872 | tf_op jit(solution)/shard_map/ppermute | solution.py:363
  73.6 3.9 %collective-permute-done.4.l1 = bf16[2,16,8,640]{3,2,1,0:T(8,128)(2,1)S(1)} collective-permute-done((bf16[2,16,8,640]{3,2,1,0:T(8,128)(2,1)S(1)}, bf16[2,16,8,640]{3,2,1,0:T(8,128)(2,1)S(1)}, u32[]{:S(2)}, u32[]{:S(2)}) %collective-permute-start.4) | collective-permute-done | bytes 327712 | tf_op jit(solution)/shard_map/ppermute | solution.py:363
  77.4 0.5 collective-permute-start.5
  77.9 1.1 collective-permute-start.12
  79.1 0.8 collective-permute-start.11
  79.9 0.2 collective-permute-start.10
  80.1 4.5 %collective-permute-done.5.l2 = bf16[2,16,8,640]{3,2,1,0:T(8,128)(2,1)S(1)} collective-permute-done((bf16[2,16,8,640]{3,2,1,0:T(8,128)(2,1)S(1)}, bf16[2,16,8,640]{3,2,1,0:T(8,128)(2,1)S(1)}, u32[]{:S(2)}, u32[]{:S(2)}) %collective-permute-start.5) | collective-permute-done | bytes 327712 | tf_op jit(solution)/shard_map/ppermute | solution.py:363
  84.6 0.6 iota_reduce_fusion
  85.2 5.6 %collective-permute-done.6.l3 = bf16[2,16,8,640]{3,2,1,0:T(8,128)(2,1)S(1)} collective-permute-done((bf16[2,16,8,640]{3,2,1,0:T(8,128)(2,1)S(1)}, bf16[2,16,8,640]{3,2,1,0:T(8,128)(2,1)S(1)}, u32[]{:S(2)}, u32[]{:S(2)}) %collective-permute-start.6) | collective-permute-done | bytes 327712 | tf_op jit(solution)/shard_map/ppermute | solution.py:363
  90.8 1.4 %shard_map.107.left = bf16[640,1024]{1,0:T(8,128)(2,1)S(1)} custom-call(s32[8]{0:T(128)S(1)} %get-tuple-element.13.place, s32[16]{0:T(128)S(1)} %broadcast_select_fusion.rows, bf16[2,16,8,640]{3,2,1,0:T(8,128)(2,1)S(1)} %bitcast.19, bf16[2,16,8,640]{3,2,1,0:T(8,128)(2,1)S(1)} %collective-permute-done.4.l1, ...), custom_call_target="tpu_custom_call" | custom-call | tf_op jit(solution)/shard_map/pallas_call | solution.py:299
  92.2 1.4 %shard_map.108.acc = f32[2,320,640]{2,1,0:T(8,128)S(1)} custom-call(bf16[640,1024]{1,0:T(8,128)(2,1)S(1)} %shard_map.107.left, bf16[256,1280]{1,0:T(8,128)(2,1)S(1)} %constant_dynamic-update-slice_fusion.r0, bf16[256,1280]{1,0:T(8,128)(2,1)S(1)} %collective-permute-done.11.r1, bf16[256,1280]{1,0:T(8,128)(2,1)S(1)} %collective-permute-done.12.r2), custom_call_target="tpu_custom_call" | custom-call | tf_op jit(solution)/shard_map/pallas_call | solution.py:334
  93.7 3.7 %collective-permute-done.10.r3 = bf16[256,1280]{1,0:T(8,128)(2,1)S(1)} collective-permute-done((bf16[256,1280]{1,0:T(8,128)(2,1)S(1)}, bf16[256,1280]{1,0:T(8,128)(2,1)S(1)}, u32[]{:S(2)}, u32[]{:S(2)}) %collective-permute-start.10) | collective-permute-done | bytes 655392 | tf_op jit(solution)/shard_map/ppermute | solution.py:363
  97.3 1.1 shard_map.109
  98.4 3.1 %collective-permute-start.13 = (bf16[320,640]{1,0:T(8,128)(2,1)S(1)}, bf16[320,640]{1,0:T(8,128)(2,1)S(1)}, u32[]{:S(2)}, u32[]{:S(2)}) collective-permute-start(bf16[320,640]{1,0:T(8,128)(2,1)S(1)} %get-tuple-element.23), channel_id=1, source_target_pairs={{0,1},{1,0},{4,5},{5,4},{8,9},{9,8},{12,13},{13,12},{16,17},{17,16... | collective-permute-start | bytes 1228808 | tf_op jit(solution)/shard_map/ppermute | solution.py:363
  101.5 1.4 %collective-permute-done.13 = bf16[320,640]{1,0:T(8,128)(2,1)S(1)} collective-permute-done((bf16[320,640]{1,0:T(8,128)(2,1)S(1)}, bf16[320,640]{1,0:T(8,128)(2,1)S(1)}, u32[]{:S(2)}, u32[]{:S(2)}) %collective-permute-start.13) | collective-permute-done | bytes 409632 | tf_op jit(solution)/shard_map/ppermute | solution.py:363
  102.9 0.1 add_convert_fusion
  103.0 14.7 %all_to_all.16.tile = bf16[4,80,640]{2,1,0:T(8,128)(2,1)} all-to-all(bf16[4,80,640]{2,1,0:T(8,128)(2,1)S(1)} %bitcast.21), channel_id=1, replica_groups=mesh['p'=4,'y'=4,'x'=4,'h'=2,'c'=2] {'p'}, dimensions={0} | all-to-all | bytes 819200 | tf_op jit(solution)/shard_map/all_to_all | solution.py:476
  117.7 2.0 %shard_map.110 = (f32[80,1280]{1,0:T(8,128)}, f32[80,1280]{1,0:T(8,128)}) custom-call(bf16[4,80,640]{2,1,0:T(8,128)(2,1)} %all_to_all.16.tile), custom_call_target="tpu_custom_call" | custom-call | tf_op jit(solution)/shard_map/pallas_call | solution.py:415
  (32 shorter events, 0.1 us)
Async XLA Ops:
  0.6 11.1 %copy-start.6 = (bf16[48,48]{1,0:T(8,128)(2,1)S(1)}, bf16[48,48]{1,0:T(8,128)(2,1)}, u32[]{:S(2)}) copy-start(bf16[48,48]{1,0:T(8,128)(2,1)} %constant.121.clone.tc) | copy-start | bytes 13828
  1.6 16.4 %collective-permute-start.2 = (bf16[48,2304]{1,0:T(8,128)(2,1)S(1)}, bf16[48,2304]{1,0:T(8,128)(2,1)S(1)}, u32[]{:S(2)}, u32[]{:S(2)}) collective-permute-start(bf16[48,2304]{1,0:T(8,128)(2,1)S(1)} %dynamic-slice_bitcast_fusion), channel_id=1, source_target_pairs={{0,64},{1,65},{4,68},{5,69},{8,72},{9,73},{12,76},{13,77},{16,80},... | collective-permute-start | bytes 663560 | tf_op jit(solution)/shard_map/ppermute | solution.py:363
  4.2 13.9 %collective-permute-start.1 = (bf16[48,2304]{1,0:T(8,128)(2,1)S(1)}, bf16[48,2304]{1,0:T(8,128)(2,1)S(1)}, u32[]{:S(2)}, u32[]{:S(2)}) collective-permute-start(bf16[48,2304]{1,0:T(8,128)(2,1)S(1)} %dynamic-slice_bitcast_fusion), channel_id=1, source_target_pairs={{0,128},{1,131},{4,132},{5,135},{8,136},{9,139},{12,140},{13,143},... | collective-permute-start | bytes 663560 | tf_op jit(solution)/shard_map/ppermute | solution.py:363
  9.3 9.9 %collective-permute-start = (bf16[48,2304]{1,0:T(8,128)(2,1)S(1)}, bf16[48,2304]{1,0:T(8,128)(2,1)S(1)}, u32[]{:S(2)}, u32[]{:S(2)}) collective-permute-start(bf16[48,2304]{1,0:T(8,128)(2,1)S(1)} %dynamic-slice_bitcast_fusion), channel_id=1, source_target_pairs={{0,194},{1,195},{4,198},{5,199},{8,202},{9,203},{12,206},{13,207},... | collective-permute-start | bytes 663560 | tf_op jit(solution)/shard_map/ppermute | solution.py:363
  10.0 0.7 copy-start.2
  10.7 1.1 copy-start
  10.7 1.3 %copy-start.1 = (bf16[2,2,48,2304]{3,2,1,0:T(8,128)(2,1)S(1)}, bf16[2,2,48,2304]{3,2,1,0:T(8,128)(2,1)}, u32[]{:S(2)}) copy-start(bf16[2,2,48,2304]{3,2,1,0:T(8,128)(2,1)} %cond.3) | copy-start | bytes 2654212
  10.7 2.1 %copy-start.3 = (bf16[2,768,768]{2,1,0:T(8,128)(2,1)S(1)}, bf16[2,768,768]{2,1,0:T(8,128)(2,1)}, u32[]{:S(2)}) copy-start(bf16[2,768,768]{2,1,0:T(8,128)(2,1)} %constant.120.clone.wide) | copy-start | bytes 7077892
  10.7 2.1 %copy-start.5 = (bf16[48,48]{1,0:T(8,128)(2,1)S(1)}, bf16[48,48]{1,0:T(8,128)(2,1)}, u32[]{:S(2)}) copy-start(bf16[48,48]{1,0:T(8,128)(2,1)} %constant.122.clone.ts) | copy-start | bytes 13828
  12.8 6.8 %copy-start.9 = (f32[4]{0:T(128)S(1)}, f32[4]{0:T(128)}, u32[]{:S(2)}) copy-start(f32[4]{0:T(128)} %param.11) | copy-start | bytes 52
  12.8 6.9 %copy-start.8 = (f32[2]{0:T(128)S(1)}, f32[2]{0:T(128)}, u32[]{:S(2)}) copy-start(f32[2]{0:T(128)} %param.12) | copy-start | bytes 28
  19.3 2.4 %collective-permute-start.3 = (bf16[3,48,2304]{2,1,0:T(8,128)(2,1)S(1)}, bf16[3,48,2304]{2,1,0:T(8,128)(2,1)S(1)}, u32[]{:S(2)}, u32[]{:S(2)}) collective-permute-start(bf16[3,48,2304]{2,1,0:T(8,128)(2,1)S(1)} %pad_maximum_fusion.part), channel_id=1, source_target_pairs={{0,1},{1,0},{4,5},{5,4},{8,9},{9,8},{12,13},{13,12},{16,17},{17,16... | collective-permute-start | bytes 1990664 | tf_op jit(solution)/shard_map/ppermute | solution.py:363
  21.7 1.7 %copy-start.4 = (bf16[2,768,768]{2,1,0:T(8,128)(2,1)S(1)}, bf16[2,768,768]{2,1,0:T(8,128)(2,1)}, u32[]{:S(2)}) copy-start(bf16[2,768,768]{2,1,0:T(8,128)(2,1)} %constant.120.clone.wide) | copy-start | bytes 7077892
  23.3 38.9 %copy-start.7 = (s32[4]{0:T(128)S(1)}, s32[4]{0:T(128)}, u32[]{:S(2)}) copy-start(s32[4]{0:T(128)} %constant.123.clone) | copy-start | bytes 52
  52.9 18.4 %all-to-all-start.1 = ((bf16[32,8,640]{2,1,0:T(8,128)(2,1)}), bf16[32,8,640]{2,1,0:T(8,128)(2,1)S(1)}, u32[]{:S(2)}, u32[]{:S(2)}) async-start(bf16[32,8,640]{2,1,0:T(8,128)(2,1)} %get-tuple-element.20), calls=%async_computation.1 | async-start | bytes 655360 | tf_op jit(solution)/shard_map/all_to_all | solution.py:404
  62.6 15.3 %collective-permute-start.9 = (bf16[64,1280]{1,0:T(8,128)(2,1)S(1)}, bf16[64,1280]{1,0:T(8,128)(2,1)S(1)}, u32[]{:S(2)}, u32[]{:S(2)}) collective-permute-start(bf16[64,1280]{1,0:T(8,128)(2,1)S(1)} %bitcast.22), channel_id=1, source_target_pairs={{0,4},{1,17},{4,8},{5,21},{8,12},{9,25},{12,0},{13,29},{16,20},{17... | collective-permute-start | bytes 491528 | tf_op jit(solution)/shard_map/ppermute | solution.py:363
  63.8 9.8 %collective-permute-start.8 = (bf16[64,1280]{1,0:T(8,128)(2,1)S(1)}, bf16[64,1280]{1,0:T(8,128)(2,1)S(1)}, u32[]{:S(2)}, u32[]{:S(2)}) collective-permute-start(bf16[64,1280]{1,0:T(8,128)(2,1)S(1)} %bitcast.23), channel_id=1, source_target_pairs={{0,12},{1,49},{4,0},{5,53},{8,4},{9,57},{12,8},{13,61},{16,28},{17... | collective-permute-start | bytes 491528 | tf_op jit(solution)/shard_map/ppermute | solution.py:363
  65.3 8.3 %collective-permute-start.7 = (bf16[64,1280]{1,0:T(8,128)(2,1)S(1)}, bf16[64,1280]{1,0:T(8,128)(2,1)S(1)}, u32[]{:S(2)}, u32[]{:S(2)}) collective-permute-start(bf16[64,1280]{1,0:T(8,128)(2,1)S(1)} %bitcast.24), channel_id=1, source_target_pairs={{0,8},{1,33},{4,12},{5,37},{8,0},{9,41},{12,4},{13,45},{16,24},{17... | collective-permute-start | bytes 491528 | tf_op jit(solution)/shard_map/ppermute | solution.py:363
  71.2 6.2 %collective-permute-start.4 = (bf16[2,16,8,640]{3,2,1,0:T(8,128)(2,1)S(1)}, bf16[2,16,8,640]{3,2,1,0:T(8,128)(2,1)S(1)}, u32[]{:S(2)}, u32[]{:S(2)}) collective-permute-start(bf16[2,16,8,640]{3,2,1,0:T(8,128)(2,1)S(1)} %bitcast.18), channel_id=1, source_target_pairs={{0,194},{1,65},{4,198},{5,69},{8,202},{9,73},{12,206},{13,77},{16,... | collective-permute-start | bytes 983048 | tf_op jit(solution)/shard_map/ppermute | solution.py:363
  77.4 7.1 %collective-permute-start.5 = (bf16[2,16,8,640]{3,2,1,0:T(8,128)(2,1)S(1)}, bf16[2,16,8,640]{3,2,1,0:T(8,128)(2,1)S(1)}, u32[]{:S(2)}, u32[]{:S(2)}) collective-permute-start(bf16[2,16,8,640]{3,2,1,0:T(8,128)(2,1)S(1)} %collective-permute-done.4.l1), channel_id=1, source_target_pairs={{0,64},{1,195},{4,68},{5,199},{8,72},{9,203},{12,76},{13,207},{16,... | collective-permute-start | bytes 983048 | tf_op jit(solution)/shard_map/ppermute | solution.py:363
  77.9 14.3 %collective-permute-start.12 = (bf16[256,1280]{1,0:T(8,128)(2,1)S(1)}, bf16[256,1280]{1,0:T(8,128)(2,1)S(1)}, u32[]{:S(2)}, u32[]{:S(2)}) collective-permute-start(bf16[256,1280]{1,0:T(8,128)(2,1)S(1)} %constant_dynamic-update-slice_fusion.r0), channel_id=1, source_target_pairs={{0,48},{1,13},{4,52},{5,1},{8,56},{9,5},{12,60},{13,9},{16,0},{17,... | collective-permute-start | bytes 1966088 | tf_op jit(solution)/shard_map/ppermute | solution.py:363
  79.1 13.1 %collective-permute-start.11 = (bf16[256,1280]{1,0:T(8,128)(2,1)S(1)}, bf16[256,1280]{1,0:T(8,128)(2,1)S(1)}, u32[]{:S(2)}, u32[]{:S(2)}) collective-permute-start(bf16[256,1280]{1,0:T(8,128)(2,1)S(1)} %constant_dynamic-update-slice_fusion.r0), channel_id=1, source_target_pairs={{0,32},{1,9},{4,36},{5,13},{8,40},{9,1},{12,44},{13,5},{16,48},{17... | collective-permute-start | bytes 1966088 | tf_op jit(solution)/shard_map/ppermute | solution.py:363
  79.9 17.4 %collective-permute-start.10 = (bf16[256,1280]{1,0:T(8,128)(2,1)S(1)}, bf16[256,1280]{1,0:T(8,128)(2,1)S(1)}, u32[]{:S(2)}, u32[]{:S(2)}) collective-permute-start(bf16[256,1280]{1,0:T(8,128)(2,1)S(1)} %constant_dynamic-update-slice_fusion.r0), channel_id=1, source_target_pairs={{0,16},{1,5},{4,20},{5,9},{8,24},{9,13},{12,28},{13,1},{16,32},{17... | collective-permute-start | bytes 1966088 | tf_op jit(solution)/shard_map/ppermute | solution.py:363
  84.6 6.2 %collective-permute-start.6 = (bf16[2,16,8,640]{3,2,1,0:T(8,128)(2,1)S(1)}, bf16[2,16,8,640]{3,2,1,0:T(8,128)(2,1)S(1)}, u32[]{:S(2)}, u32[]{:S(2)}) collective-permute-start(bf16[2,16,8,640]{3,2,1,0:T(8,128)(2,1)S(1)} %collective-permute-done.5.l2), channel_id=1, source_target_pairs={{0,194},{1,65},{4,198},{5,69},{8,202},{9,73},{12,206},{13,77},{16,... | collective-permute-start | bytes 983048 | tf_op jit(solution)/shard_map/ppermute | solution.py:363
  98.4 4.5 %collective-permute-start.13 = (bf16[320,640]{1,0:T(8,128)(2,1)S(1)}, bf16[320,640]{1,0:T(8,128)(2,1)S(1)}, u32[]{:S(2)}, u32[]{:S(2)}) collective-permute-start(bf16[320,640]{1,0:T(8,128)(2,1)S(1)} %get-tuple-element.23), channel_id=1, source_target_pairs={{0,1},{1,0},{4,5},{5,4},{8,9},{9,8},{12,13},{13,12},{16,17},{17,16... | collective-permute-start | bytes 1228808 | tf_op jit(solution)/shard_map/ppermute | solution.py:363

commit v5 on v4

--- a/solution.py
+++ b/solution.py
@@ -16,7 +16,7 @@
 F32 = jnp.float32
 BF16 = jnp.bfloat16
 WINDOW = 256
-GROUP = 4
+GROUP = 20
 BUCKETS = 24
 VM = pl.BlockSpec(memory_space=pltpu.VMEM)
 SM = pl.BlockSpec(memory_space=pltpu.SMEM)
@@ -48,7 +48,7 @@
     for j, tab in enumerate((cs[:24], half)):
         wy[:, :, :, j] = np.einsum("ab,kmi->maibk", eye16, tab.reshape(24, 6, 8))
     wy = wy.reshape(768, 768)
-    return np.stack([wz, wy]).astype(ml_dtypes.bfloat16), cos, sin
+    return wz.astype(ml_dtypes.bfloat16), wy.astype(ml_dtypes.bfloat16), cos, sin
 
 
 def column_of(y, z):
@@ -118,11 +118,11 @@
             xs[k, rows, 384:768] = (vr * ci - vi * cr).astype(BF16)
 
 
-def sections(val, cond, wide, xs, zs, s):
+def sections(val, cond, wz, wy, xs, zs, s):
     count = zs.shape[1] // 2
     for i in range(6):
         densities(val, cond, slice(i * 384, (i + 1) * 384), xs, i % 2)
-        out = jnp.dot(xs[i % 2], wide[0], preferred_element_type=F32).astype(BF16)
+        out = jnp.dot(xs[i % 2], wz[...], preferred_element_type=F32).astype(BF16)
         for t in range(3):
             for f in range(2):
                 zs[t, f * count : (f + 1) * count, i * 128 : (i + 1) * 128] = out[
@@ -130,8 +130,8 @@
                 ]
     edge = lax.broadcasted_iota(jnp.int32, (1, 384), 1) % 24 == 0
     for t in range(3):
-        cp = jnp.dot(zs[t], wide[1, :, :384], preferred_element_type=F32)
-        sp = jnp.dot(zs[t], wide[1, :, 384:], preferred_element_type=F32)
+        cp = jnp.dot(zs[t], wy[:, :384], preferred_element_type=F32)
+        sp = jnp.dot(zs[t], wy[:, 384:], preferred_element_type=F32)
         cre, cim, sre, sim = cp[:count], cp[count:], sp[:count], sp[count:]
         outs = (
             (jnp.where(edge, cre, cre + sim), jnp.where(edge, sre, cre - sim)),
@@ -189,32 +189,32 @@
     lax.fori_loop(0, 20 // GROUP, step, 0)
 
 
-def own_kernel(val, cond, wide, tc, ts, starts, key, m, xs, zs, s):
+def own_kernel(val, cond, wz, wy, tc, ts, starts, key, m, xs, zs, s):
     def band(cols):
         return val[0, 0, :, cols].astype(F32), val[0, 1, :, cols].astype(F32)
 
-    sections([band], cond, wide, xs, zs, s)
+    sections([band], cond, wz, wy, xs, zs, s)
     select(s, tc, ts, starts, key, m, 0)
 
 
-def rest_kernel(core, part, other, cond, wide, tc, ts, starts, key, back, w, owned, left, right, xs, zs, s, m, mo):
+def rest_kernel(core, ve, ce, p0, p1, p2, o0, o1, o2, cond, wz, wy, tc, ts, starts, key, back, owned, left, right, xs, zs, s, m, mo):
     first = core[0] == 0
 
     def band(v):
         def read(cols):
-            a = part[v, :, cols].astype(F32)
-            b = other[v, :, cols].astype(F32)
+            a = (p0, p1, p2)[v][:, cols].astype(F32)
+            b = (o0, o1, o2)[v][:, cols].astype(F32)
             return jnp.where(first, a, b), jnp.where(first, b, a)
 
         return read
 
-    sections([band(v) for v in range(3)], cond, wide, xs, zs, s)
+    sections([band(v) for v in range(3)], cond, wz, wy, xs, zs, s)
     select(s, tc, ts, starts, key, m, 2)
     m[:, 0:2, :] = owned[...]
 
     def unsort(group, _):
-        for u in range(4):
-            cols = pl.ds(pl.multiple_of((group * 4 + u) * 128, 128), 128)
+        for u in range(8):
+            cols = pl.ds(pl.multiple_of((group * 8 + u) * 128, 128), 128)
             place = jnp.broadcast_to(back[:, cols], (8, 128))
             source = place >> 7
             lane = place & 127
@@ -228,11 +228,16 @@
                 mo[f, :, cols] = outs[f]
         return 0
 
-    lax.fori_loop(0, 10, unsort, 0)
+    lax.fori_loop(0, 5, unsort, 0)
     for z in range(8):
         for f in range(2):
             right[z, :, f * 640 : (f + 1) * 640] = mo[f, :, z * 640 : (z + 1) * 640].astype(BF16)
-    weight = w[...]
+    pair = lax.broadcasted_iota(jnp.int32, (8, 1), 0)
+    gap = jnp.zeros((8, 1), F32)
+    for v in range(NV):
+        for c in range(2):
+            gap = jnp.where(pair == v * 2 + c, ve[(core[1] + v) & 3] - ce[c], gap)
+    weight = 2.0 / (gap * math.sqrt(NV * 512))
     for r in range(16):
         parts = []
         for f in range(2):
@@ -257,7 +262,7 @@
     return pl.pallas_call(
         own_kernel,
         out_shape=jax.ShapeDtypeStruct((2, 2, NG), F32),
-        in_specs=[VM] * 5 + [SM, VM],
+        in_specs=[VM] * 6 + [SM, VM],
         out_specs=VM,
         scratch_shapes=scratch(2),
         compiler_params=pltpu.CompilerParams(vmem_limit_bytes=16 * 2**20),
@@ -265,19 +270,19 @@
     )(val, cond, *wide, key, key)
 
 
-def coefficients(core, part, other, cond, wide, key, back, w, owned):
+def coefficients(core, ve, ce, part, other, cond, wide, key, back, owned):
     return pl.pallas_call(
         rest_kernel,
         out_shape=(
             jax.ShapeDtypeStruct((32, 8, 640), BF16),
             jax.ShapeDtypeStruct((8, 8, 1280), BF16),
         ),
-        in_specs=[SM] + [VM] * 6 + [SM] + [VM] * 4,
+        in_specs=[SM] * 3 + [VM] * 11 + [SM] + [VM] * 3,
         out_specs=(VM, VM),
         scratch_shapes=scratch(6) + [pltpu.VMEM((2, 8, NG), F32)] * 2,
         compiler_params=pltpu.CompilerParams(vmem_limit_bytes=24 * 2**20),
         cost_estimate=pl.CostEstimate(flops=10**10, bytes_accessed=5 * 10**7, transcendentals=0),
-    )(core, part, other, cond, *wide, key, key, back, w, owned)
+    )(core, ve, ce, *part, *other, cond, *wide, key, key, back, owned)
 
 
 def left_kernel(place, rows, l0, l1, l2, l3, turned, held, lk):
@@ -426,26 +431,21 @@
     core = jnp.reshape(c, (1,)).astype(jnp.int32)
 
     piece = lax.dynamic_index_in_dim(valence[0], c, 0, keepdims=False)
-    part = jnp.concatenate(
-        [
-            send_z(piece, -1)[None],
-            send(piece, lambda z, y, x, c: (z + 2 - 4 * c, y, x, c))[None],
-            send_z(piece, 1)[None],
-        ]
-    )
+    part = [
+        send_z(piece, -1),
+        send(piece, lambda z, y, x, c: (z + 2 - 4 * c, y, x, c)),
+        send_z(piece, 1),
+    ]
 
     key, back = sort_waves(g_index.reshape(1, NG))
-
-    energies = lax.dynamic_slice(jnp.tile(valence_energy, 2), (p,), (NV,))
-    scale = math.sqrt(NV * 512)
-    weight = 2.0 / ((energies[:, None] - conduction_energy[None, :]) * scale)
 
     wide = [jnp.asarray(t) for t in wide_tables()]
     owned = own_coefficients(valence, conduction, wide, key)
     part, owned = lax.optimization_barrier((part, owned))
-    other = send_core(part)
+    other = [send_core(v) for v in part]
+    mine = jnp.stack([c, p]).astype(jnp.int32)
     left, right = coefficients(
-        core, part, other, conduction, wide, key, back, weight.reshape(8, 1), owned
+        mine, valence_energy, conduction_energy, part, other, conduction, wide, key, back, owned
     )
 
     right = lax.all_to_all(right, ("h", "p"), 0, 0, tiled=True).reshape(64, 1280)

time: 120 us -> 119 us (level)
    unnamed x23 -> x25, local copies, waits for them, and re-layouts: 3.48 us -> 3.02 us
    ppermute x14 -> x16, starting transfers between devices: 18.7 us -> 18.9 us  [send(): return lax.ppermute(values, AXES, pairs)]
    ppermute x14 -> x16, waiting for transfers between devices: 24.2 us -> 24.2 us  [send(): return lax.ppermute(values, AXES, pairs)]
  transfers between devices with their start and end apart: 15 -> 17, of which waited for: 9 -> 11; matrix products, arithmetic and copies ran while one was open for 1% -> 1% of each run, Pallas kernels for 8% -> 8%
where the time goes in v5:
time: 119 us; the launch traced here: 118 us
  blocking collectives  28.7 us (24%)
  waiting for transfers between devices  28.6 us (24%)
  starting transfers between devices  28.1 us (24%)
  Pallas kernels  27 us (23%)
  local copies, waits for them, and re-layouts  4.32 us (4%)
    ppermute x16, waiting for transfers between devices, send(): return lax.ppermute(values, AXES, pairs)  24.2 us
    ppermute x16, starting transfers between devices, send(): return lax.ppermute(values, AXES, pairs)  18.9 us
    pallas_call x1, Pallas kernels, coefficients(): pl.pallas_call(rest_kernel, out_shape=(jax.ShapeDtypeStruct((32, 8, 640),...  15 us
    all_to_all x1, blocking collectives, local(): return assemble(lax.all_to_all(tile, 'p', 0, 0, tiled=True))  14.7 us
    all_to_all x1, blocking collectives, local(): lax.all_to_all(right, ('h', 'p'), 0, 0, tiled=True).reshape(64, 1280)  14 us
    all_to_all x1, starting transfers between devices, pair_exchange(): got = lax.all_to_all(left, AXES, 0, 0, axis_index_groups=groups, tiled=True)  9.2 us
    pallas_call x1, Pallas kernels, own_coefficients(): pl.pallas_call(own_kernel, out_shape=jax.ShapeDtypeStruct((2, 2, NG), F32...  5.03 us
    all_to_all x1, waiting for transfers between devices, pair_exchange(): got = lax.all_to_all(left, AXES, 0, 0, axis_index_groups=groups, tiled=True)  4.43 us
  transfers between devices with their start and end apart: 17, of which 11 were waited for; matrix products, arithmetic and copies ran while one was open for 1% of the time, Pallas kernels for 8%

profile of v5, /device:TPU:1, one launch (start us, length us, event | category | flops | bytes accessed | tf_op | source)
XLA Modules:
  0.0 118.5 jit_solution(1672672163172428932)
XLA Ops:
  0.6 0.0 copy-start.9
  0.6 1.0 dynamic-slice_bitcast_fusion
  1.6 2.5 %collective-permute-start.2 = (bf16[48,2304]{1,0:T(8,128)(2,1)S(1)}, bf16[48,2304]{1,0:T(8,128)(2,1)S(1)}, u32[]{:S(2)}, u32[]{:S(2)}) collective-permute-start(bf16[48,2304]{1,0:T(8,128)(2,1)S(1)} %dynamic-slice_bitcast_fusion), channel_id=1, source_target_pairs={{0,64},{1,65},{4,68},{5,69},{8,72},{9,73},{12,76},{13,77},{16,80},... | collective-permute-start | bytes 663560 | tf_op jit(solution)/shard_map/ppermute | solution.py:368
  4.2 5.1 %collective-permute-start.1 = (bf16[48,2304]{1,0:T(8,128)(2,1)S(1)}, bf16[48,2304]{1,0:T(8,128)(2,1)S(1)}, u32[]{:S(2)}, u32[]{:S(2)}) collective-permute-start(bf16[48,2304]{1,0:T(8,128)(2,1)S(1)} %dynamic-slice_bitcast_fusion), channel_id=1, source_target_pairs={{0,128},{1,131},{4,132},{5,135},{8,136},{9,139},{12,140},{13,143},... | collective-permute-start | bytes 663560 | tf_op jit(solution)/shard_map/ppermute | solution.py:368
  9.3 0.7 collective-permute-start
  10.0 0.7 copy-done.2
  10.7 0.0 copy-start.8
  10.8 1.0 shard_map.113
  11.8 0.2 copy-done.1
  12.0 0.4 copy-done.5
  12.4 0.4 copy-done.6
  12.8 5.0 %shard_map.114.owned = f32[2,2,5120]{2,1,0:T(2,128)S(1)} custom-call(bf16[1,2,48,2304]{3,2,1,0:T(8,128)(2,1)S(1)} %copy-done, bf16[2,2,48,2304]{3,2,1,0:T(8,128)(2,1)S(1)} %copy-done.1, bf16[768,768]{1,0:T(8,128)(2,1)S(1)} %copy-done.6, bf16[768,768]{1,0:T(8,128)(2,1)S(1)} %copy-done.5, bf16[48,48]{1,0:T(8,128)(2,1)S(1)} %copy-done.9, ...), custom_call_target="tpu_custom_call" | custom-call | flops 5000000000 | bytes 30000000 | tf_op jit(solution)/shard_map/pallas_call | solution.py:262
  17.8 1.4 %collective-permute-done.p0 = bf16[48,2304]{1,0:T(8,128)(2,1)S(1)} collective-permute-done((bf16[48,2304]{1,0:T(8,128)(2,1)S(1)}, bf16[48,2304]{1,0:T(8,128)(2,1)S(1)}, u32[]{:S(2)}, u32[]{:S(2)}) %collective-permute-start) | collective-permute-done | bytes 221216 | tf_op jit(solution)/shard_map/ppermute | solution.py:368
  19.2 0.5 collective-permute-start.4
  19.7 0.1 pad_add_fusion.core
  19.8 0.9 collective-permute-done.3.o0
  20.7 0.3 collective-permute-done.4.o1
  21.0 0.3 collective-permute-done.5.o2
  21.3 1.3 %copy-done.7 = bf16[768,768]{1,0:T(8,128)(2,1)S(1)} copy-done((bf16[768,768]{1,0:T(8,128)(2,1)S(1)}, bf16[768,768]{1,0:T(8,128)(2,1)}, u32[]{:S(2)}) %copy-start.7) | copy-done | bytes 1179672
  22.6 15.0 %shard_map.115 = (bf16[32,8,640]{2,1,0:T(8,128)(2,1)}, bf16[8,8,1280]{2,1,0:T(8,128)(2,1)S(1)}) custom-call(s32[2]{0:T(128)S(1)} %pad_add_fusion.core, f32[4]{0:T(128)S(1)} %copy-done.3, f32[2]{0:T(128)S(1)} %copy-done.4, bf16[48,2304]{1,0:T(8,128)(2,1)S(1)} %collective-permute-done.p0, bf16[48,2304]{1,0:T(8,128)(2,1)S(1)} %collective-permute-done.1.p1, ...), custom_call_target="tpu_custom_call" | custom-call | flops 10000000000 | bytes 50000000 | tf_op jit(solution)/shard_map/pallas_call | solution.py:274
  37.6 14.0 %all_to_all.15 = bf16[8,8,1280]{2,1,0:T(8,128)(2,1)S(1)} all-to-all(bf16[8,8,1280]{2,1,0:T(8,128)(2,1)S(1)} %get-tuple-element.23), channel_id=1, replica_groups=mesh['p'=4,'y'=4,'x'=4,'h'=2,'c'=2] {'h','p'}, dimensions={0} | all-to-all | bytes 327680 | tf_op jit(solution)/shard_map/all_to_all | solution.py:451
  51.6 9.2 %all-to-all-start.1 = ((bf16[32,8,640]{2,1,0:T(8,128)(2,1)}), bf16[32,8,640]{2,1,0:T(8,128)(2,1)S(1)}, u32[]{:S(2)}, u32[]{:S(2)}) async-start(bf16[32,8,640]{2,1,0:T(8,128)(2,1)} %get-tuple-element.24), calls=%async_computation.1 | async-start | bytes 655360 | tf_op jit(solution)/shard_map/all_to_all | solution.py:409
  61.0 0.1 tile.10
  61.1 0.1 broadcast_in_dim.2
  61.1 0.1 reshape.102
  61.2 0.1 stack.42
  61.3 1.2 %collective-permute-start.11 = (bf16[64,1280]{1,0:T(8,128)(2,1)S(1)}, bf16[64,1280]{1,0:T(8,128)(2,1)S(1)}, u32[]{:S(2)}, u32[]{:S(2)}) collective-permute-start(bf16[64,1280]{1,0:T(8,128)(2,1)S(1)} %bitcast.20), channel_id=1, source_target_pairs={{0,4},{1,17},{4,8},{5,21},{8,12},{9,25},{12,0},{13,29},{16,20},{17... | collective-permute-start | bytes 491528 | tf_op jit(solution)/shard_map/ppermute | solution.py:368
  62.5 1.5 %collective-permute-start.10 = (bf16[64,1280]{1,0:T(8,128)(2,1)S(1)}, bf16[64,1280]{1,0:T(8,128)(2,1)S(1)}, u32[]{:S(2)}, u32[]{:S(2)}) collective-permute-start(bf16[64,1280]{1,0:T(8,128)(2,1)S(1)} %bitcast.21), channel_id=1, source_target_pairs={{0,12},{1,49},{4,0},{5,53},{8,4},{9,57},{12,8},{13,61},{16,28},{17... | collective-permute-start | bytes 491528 | tf_op jit(solution)/shard_map/ppermute | solution.py:368
  64.0 1.5 %collective-permute-start.9 = (bf16[64,1280]{1,0:T(8,128)(2,1)S(1)}, bf16[64,1280]{1,0:T(8,128)(2,1)S(1)}, u32[]{:S(2)}, u32[]{:S(2)}) collective-permute-start(bf16[64,1280]{1,0:T(8,128)(2,1)S(1)} %bitcast.22), channel_id=1, source_target_pairs={{0,8},{1,33},{4,12},{5,37},{8,0},{9,41},{12,4},{13,45},{16,24},{17... | collective-permute-start | bytes 491528 | tf_op jit(solution)/shard_map/ppermute | solution.py:368
  65.5 4.4 %all-to-all-done.1 = bf16[32,8,640]{2,1,0:T(8,128)(2,1)S(1)} async-done(((bf16[32,8,640]{2,1,0:T(8,128)(2,1)}), bf16[32,8,640]{2,1,0:T(8,128)(2,1)S(1)}, u32[]{:S(2)}, u32[]{:S(2)}) %all-to-all-start.1) | async-done | bytes 327712 | tf_op jit(solution)/shard_map/all_to_all | solution.py:409
  70.0 2.3 %collective-permute-done.9 = bf16[64,1280]{1,0:T(8,128)(2,1)S(1)} collective-permute-done((bf16[64,1280]{1,0:T(8,128)(2,1)S(1)}, bf16[64,1280]{1,0:T(8,128)(2,1)S(1)}, u32[]{:S(2)}, u32[]{:S(2)}) %collective-permute-start.9) | collective-permute-done | bytes 163872 | tf_op jit(solution)/shard_map/ppermute | solution.py:368
  72.3 3.9 %collective-permute-done.6.l1 = bf16[2,16,8,640]{3,2,1,0:T(8,128)(2,1)S(1)} collective-permute-done((bf16[2,16,8,640]{3,2,1,0:T(8,128)(2,1)S(1)}, bf16[2,16,8,640]{3,2,1,0:T(8,128)(2,1)S(1)}, u32[]{:S(2)}, u32[]{:S(2)}) %collective-permute-start.6) | collective-permute-done | bytes 327712 | tf_op jit(solution)/shard_map/ppermute | solution.py:368
  76.2 0.5 collective-permute-start.7
  76.7 1.1 collective-permute-start.14
  77.8 0.8 collective-permute-start.13
  78.6 0.2 collective-permute-start.12
  78.9 4.5 %collective-permute-done.7.l2 = bf16[2,16,8,640]{3,2,1,0:T(8,128)(2,1)S(1)} collective-permute-done((bf16[2,16,8,640]{3,2,1,0:T(8,128)(2,1)S(1)}, bf16[2,16,8,640]{3,2,1,0:T(8,128)(2,1)S(1)}, u32[]{:S(2)}, u32[]{:S(2)}) %collective-permute-start.7) | collective-permute-done | bytes 327712 | tf_op jit(solution)/shard_map/ppermute | solution.py:368
  83.3 0.6 iota_reduce_fusion
  84.0 5.6 %collective-permute-done.8.l3 = bf16[2,16,8,640]{3,2,1,0:T(8,128)(2,1)S(1)} collective-permute-done((bf16[2,16,8,640]{3,2,1,0:T(8,128)(2,1)S(1)}, bf16[2,16,8,640]{3,2,1,0:T(8,128)(2,1)S(1)}, u32[]{:S(2)}, u32[]{:S(2)}) %collective-permute-start.8) | collective-permute-done | bytes 327712 | tf_op jit(solution)/shard_map/ppermute | solution.py:368
  89.5 1.4 %shard_map.116.left = bf16[640,1024]{1,0:T(8,128)(2,1)S(1)} custom-call(s32[8]{0:T(128)S(1)} %get-tuple-element.15.place, s32[16]{0:T(128)S(1)} %broadcast_select_fusion.rows, bf16[2,16,8,640]{3,2,1,0:T(8,128)(2,1)S(1)} %bitcast.17, bf16[2,16,8,640]{3,2,1,0:T(8,128)(2,1)S(1)} %collective-permute-done.6.l1, ...), custom_call_target="tpu_custom_call" | custom-call | tf_op jit(solution)/shard_map/pallas_call | solution.py:304
  91.0 1.4 %shard_map.117.acc = f32[2,320,640]{2,1,0:T(8,128)S(1)} custom-call(bf16[640,1024]{1,0:T(8,128)(2,1)S(1)} %shard_map.116.left, bf16[256,1280]{1,0:T(8,128)(2,1)S(1)} %constant_dynamic-update-slice_fusion.r0, bf16[256,1280]{1,0:T(8,128)(2,1)S(1)} %collective-permute-done.13.r1, bf16[256,1280]{1,0:T(8,128)(2,1)S(1)} %collective-permute-done.14.r2), custom_call_target="tpu_custom_call" | custom-call | tf_op jit(solution)/shard_map/pallas_call | solution.py:339
  92.4 3.7 %collective-permute-done.12.r3 = bf16[256,1280]{1,0:T(8,128)(2,1)S(1)} collective-permute-done((bf16[256,1280]{1,0:T(8,128)(2,1)S(1)}, bf16[256,1280]{1,0:T(8,128)(2,1)S(1)}, u32[]{:S(2)}, u32[]{:S(2)}) %collective-permute-start.12) | collective-permute-done | bytes 655392 | tf_op jit(solution)/shard_map/ppermute | solution.py:368
  96.1 1.1 shard_map.118
  97.1 3.1 %collective-permute-start.15 = (bf16[320,640]{1,0:T(8,128)(2,1)S(1)}, bf16[320,640]{1,0:T(8,128)(2,1)S(1)}, u32[]{:S(2)}, u32[]{:S(2)}) collective-permute-start(bf16[320,640]{1,0:T(8,128)(2,1)S(1)} %get-tuple-element.27), channel_id=1, source_target_pairs={{0,1},{1,0},{4,5},{5,4},{8,9},{9,8},{12,13},{13,12},{16,17},{17,16... | collective-permute-start | bytes 1228808 | tf_op jit(solution)/shard_map/ppermute | solution.py:368
  100.3 1.4 %collective-permute-done.15 = bf16[320,640]{1,0:T(8,128)(2,1)S(1)} collective-permute-done((bf16[320,640]{1,0:T(8,128)(2,1)S(1)}, bf16[320,640]{1,0:T(8,128)(2,1)S(1)}, u32[]{:S(2)}, u32[]{:S(2)}) %collective-permute-start.15) | collective-permute-done | bytes 409632 | tf_op jit(solution)/shard_map/ppermute | solution.py:368
  101.7 0.1 add_convert_fusion
  101.8 14.7 %all_to_all.16.tile = bf16[4,80,640]{2,1,0:T(8,128)(2,1)} all-to-all(bf16[4,80,640]{2,1,0:T(8,128)(2,1)S(1)} %bitcast.19), channel_id=1, replica_groups=mesh['p'=4,'y'=4,'x'=4,'h'=2,'c'=2] {'p'}, dimensions={0} | all-to-all | bytes 819200 | tf_op jit(solution)/shard_map/all_to_all | solution.py:476
  116.5 2.0 %shard_map.119 = (f32[80,1280]{1,0:T(8,128)}, f32[80,1280]{1,0:T(8,128)}) custom-call(bf16[4,80,640]{2,1,0:T(8,128)(2,1)} %all_to_all.16.tile), custom_call_target="tpu_custom_call" | custom-call | tf_op jit(solution)/shard_map/pallas_call | solution.py:420
  (33 shorter events, 0.1 us)
Async XLA Ops:
  0.6 11.2 %copy-start.9 = (bf16[48,48]{1,0:T(8,128)(2,1)S(1)}, bf16[48,48]{1,0:T(8,128)(2,1)}, u32[]{:S(2)}) copy-start(bf16[48,48]{1,0:T(8,128)(2,1)} %constant.120.clone.tc) | copy-start | bytes 13828
  1.6 16.2 %collective-permute-start.2 = (bf16[48,2304]{1,0:T(8,128)(2,1)S(1)}, bf16[48,2304]{1,0:T(8,128)(2,1)S(1)}, u32[]{:S(2)}, u32[]{:S(2)}) collective-permute-start(bf16[48,2304]{1,0:T(8,128)(2,1)S(1)} %dynamic-slice_bitcast_fusion), channel_id=1, source_target_pairs={{0,64},{1,65},{4,68},{5,69},{8,72},{9,73},{12,76},{13,77},{16,80},... | collective-permute-start | bytes 663560 | tf_op jit(solution)/shard_map/ppermute | solution.py:368
  4.2 13.7 %collective-permute-start.1 = (bf16[48,2304]{1,0:T(8,128)(2,1)S(1)}, bf16[48,2304]{1,0:T(8,128)(2,1)S(1)}, u32[]{:S(2)}, u32[]{:S(2)}) collective-permute-start(bf16[48,2304]{1,0:T(8,128)(2,1)S(1)} %dynamic-slice_bitcast_fusion), channel_id=1, source_target_pairs={{0,128},{1,131},{4,132},{5,135},{8,136},{9,139},{12,140},{13,143},... | collective-permute-start | bytes 663560 | tf_op jit(solution)/shard_map/ppermute | solution.py:368
  9.3 9.9 %collective-permute-start = (bf16[48,2304]{1,0:T(8,128)(2,1)S(1)}, bf16[48,2304]{1,0:T(8,128)(2,1)S(1)}, u32[]{:S(2)}, u32[]{:S(2)}) collective-permute-start(bf16[48,2304]{1,0:T(8,128)(2,1)S(1)} %dynamic-slice_bitcast_fusion), channel_id=1, source_target_pairs={{0,194},{1,195},{4,198},{5,199},{8,202},{9,203},{12,206},{13,207},... | collective-permute-start | bytes 663560 | tf_op jit(solution)/shard_map/ppermute | solution.py:368
  10.0 0.7 copy-start.2
  10.7 1.1 copy-start
  10.7 1.3 %copy-start.1 = (bf16[2,2,48,2304]{3,2,1,0:T(8,128)(2,1)S(1)}, bf16[2,2,48,2304]{3,2,1,0:T(8,128)(2,1)}, u32[]{:S(2)}) copy-start(bf16[2,2,48,2304]{3,2,1,0:T(8,128)(2,1)} %cond.3) | copy-start | bytes 2654212
  10.7 1.7 %copy-start.5 = (bf16[768,768]{1,0:T(8,128)(2,1)S(1)}, bf16[768,768]{1,0:T(8,128)(2,1)}, u32[]{:S(2)}) copy-start(bf16[768,768]{1,0:T(8,128)(2,1)} %constant.119.clone.wy) | copy-start | bytes 3538948
  10.7 2.0 %copy-start.6 = (bf16[768,768]{1,0:T(8,128)(2,1)S(1)}, bf16[768,768]{1,0:T(8,128)(2,1)}, u32[]{:S(2)}) copy-start(bf16[768,768]{1,0:T(8,128)(2,1)} %constant.118.clone.wz) | copy-start | bytes 3538948
  10.7 2.0 %copy-start.8 = (bf16[48,48]{1,0:T(8,128)(2,1)S(1)}, bf16[48,48]{1,0:T(8,128)(2,1)}, u32[]{:S(2)}) copy-start(bf16[48,48]{1,0:T(8,128)(2,1)} %constant.121.clone.ts) | copy-start | bytes 13828
  12.8 8.6 %copy-start.3 = (f32[4]{0:T(128)S(1)}, f32[4]{0:T(128)}, u32[]{:S(2)}) copy-start(f32[4]{0:T(128)} %ve.1) | copy-start | bytes 52
  12.8 8.6 %copy-start.4 = (f32[2]{0:T(128)S(1)}, f32[2]{0:T(128)}, u32[]{:S(2)}) copy-start(f32[2]{0:T(128)} %ce.1) | copy-start | bytes 28
  19.2 1.5 %collective-permute-start.3 = (bf16[48,2304]{1,0:T(8,128)(2,1)S(1)}, bf16[48,2304]{1,0:T(8,128)(2,1)S(1)}, u32[]{:S(2)}, u32[]{:S(2)}) collective-permute-start(bf16[48,2304]{1,0:T(8,128)(2,1)S(1)} %collective-permute-done.p0), channel_id=1, source_target_pairs={{0,1},{1,0},{4,5},{5,4},{8,9},{9,8},{12,13},{13,12},{16,17},{17,16... | collective-permute-start | bytes 663560 | tf_op jit(solution)/shard_map/ppermute | solution.py:368
  19.2 1.8 %collective-permute-start.4 = (bf16[48,2304]{1,0:T(8,128)(2,1)S(1)}, bf16[48,2304]{1,0:T(8,128)(2,1)S(1)}, u32[]{:S(2)}, u32[]{:S(2)}) collective-permute-start(bf16[48,2304]{1,0:T(8,128)(2,1)S(1)} %collective-permute-done.1.p1), channel_id=1, source_target_pairs={{0,1},{1,0},{4,5},{5,4},{8,9},{9,8},{12,13},{13,12},{16,17},{17,16... | collective-permute-start | bytes 663560 | tf_op jit(solution)/shard_map/ppermute | solution.py:368
  19.7 1.6 %collective-permute-start.5 = (bf16[48,2304]{1,0:T(8,128)(2,1)S(1)}, bf16[48,2304]{1,0:T(8,128)(2,1)S(1)}, u32[]{:S(2)}, u32[]{:S(2)}) collective-permute-start(bf16[48,2304]{1,0:T(8,128)(2,1)S(1)} %collective-permute-done.2.p2), channel_id=1, source_target_pairs={{0,1},{1,0},{4,5},{5,4},{8,9},{9,8},{12,13},{13,12},{16,17},{17,16... | collective-permute-start | bytes 663560 | tf_op jit(solution)/shard_map/ppermute | solution.py:368
  21.3 1.3 %copy-start.7 = (bf16[768,768]{1,0:T(8,128)(2,1)S(1)}, bf16[768,768]{1,0:T(8,128)(2,1)}, u32[]{:S(2)}) copy-start(bf16[768,768]{1,0:T(8,128)(2,1)} %constant.118.clone.wz) | copy-start | bytes 3538948
  22.6 38.3 %copy-start.10 = (s32[4]{0:T(128)S(1)}, s32[4]{0:T(128)}, u32[]{:S(2)}) copy-start(s32[4]{0:T(128)} %constant.122.clone) | copy-start | bytes 52
  51.6 18.4 %all-to-all-start.1 = ((bf16[32,8,640]{2,1,0:T(8,128)(2,1)}), bf16[32,8,640]{2,1,0:T(8,128)(2,1)S(1)}, u32[]{:S(2)}, u32[]{:S(2)}) async-start(bf16[32,8,640]{2,1,0:T(8,128)(2,1)} %get-tuple-element.24), calls=%async_computation.1 | async-start | bytes 655360 | tf_op jit(solution)/shard_map/all_to_all | solution.py:409
  61.3 15.3 %collective-permute-start.11 = (bf16[64,1280]{1,0:T(8,128)(2,1)S(1)}, bf16[64,1280]{1,0:T(8,128)(2,1)S(1)}, u32[]{:S(2)}, u32[]{:S(2)}) collective-permute-start(bf16[64,1280]{1,0:T(8,128)(2,1)S(1)} %bitcast.20), channel_id=1, source_target_pairs={{0,4},{1,17},{4,8},{5,21},{8,12},{9,25},{12,0},{13,29},{16,20},{17... | collective-permute-start | bytes 491528 | tf_op jit(solution)/shard_map/ppermute | solution.py:368
  62.5 9.8 %collective-permute-start.10 = (bf16[64,1280]{1,0:T(8,128)(2,1)S(1)}, bf16[64,1280]{1,0:T(8,128)(2,1)S(1)}, u32[]{:S(2)}, u32[]{:S(2)}) collective-permute-start(bf16[64,1280]{1,0:T(8,128)(2,1)S(1)} %bitcast.21), channel_id=1, source_target_pairs={{0,12},{1,49},{4,0},{5,53},{8,4},{9,57},{12,8},{13,61},{16,28},{17... | collective-permute-start | bytes 491528 | tf_op jit(solution)/shard_map/ppermute | solution.py:368
  64.0 8.3 %collective-permute-start.9 = (bf16[64,1280]{1,0:T(8,128)(2,1)S(1)}, bf16[64,1280]{1,0:T(8,128)(2,1)S(1)}, u32[]{:S(2)}, u32[]{:S(2)}) collective-permute-start(bf16[64,1280]{1,0:T(8,128)(2,1)S(1)} %bitcast.22), channel_id=1, source_target_pairs={{0,8},{1,33},{4,12},{5,37},{8,0},{9,41},{12,4},{13,45},{16,24},{17... | collective-permute-start | bytes 491528 | tf_op jit(solution)/shard_map/ppermute | solution.py:368
  70.0 6.2 %collective-permute-start.6 = (bf16[2,16,8,640]{3,2,1,0:T(8,128)(2,1)S(1)}, bf16[2,16,8,640]{3,2,1,0:T(8,128)(2,1)S(1)}, u32[]{:S(2)}, u32[]{:S(2)}) collective-permute-start(bf16[2,16,8,640]{3,2,1,0:T(8,128)(2,1)S(1)} %bitcast.16), channel_id=1, source_target_pairs={{0,194},{1,65},{4,198},{5,69},{8,202},{9,73},{12,206},{13,77},{16,... | collective-permute-start | bytes 983048 | tf_op jit(solution)/shard_map/ppermute | solution.py:368
  76.2 7.1 %collective-permute-start.7 = (bf16[2,16,8,640]{3,2,1,0:T(8,128)(2,1)S(1)}, bf16[2,16,8,640]{3,2,1,0:T(8,128)(2,1)S(1)}, u32[]{:S(2)}, u32[]{:S(2)}) collective-permute-start(bf16[2,16,8,640]{3,2,1,0:T(8,128)(2,1)S(1)} %collective-permute-done.6.l1), channel_id=1, source_target_pairs={{0,64},{1,195},{4,68},{5,199},{8,72},{9,203},{12,76},{13,207},{16,... | collective-permute-start | bytes 983048 | tf_op jit(solution)/shard_map/ppermute | solution.py:368
  76.7 14.3 %collective-permute-start.14 = (bf16[256,1280]{1,0:T(8,128)(2,1)S(1)}, bf16[256,1280]{1,0:T(8,128)(2,1)S(1)}, u32[]{:S(2)}, u32[]{:S(2)}) collective-permute-start(bf16[256,1280]{1,0:T(8,128)(2,1)S(1)} %constant_dynamic-update-slice_fusion.r0), channel_id=1, source_target_pairs={{0,48},{1,13},{4,52},{5,1},{8,56},{9,5},{12,60},{13,9},{16,0},{17,... | collective-permute-start | bytes 1966088 | tf_op jit(solution)/shard_map/ppermute | solution.py:368
  77.8 13.1 %collective-permute-start.13 = (bf16[256,1280]{1,0:T(8,128)(2,1)S(1)}, bf16[256,1280]{1,0:T(8,128)(2,1)S(1)}, u32[]{:S(2)}, u32[]{:S(2)}) collective-permute-start(bf16[256,1280]{1,0:T(8,128)(2,1)S(1)} %constant_dynamic-update-slice_fusion.r0), channel_id=1, source_target_pairs={{0,32},{1,9},{4,36},{5,13},{8,40},{9,1},{12,44},{13,5},{16,48},{17... | collective-permute-start | bytes 1966088 | tf_op jit(solution)/shard_map/ppermute | solution.py:368
  78.6 17.4 %collective-permute-start.12 = (bf16[256,1280]{1,0:T(8,128)(2,1)S(1)}, bf16[256,1280]{1,0:T(8,128)(2,1)S(1)}, u32[]{:S(2)}, u32[]{:S(2)}) collective-permute-start(bf16[256,1280]{1,0:T(8,128)(2,1)S(1)} %constant_dynamic-update-slice_fusion.r0), channel_id=1, source_target_pairs={{0,16},{1,5},{4,20},{5,9},{8,24},{9,13},{12,28},{13,1},{16,32},{17... | collective-permute-start | bytes 1966088 | tf_op jit(solution)/shard_map/ppermute | solution.py:368
  83.3 6.2 %collective-permute-start.8 = (bf16[2,16,8,640]{3,2,1,0:T(8,128)(2,1)S(1)}, bf16[2,16,8,640]{3,2,1,0:T(8,128)(2,1)S(1)}, u32[]{:S(2)}, u32[]{:S(2)}) collective-permute-start(bf16[2,16,8,640]{3,2,1,0:T(8,128)(2,1)S(1)} %collective-permute-done.7.l2), channel_id=1, source_target_pairs={{0,194},{1,65},{4,198},{5,69},{8,202},{9,73},{12,206},{13,77},{16,... | collective-permute-start | bytes 983048 | tf_op jit(solution)/shard_map/ppermute | solution.py:368
  97.1 4.5 %collective-permute-start.15 = (bf16[320,640]{1,0:T(8,128)(2,1)S(1)}, bf16[320,640]{1,0:T(8,128)(2,1)S(1)}, u32[]{:S(2)}, u32[]{:S(2)}) collective-permute-start(bf16[320,640]{1,0:T(8,128)(2,1)S(1)} %get-tuple-element.27), channel_id=1, source_target_pairs={{0,1},{1,0},{4,5},{5,4},{8,9},{9,8},{12,13},{13,12},{16,17},{17,16... | collective-permute-start | bytes 1228808 | tf_op jit(solution)/shard_map/ppermute | solution.py:368

commit v6 on v5

--- a/solution.py
+++ b/solution.py
@@ -463,8 +463,8 @@
     held = (held + c) % 8
     place = jnp.argmax(held[None, :] == jnp.arange(8)[:, None], axis=1).astype(jnp.int32)
 
-    moves = (lambda i: i + 2, lambda i: i - 1, lambda i: i + 1)
-    offsets = jnp.array([0, 2, 1, 3])
+    moves = (lambda i: i + 2, lambda i: i + 1, lambda i: i - 1)
+    offsets = jnp.array([0, 2, 3, 1])
     four = jnp.concatenate([right] + [send(right, plane(0, move)) for move in moves])
     rights = [four] + [send(four, plane(1, move)) for move in moves]
     aa = jnp.tile((jnp.where(c == 0, x, y) + offsets) % 4, 4)

time: 119 us -> 119 us (level)
  starting transfers between devices: 28.1 us -> 29.4 us
    ppermute x16, starting transfers between devices: 18.9 us -> 20.2 us  [send(): return lax.ppermute(values, AXES, pairs)]
  transfers between devices with their start and end apart: 17 -> 17, of which waited for: 11 -> 12; matrix products, arithmetic and copies ran while one was open for 1% -> 1% of each run, Pallas kernels for 8% -> 7%
where the time goes in v6:
time: 119 us
  starting transfers between devices  29.4 us (25%)
  blocking collectives  28.7 us (24%)
  waiting for transfers between devices  27.5 us (23%)
  Pallas kernels  27 us (23%)
  local copies, waits for them, and re-layouts  4.32 us (4%)
    ppermute x16, waiting for transfers between devices, send(): return lax.ppermute(values, AXES, pairs)  23.1 us
    ppermute x16, starting transfers between devices, send(): return lax.ppermute(values, AXES, pairs)  20.2 us
    pallas_call x1, Pallas kernels, coefficients(): pl.pallas_call(rest_kernel, out_shape=(jax.ShapeDtypeStruct((32, 8, 640),...  15 us
    all_to_all x1, blocking collectives, local(): return assemble(lax.all_to_all(tile, 'p', 0, 0, tiled=True))  14.7 us
    all_to_all x1, blocking collectives, local(): lax.all_to_all(right, ('h', 'p'), 0, 0, tiled=True).reshape(64, 1280)  14 us
    all_to_all x1, starting transfers between devices, pair_exchange(): got = lax.all_to_all(left, AXES, 0, 0, axis_index_groups=groups, tiled=True)  9.2 us
    pallas_call x1, Pallas kernels, own_coefficients(): pl.pallas_call(own_kernel, out_shape=jax.ShapeDtypeStruct((2, 2, NG), F32...  5.03 us
    all_to_all x1, waiting for transfers between devices, pair_exchange(): got = lax.all_to_all(left, AXES, 0, 0, axis_index_groups=groups, tiled=True)  4.43 us
  transfers between devices with their start and end apart: 17, of which 12 were waited for; matrix products, arithmetic and copies ran while one was open for 1% of the time, Pallas kernels for 7%

profile of v6, /device:TPU:1, one launch (start us, length us, event | category | flops | bytes accessed | tf_op | source)
XLA Modules:
  0.0 118.7 jit_solution(1316624485539313708)
XLA Ops:
  0.6 0.0 copy-start.9
  0.6 1.0 dynamic-slice_bitcast_fusion
  1.6 2.5 %collective-permute-start.2 = (bf16[48,2304]{1,0:T(8,128)(2,1)S(1)}, bf16[48,2304]{1,0:T(8,128)(2,1)S(1)}, u32[]{:S(2)}, u32[]{:S(2)}) collective-permute-start(bf16[48,2304]{1,0:T(8,128)(2,1)S(1)} %dynamic-slice_bitcast_fusion), channel_id=1, source_target_pairs={{0,64},{1,65},{4,68},{5,69},{8,72},{9,73},{12,76},{13,77},{16,80},... | collective-permute-start | bytes 663560 | tf_op jit(solution)/shard_map/ppermute | solution.py:368
  4.2 5.1 %collective-permute-start.1 = (bf16[48,2304]{1,0:T(8,128)(2,1)S(1)}, bf16[48,2304]{1,0:T(8,128)(2,1)S(1)}, u32[]{:S(2)}, u32[]{:S(2)}) collective-permute-start(bf16[48,2304]{1,0:T(8,128)(2,1)S(1)} %dynamic-slice_bitcast_fusion), channel_id=1, source_target_pairs={{0,128},{1,131},{4,132},{5,135},{8,136},{9,139},{12,140},{13,143},... | collective-permute-start | bytes 663560 | tf_op jit(solution)/shard_map/ppermute | solution.py:368
  9.3 0.7 collective-permute-start
  10.0 0.7 copy-done.2
  10.7 0.0 copy-start.8
  10.8 1.0 shard_map.113
  11.8 0.2 copy-done.1
  12.0 0.4 copy-done.5
  12.4 0.4 copy-done.6
  12.8 5.0 %shard_map.114.owned = f32[2,2,5120]{2,1,0:T(2,128)S(1)} custom-call(bf16[1,2,48,2304]{3,2,1,0:T(8,128)(2,1)S(1)} %copy-done, bf16[2,2,48,2304]{3,2,1,0:T(8,128)(2,1)S(1)} %copy-done.1, bf16[768,768]{1,0:T(8,128)(2,1)S(1)} %copy-done.6, bf16[768,768]{1,0:T(8,128)(2,1)S(1)} %copy-done.5, bf16[48,48]{1,0:T(8,128)(2,1)S(1)} %copy-done.9, ...), custom_call_target="tpu_custom_call" | custom-call | flops 5000000000 | bytes 30000000 | tf_op jit(solution)/shard_map/pallas_call | solution.py:262
  17.8 1.4 %collective-permute-done.p0 = bf16[48,2304]{1,0:T(8,128)(2,1)S(1)} collective-permute-done((bf16[48,2304]{1,0:T(8,128)(2,1)S(1)}, bf16[48,2304]{1,0:T(8,128)(2,1)S(1)}, u32[]{:S(2)}, u32[]{:S(2)}) %collective-permute-start) | collective-permute-done | bytes 221216 | tf_op jit(solution)/shard_map/ppermute | solution.py:368
  19.2 0.5 collective-permute-start.4
  19.7 0.1 pad_add_fusion.core
  19.8 0.9 collective-permute-done.3.o0
  20.7 0.3 collective-permute-done.4.o1
  21.0 0.3 collective-permute-done.5.o2
  21.3 1.3 %copy-done.7 = bf16[768,768]{1,0:T(8,128)(2,1)S(1)} copy-done((bf16[768,768]{1,0:T(8,128)(2,1)S(1)}, bf16[768,768]{1,0:T(8,128)(2,1)}, u32[]{:S(2)}) %copy-start.7) | copy-done | bytes 1179672
  22.6 15.0 %shard_map.115 = (bf16[32,8,640]{2,1,0:T(8,128)(2,1)}, bf16[8,8,1280]{2,1,0:T(8,128)(2,1)S(1)}) custom-call(s32[2]{0:T(128)S(1)} %pad_add_fusion.core, f32[4]{0:T(128)S(1)} %copy-done.3, f32[2]{0:T(128)S(1)} %copy-done.4, bf16[48,2304]{1,0:T(8,128)(2,1)S(1)} %collective-permute-done.p0, bf16[48,2304]{1,0:T(8,128)(2,1)S(1)} %collective-permute-done.1.p1, ...), custom_call_target="tpu_custom_call" | custom-call | flops 10000000000 | bytes 50000000 | tf_op jit(solution)/shard_map/pallas_call | solution.py:274
  37.6 14.0 %all_to_all.15 = bf16[8,8,1280]{2,1,0:T(8,128)(2,1)S(1)} all-to-all(bf16[8,8,1280]{2,1,0:T(8,128)(2,1)S(1)} %get-tuple-element.23), channel_id=1, replica_groups=mesh['p'=4,'y'=4,'x'=4,'h'=2,'c'=2] {'h','p'}, dimensions={0} | all-to-all | bytes 327680 | tf_op jit(solution)/shard_map/all_to_all | solution.py:451
  51.6 9.2 %all-to-all-start.1 = ((bf16[32,8,640]{2,1,0:T(8,128)(2,1)}), bf16[32,8,640]{2,1,0:T(8,128)(2,1)S(1)}, u32[]{:S(2)}, u32[]{:S(2)}) async-start(bf16[32,8,640]{2,1,0:T(8,128)(2,1)} %get-tuple-element.24), calls=%async_computation.1 | async-start | bytes 655360 | tf_op jit(solution)/shard_map/all_to_all | solution.py:409
  61.0 0.1 tile.10
  61.1 0.1 broadcast_in_dim.2
  61.1 0.1 reshape.102
  61.2 0.1 stack.42
  61.3 2.5 %collective-permute-start.11 = (bf16[64,1280]{1,0:T(8,128)(2,1)S(1)}, bf16[64,1280]{1,0:T(8,128)(2,1)S(1)}, u32[]{:S(2)}, u32[]{:S(2)}) collective-permute-start(bf16[64,1280]{1,0:T(8,128)(2,1)S(1)} %bitcast.20), channel_id=1, source_target_pairs={{0,12},{1,49},{4,0},{5,53},{8,4},{9,57},{12,8},{13,61},{16,28},{17... | collective-permute-start | bytes 491528 | tf_op jit(solution)/shard_map/ppermute | solution.py:368
  63.8 1.7 %collective-permute-start.9 = (bf16[64,1280]{1,0:T(8,128)(2,1)S(1)}, bf16[64,1280]{1,0:T(8,128)(2,1)S(1)}, u32[]{:S(2)}, u32[]{:S(2)}) collective-permute-start(bf16[64,1280]{1,0:T(8,128)(2,1)S(1)} %bitcast.22), channel_id=1, source_target_pairs={{0,8},{1,33},{4,12},{5,37},{8,0},{9,41},{12,4},{13,45},{16,24},{17... | collective-permute-start | bytes 491528 | tf_op jit(solution)/shard_map/ppermute | solution.py:368
  65.5 4.4 %all-to-all-done.1 = bf16[32,8,640]{2,1,0:T(8,128)(2,1)S(1)} async-done(((bf16[32,8,640]{2,1,0:T(8,128)(2,1)}), bf16[32,8,640]{2,1,0:T(8,128)(2,1)S(1)}, u32[]{:S(2)}, u32[]{:S(2)}) %all-to-all-start.1) | async-done | bytes 327712 | tf_op jit(solution)/shard_map/all_to_all | solution.py:409
  70.0 2.7 %collective-permute-done.9 = bf16[64,1280]{1,0:T(8,128)(2,1)S(1)} collective-permute-done((bf16[64,1280]{1,0:T(8,128)(2,1)S(1)}, bf16[64,1280]{1,0:T(8,128)(2,1)S(1)}, u32[]{:S(2)}, u32[]{:S(2)}) %collective-permute-start.9) | collective-permute-done | bytes 163872 | tf_op jit(solution)/shard_map/ppermute | solution.py:368
  72.7 0.1 collective-permute-done.10
  72.8 3.4 %collective-permute-done.6.l1 = bf16[2,16,8,640]{3,2,1,0:T(8,128)(2,1)S(1)} collective-permute-done((bf16[2,16,8,640]{3,2,1,0:T(8,128)(2,1)S(1)}, bf16[2,16,8,640]{3,2,1,0:T(8,128)(2,1)S(1)}, u32[]{:S(2)}, u32[]{:S(2)}) %collective-permute-start.6) | collective-permute-done | bytes 327712 | tf_op jit(solution)/shard_map/ppermute | solution.py:368
  76.2 0.5 collective-permute-start.7
  76.7 0.2 collective-permute-start.14
  76.9 2.1 %collective-permute-start.13 = (bf16[256,1280]{1,0:T(8,128)(2,1)S(1)}, bf16[256,1280]{1,0:T(8,128)(2,1)S(1)}, u32[]{:S(2)}, u32[]{:S(2)}) collective-permute-start(bf16[256,1280]{1,0:T(8,128)(2,1)S(1)} %constant_dynamic-update-slice_fusion.r0), channel_id=1, source_target_pairs={{0,32},{1,9},{4,36},{5,13},{8,40},{9,1},{12,44},{13,5},{16,48},{17... | collective-permute-start | bytes 1966088 | tf_op jit(solution)/shard_map/ppermute | solution.py:368
  79.0 1.1 collective-permute-start.12
  80.1 3.5 %collective-permute-done.7.l2 = bf16[2,16,8,640]{3,2,1,0:T(8,128)(2,1)S(1)} collective-permute-done((bf16[2,16,8,640]{3,2,1,0:T(8,128)(2,1)S(1)}, bf16[2,16,8,640]{3,2,1,0:T(8,128)(2,1)S(1)}, u32[]{:S(2)}, u32[]{:S(2)}) %collective-permute-start.7) | collective-permute-done | bytes 327712 | tf_op jit(solution)/shard_map/ppermute | solution.py:368
  83.6 0.6 iota_reduce_fusion
  84.3 5.6 %collective-permute-done.8.l3 = bf16[2,16,8,640]{3,2,1,0:T(8,128)(2,1)S(1)} collective-permute-done((bf16[2,16,8,640]{3,2,1,0:T(8,128)(2,1)S(1)}, bf16[2,16,8,640]{3,2,1,0:T(8,128)(2,1)S(1)}, u32[]{:S(2)}, u32[]{:S(2)}) %collective-permute-start.8) | collective-permute-done | bytes 327712 | tf_op jit(solution)/shard_map/ppermute | solution.py:368
  89.8 1.4 %shard_map.116.left = bf16[640,1024]{1,0:T(8,128)(2,1)S(1)} custom-call(s32[8]{0:T(128)S(1)} %get-tuple-element.15.place, s32[16]{0:T(128)S(1)} %broadcast_select_fusion.rows, bf16[2,16,8,640]{3,2,1,0:T(8,128)(2,1)S(1)} %bitcast.17, bf16[2,16,8,640]{3,2,1,0:T(8,128)(2,1)S(1)} %collective-permute-done.6.l1, ...), custom_call_target="tpu_custom_call" | custom-call | tf_op jit(solution)/shard_map/pallas_call | solution.py:304
  91.2 3.5 %collective-permute-done.14.r2 = bf16[256,1280]{1,0:T(8,128)(2,1)S(1)} collective-permute-done((bf16[256,1280]{1,0:T(8,128)(2,1)S(1)}, bf16[256,1280]{1,0:T(8,128)(2,1)S(1)}, u32[]{:S(2)}, u32[]{:S(2)}) %collective-permute-start.14) | collective-permute-done | bytes 655392 | tf_op jit(solution)/shard_map/ppermute | solution.py:368
  94.7 1.4 %shard_map.117.acc = f32[2,320,640]{2,1,0:T(8,128)S(1)} custom-call(bf16[640,1024]{1,0:T(8,128)(2,1)S(1)} %shard_map.116.left, bf16[256,1280]{1,0:T(8,128)(2,1)S(1)} %constant_dynamic-update-slice_fusion.r0, bf16[256,1280]{1,0:T(8,128)(2,1)S(1)} %collective-permute-done.13.r1, bf16[256,1280]{1,0:T(8,128)(2,1)S(1)} %collective-permute-done.14.r2), custom_call_target="tpu_custom_call" | custom-call | tf_op jit(solution)/shard_map/pallas_call | solution.py:339
  96.2 1.1 shard_map.118
  97.2 3.2 %collective-permute-start.15 = (bf16[320,640]{1,0:T(8,128)(2,1)S(1)}, bf16[320,640]{1,0:T(8,128)(2,1)S(1)}, u32[]{:S(2)}, u32[]{:S(2)}) collective-permute-start(bf16[320,640]{1,0:T(8,128)(2,1)S(1)} %get-tuple-element.27), channel_id=1, source_target_pairs={{0,1},{1,0},{4,5},{5,4},{8,9},{9,8},{12,13},{13,12},{16,17},{17,16... | collective-permute-start | bytes 1228808 | tf_op jit(solution)/shard_map/ppermute | solution.py:368
  100.5 1.4 %collective-permute-done.15 = bf16[320,640]{1,0:T(8,128)(2,1)S(1)} collective-permute-done((bf16[320,640]{1,0:T(8,128)(2,1)S(1)}, bf16[320,640]{1,0:T(8,128)(2,1)S(1)}, u32[]{:S(2)}, u32[]{:S(2)}) %collective-permute-start.15) | collective-permute-done | bytes 409632 | tf_op jit(solution)/shard_map/ppermute | solution.py:368
  101.8 0.1 add_convert_fusion
  101.9 14.7 %all_to_all.16.tile = bf16[4,80,640]{2,1,0:T(8,128)(2,1)} all-to-all(bf16[4,80,640]{2,1,0:T(8,128)(2,1)S(1)} %bitcast.19), channel_id=1, replica_groups=mesh['p'=4,'y'=4,'x'=4,'h'=2,'c'=2] {'p'}, dimensions={0} | all-to-all | bytes 819200 | tf_op jit(solution)/shard_map/all_to_all | solution.py:476
  116.7 2.0 %shard_map.119 = (f32[80,1280]{1,0:T(8,128)}, f32[80,1280]{1,0:T(8,128)}) custom-call(bf16[4,80,640]{2,1,0:T(8,128)(2,1)} %all_to_all.16.tile), custom_call_target="tpu_custom_call" | custom-call | tf_op jit(solution)/shard_map/pallas_call | solution.py:420
  (33 shorter events, 0.1 us)
Async XLA Ops:
  0.6 11.2 %copy-start.9 = (bf16[48,48]{1,0:T(8,128)(2,1)S(1)}, bf16[48,48]{1,0:T(8,128)(2,1)}, u32[]{:S(2)}) copy-start(bf16[48,48]{1,0:T(8,128)(2,1)} %constant.120.clone.tc) | copy-start | bytes 13828
  1.6 16.2 %collective-permute-start.2 = (bf16[48,2304]{1,0:T(8,128)(2,1)S(1)}, bf16[48,2304]{1,0:T(8,128)(2,1)S(1)}, u32[]{:S(2)}, u32[]{:S(2)}) collective-permute-start(bf16[48,2304]{1,0:T(8,128)(2,1)S(1)} %dynamic-slice_bitcast_fusion), channel_id=1, source_target_pairs={{0,64},{1,65},{4,68},{5,69},{8,72},{9,73},{12,76},{13,77},{16,80},... | collective-permute-start | bytes 663560 | tf_op jit(solution)/shard_map/ppermute | solution.py:368
  4.2 13.7 %collective-permute-start.1 = (bf16[48,2304]{1,0:T(8,128)(2,1)S(1)}, bf16[48,2304]{1,0:T(8,128)(2,1)S(1)}, u32[]{:S(2)}, u32[]{:S(2)}) collective-permute-start(bf16[48,2304]{1,0:T(8,128)(2,1)S(1)} %dynamic-slice_bitcast_fusion), channel_id=1, source_target_pairs={{0,128},{1,131},{4,132},{5,135},{8,136},{9,139},{12,140},{13,143},... | collective-permute-start | bytes 663560 | tf_op jit(solution)/shard_map/ppermute | solution.py:368
  9.3 9.9 %collective-permute-start = (bf16[48,2304]{1,0:T(8,128)(2,1)S(1)}, bf16[48,2304]{1,0:T(8,128)(2,1)S(1)}, u32[]{:S(2)}, u32[]{:S(2)}) collective-permute-start(bf16[48,2304]{1,0:T(8,128)(2,1)S(1)} %dynamic-slice_bitcast_fusion), channel_id=1, source_target_pairs={{0,194},{1,195},{4,198},{5,199},{8,202},{9,203},{12,206},{13,207},... | collective-permute-start | bytes 663560 | tf_op jit(solution)/shard_map/ppermute | solution.py:368
  10.0 0.7 copy-start.2
  10.7 1.1 copy-start
  10.7 1.3 %copy-start.1 = (bf16[2,2,48,2304]{3,2,1,0:T(8,128)(2,1)S(1)}, bf16[2,2,48,2304]{3,2,1,0:T(8,128)(2,1)}, u32[]{:S(2)}) copy-start(bf16[2,2,48,2304]{3,2,1,0:T(8,128)(2,1)} %cond.3) | copy-start | bytes 2654212
  10.7 1.7 %copy-start.5 = (bf16[768,768]{1,0:T(8,128)(2,1)S(1)}, bf16[768,768]{1,0:T(8,128)(2,1)}, u32[]{:S(2)}) copy-start(bf16[768,768]{1,0:T(8,128)(2,1)} %constant.119.clone.wy) | copy-start | bytes 3538948
  10.7 2.0 %copy-start.6 = (bf16[768,768]{1,0:T(8,128)(2,1)S(1)}, bf16[768,768]{1,0:T(8,128)(2,1)}, u32[]{:S(2)}) copy-start(bf16[768,768]{1,0:T(8,128)(2,1)} %constant.118.clone.wz) | copy-start | bytes 3538948
  10.7 2.0 %copy-start.8 = (bf16[48,48]{1,0:T(8,128)(2,1)S(1)}, bf16[48,48]{1,0:T(8,128)(2,1)}, u32[]{:S(2)}) copy-start(bf16[48,48]{1,0:T(8,128)(2,1)} %constant.121.clone.ts) | copy-start | bytes 13828
  12.8 8.6 %copy-start.3 = (f32[4]{0:T(128)S(1)}, f32[4]{0:T(128)}, u32[]{:S(2)}) copy-start(f32[4]{0:T(128)} %ve.1) | copy-start | bytes 52
  12.8 8.6 %copy-start.4 = (f32[2]{0:T(128)S(1)}, f32[2]{0:T(128)}, u32[]{:S(2)}) copy-start(f32[2]{0:T(128)} %ce.1) | copy-start | bytes 28
  19.2 1.5 %collective-permute-start.3 = (bf16[48,2304]{1,0:T(8,128)(2,1)S(1)}, bf16[48,2304]{1,0:T(8,128)(2,1)S(1)}, u32[]{:S(2)}, u32[]{:S(2)}) collective-permute-start(bf16[48,2304]{1,0:T(8,128)(2,1)S(1)} %collective-permute-done.p0), channel_id=1, source_target_pairs={{0,1},{1,0},{4,5},{5,4},{8,9},{9,8},{12,13},{13,12},{16,17},{17,16... | collective-permute-start | bytes 663560 | tf_op jit(solution)/shard_map/ppermute | solution.py:368
  19.2 1.8 %collective-permute-start.4 = (bf16[48,2304]{1,0:T(8,128)(2,1)S(1)}, bf16[48,2304]{1,0:T(8,128)(2,1)S(1)}, u32[]{:S(2)}, u32[]{:S(2)}) collective-permute-start(bf16[48,2304]{1,0:T(8,128)(2,1)S(1)} %collective-permute-done.1.p1), channel_id=1, source_target_pairs={{0,1},{1,0},{4,5},{5,4},{8,9},{9,8},{12,13},{13,12},{16,17},{17,16... | collective-permute-start | bytes 663560 | tf_op jit(solution)/shard_map/ppermute | solution.py:368
  19.7 1.6 %collective-permute-start.5 = (bf16[48,2304]{1,0:T(8,128)(2,1)S(1)}, bf16[48,2304]{1,0:T(8,128)(2,1)S(1)}, u32[]{:S(2)}, u32[]{:S(2)}) collective-permute-start(bf16[48,2304]{1,0:T(8,128)(2,1)S(1)} %collective-permute-done.2.p2), channel_id=1, source_target_pairs={{0,1},{1,0},{4,5},{5,4},{8,9},{9,8},{12,13},{13,12},{16,17},{17,16... | collective-permute-start | bytes 663560 | tf_op jit(solution)/shard_map/ppermute | solution.py:368
  21.3 1.3 %copy-start.7 = (bf16[768,768]{1,0:T(8,128)(2,1)S(1)}, bf16[768,768]{1,0:T(8,128)(2,1)}, u32[]{:S(2)}) copy-start(bf16[768,768]{1,0:T(8,128)(2,1)} %constant.118.clone.wz) | copy-start | bytes 3538948
  22.6 38.3 %copy-start.10 = (s32[4]{0:T(128)S(1)}, s32[4]{0:T(128)}, u32[]{:S(2)}) copy-start(s32[4]{0:T(128)} %constant.122.clone) | copy-start | bytes 52
  51.6 18.4 %all-to-all-start.1 = ((bf16[32,8,640]{2,1,0:T(8,128)(2,1)}), bf16[32,8,640]{2,1,0:T(8,128)(2,1)S(1)}, u32[]{:S(2)}, u32[]{:S(2)}) async-start(bf16[32,8,640]{2,1,0:T(8,128)(2,1)} %get-tuple-element.24), calls=%async_computation.1 | async-start | bytes 655360 | tf_op jit(solution)/shard_map/all_to_all | solution.py:409
  61.3 15.4 %collective-permute-start.11 = (bf16[64,1280]{1,0:T(8,128)(2,1)S(1)}, bf16[64,1280]{1,0:T(8,128)(2,1)S(1)}, u32[]{:S(2)}, u32[]{:S(2)}) collective-permute-start(bf16[64,1280]{1,0:T(8,128)(2,1)S(1)} %bitcast.20), channel_id=1, source_target_pairs={{0,12},{1,49},{4,0},{5,53},{8,4},{9,57},{12,8},{13,61},{16,28},{17... | collective-permute-start | bytes 491528 | tf_op jit(solution)/shard_map/ppermute | solution.py:368
  63.8 9.0 %collective-permute-start.10 = (bf16[64,1280]{1,0:T(8,128)(2,1)S(1)}, bf16[64,1280]{1,0:T(8,128)(2,1)S(1)}, u32[]{:S(2)}, u32[]{:S(2)}) collective-permute-start(bf16[64,1280]{1,0:T(8,128)(2,1)S(1)} %bitcast.21), channel_id=1, source_target_pairs={{0,4},{1,17},{4,8},{5,21},{8,12},{9,25},{12,0},{13,29},{16,20},{17... | collective-permute-start | bytes 491528 | tf_op jit(solution)/shard_map/ppermute | solution.py:368
  63.8 8.9 %collective-permute-start.9 = (bf16[64,1280]{1,0:T(8,128)(2,1)S(1)}, bf16[64,1280]{1,0:T(8,128)(2,1)S(1)}, u32[]{:S(2)}, u32[]{:S(2)}) collective-permute-start(bf16[64,1280]{1,0:T(8,128)(2,1)S(1)} %bitcast.22), channel_id=1, source_target_pairs={{0,8},{1,33},{4,12},{5,37},{8,0},{9,41},{12,4},{13,45},{16,24},{17... | collective-permute-start | bytes 491528 | tf_op jit(solution)/shard_map/ppermute | solution.py:368
  70.0 6.2 %collective-permute-start.6 = (bf16[2,16,8,640]{3,2,1,0:T(8,128)(2,1)S(1)}, bf16[2,16,8,640]{3,2,1,0:T(8,128)(2,1)S(1)}, u32[]{:S(2)}, u32[]{:S(2)}) collective-permute-start(bf16[2,16,8,640]{3,2,1,0:T(8,128)(2,1)S(1)} %bitcast.16), channel_id=1, source_target_pairs={{0,194},{1,65},{4,198},{5,69},{8,202},{9,73},{12,206},{13,77},{16,... | collective-permute-start | bytes 983048 | tf_op jit(solution)/shard_map/ppermute | solution.py:368
  76.2 7.4 %collective-permute-start.7 = (bf16[2,16,8,640]{3,2,1,0:T(8,128)(2,1)S(1)}, bf16[2,16,8,640]{3,2,1,0:T(8,128)(2,1)S(1)}, u32[]{:S(2)}, u32[]{:S(2)}) collective-permute-start(bf16[2,16,8,640]{3,2,1,0:T(8,128)(2,1)S(1)} %collective-permute-done.6.l1), channel_id=1, source_target_pairs={{0,64},{1,195},{4,68},{5,199},{8,72},{9,203},{12,76},{13,207},{16,... | collective-permute-start | bytes 983048 | tf_op jit(solution)/shard_map/ppermute | solution.py:368
  76.7 18.0 %collective-permute-start.14 = (bf16[256,1280]{1,0:T(8,128)(2,1)S(1)}, bf16[256,1280]{1,0:T(8,128)(2,1)S(1)}, u32[]{:S(2)}, u32[]{:S(2)}) collective-permute-start(bf16[256,1280]{1,0:T(8,128)(2,1)S(1)} %constant_dynamic-update-slice_fusion.r0), channel_id=1, source_target_pairs={{0,16},{1,5},{4,20},{5,9},{8,24},{9,13},{12,28},{13,1},{16,32},{17... | collective-permute-start | bytes 1966088 | tf_op jit(solution)/shard_map/ppermute | solution.py:368
  76.9 17.9 %collective-permute-start.13 = (bf16[256,1280]{1,0:T(8,128)(2,1)S(1)}, bf16[256,1280]{1,0:T(8,128)(2,1)S(1)}, u32[]{:S(2)}, u32[]{:S(2)}) collective-permute-start(bf16[256,1280]{1,0:T(8,128)(2,1)S(1)} %constant_dynamic-update-slice_fusion.r0), channel_id=1, source_target_pairs={{0,32},{1,9},{4,36},{5,13},{8,40},{9,1},{12,44},{13,5},{16,48},{17... | collective-permute-start | bytes 1966088 | tf_op jit(solution)/shard_map/ppermute | solution.py:368
  79.0 17.2 %collective-permute-start.12 = (bf16[256,1280]{1,0:T(8,128)(2,1)S(1)}, bf16[256,1280]{1,0:T(8,128)(2,1)S(1)}, u32[]{:S(2)}, u32[]{:S(2)}) collective-permute-start(bf16[256,1280]{1,0:T(8,128)(2,1)S(1)} %constant_dynamic-update-slice_fusion.r0), channel_id=1, source_target_pairs={{0,48},{1,13},{4,52},{5,1},{8,56},{9,5},{12,60},{13,9},{16,0},{17,... | collective-permute-start | bytes 1966088 | tf_op jit(solution)/shard_map/ppermute | solution.py:368
  83.6 6.2 %collective-permute-start.8 = (bf16[2,16,8,640]{3,2,1,0:T(8,128)(2,1)S(1)}, bf16[2,16,8,640]{3,2,1,0:T(8,128)(2,1)S(1)}, u32[]{:S(2)}, u32[]{:S(2)}) collective-permute-start(bf16[2,16,8,640]{3,2,1,0:T(8,128)(2,1)S(1)} %collective-permute-done.7.l2), channel_id=1, source_target_pairs={{0,194},{1,65},{4,198},{5,69},{8,202},{9,73},{12,206},{13,77},{16,... | collective-permute-start | bytes 983048 | tf_op jit(solution)/shard_map/ppermute | solution.py:368
  97.2 4.6 %collective-permute-start.15 = (bf16[320,640]{1,0:T(8,128)(2,1)S(1)}, bf16[320,640]{1,0:T(8,128)(2,1)S(1)}, u32[]{:S(2)}, u32[]{:S(2)}) collective-permute-start(bf16[320,640]{1,0:T(8,128)(2,1)S(1)} %get-tuple-element.27), channel_id=1, source_target_pairs={{0,1},{1,0},{4,5},{5,4},{8,9},{9,8},{12,13},{13,12},{16,17},{17,16... | collective-permute-start | bytes 1228808 | tf_op jit(solution)/shard_map/ppermute | solution.py:368
